TPU v7x, 256 devices: a whole 4x4x8 slice. The times are simulated.
256 devices in a mesh: dp: 16 (over x, y), feat: 16 (over z, core).
Axes of the slice: x: 4, y: 4, z: 8, core: 2. Of those that a mesh axis runs over, the one named last changes fastest.
Arguments:
- x_table: bfloat16 [1024, 131072], P('feat', 'dp'), may hold values from -6 to 6
- hub_feats: bfloat16 [1024, 2048], P('feat'), may hold values from -6 to 6
- send_rows: int32 [16, 16, 2048], P('dp'), may hold values from 0 to 8191
- self_slot: int32 [65536], P('dp'), may hold values from 0 to 34815
- nbr1: int32 [10, 65536], P(None, 'dp'), may hold values from 0 to 34815
- cnt1: int32 [65536], P('dp'), may hold values from 1 to 10
- h_saved: bfloat16 [65536, 512], P(('dp', 'feat')), as said below
- seed_self: int32 [65536], P(('dp', 'feat')), may hold values from 0 to 4095
- nbr2: int32 [65536, 25], P(('dp', 'feat')), may hold values from 0 to 4095
- cnt2: int32 [65536], P(('dp', 'feat')), may hold values from 1 to 25
- d_logits: bfloat16 [65536, 172], P(('dp', 'feat')), may hold values from -0.0234375 to 0.0234375
- w_self2: bfloat16 [512, 172], replicated, may hold values from -0.25 to 0.25
- w_nbr2: bfloat16 [512, 172], replicated, may hold values from -0.25 to 0.25
Outputs:
- grad_self1: float32 [1024, 512], P('feat')
- grad_nbr1: float32 [1024, 512], P('feat')
- grad_self2: float32 [512, 172], replicated
- grad_nbr2: float32 [512, 172], replicated
Inputs may be any that keep to these rules, and one draw needn't show every extreme that they name: Entries nbr1[j, u] with j at or past cnt1[u] are padding and are not read. `nbr2`: entries of a row at positions at or past its count are padding and are not read. Every entry of h_saved is zero or positive.
All inputs are finite; a program needn't handle non-finite values.
Results may differ from a plain program's by a relative error of at most 0.0039.
Values may be sent and summed in bfloat16 or wider, within the bound.
A program may use at most 128 MiB of HBM per device.

v0:
```python
import jax
import jax.numpy as jnp
from jax import lax
from jax.sharding import PartitionSpec as P


def body(
    x_table,
    hub_feats,
    send_rows,
    self_slot,
    nbr1,
    cnt1,
    h_saved,
    seed_self,
    nbr2,
    cnt2,
    d_logits,
    w_self2,
    w_nbr2,
):
    highest = lax.Precision.HIGHEST
    slice_width = x_table.shape[0]
    node_rows = x_table.T
    outgoing = jnp.take(node_rows, send_rows[0], axis=0)
    fetched = lax.all_to_all(outgoing, "dp", split_axis=0, concat_axis=0, tiled=True)
    lookup = jnp.concatenate([fetched.reshape(-1, slice_width), hub_feats.T], axis=0)
    fanin = nbr1.shape[0]
    picks = jnp.concatenate([self_slot[:, None], nbr1.T], axis=1)
    gathered = jnp.take(lookup, picks, axis=0)
    self_rows = gathered[:, 0, :]
    valid = lax.iota(jnp.int32, fanin)[None, :] < cnt1[:, None]
    total = jnp.sum(
        jnp.where(valid[:, :, None], gathered[:, 1:, :].astype(jnp.float32), jnp.float32(0.0)),
        axis=1,
    )
    mean_rows = (total / cnt1[:, None].astype(jnp.float32)).astype(jnp.bfloat16)
    both_rows = jnp.concatenate([self_rows, mean_rows], axis=1)
    classes = d_logits.shape[1]
    fanout = nbr2.shape[1]
    local_rows = h_saved.shape[0]
    dims = (((0,), (0,)), ((), ()))
    dz_mean = (d_logits.astype(jnp.float32) / cnt2[:, None].astype(jnp.float32)).astype(
        jnp.bfloat16
    )
    row_ids = lax.iota(jnp.int32, lax.axis_size("feat") * local_rows)
    tallies = jnp.zeros((nbr2.shape[0], row_ids.shape[0]), jnp.float32)
    for column in range(fanout):
        match = (nbr2[:, column : column + 1] == row_ids[None, :]) & (column < cnt2)[:, None]
        tallies = tallies + match.astype(jnp.float32)
    own_rows = (seed_self[:, None] == row_ids[None, :]).astype(jnp.bfloat16)
    part_nbr = lax.dot_general(
        tallies.astype(jnp.bfloat16), dz_mean, dims, preferred_element_type=jnp.float32
    )
    part_self = lax.dot_general(own_rows, d_logits, dims, preferred_element_type=jnp.float32)
    row_grads = lax.psum_scatter(
        jnp.concatenate([part_nbr, part_self], axis=1), "feat", scatter_dimension=0, tiled=True
    )
    grad_nbr = row_grads[:, :classes]
    grad_self = row_grads[:, classes:]
    h_float = h_saved.astype(jnp.float32)
    second = jnp.dot(h_float.T, row_grads, precision=highest)
    d_hidden = jnp.dot(grad_nbr, w_nbr2.astype(jnp.float32).T, precision=highest)
    d_hidden = d_hidden + jnp.dot(grad_self, w_self2.astype(jnp.float32).T, precision=highest)
    d_pre = jnp.where(h_saved > 0, d_hidden, jnp.float32(0.0)).astype(jnp.bfloat16)
    hidden_width = h_saved.shape[1]
    summed = lax.dot_general(
        both_rows,
        lax.all_gather(d_pre, "feat", axis=0, tiled=True),
        dims,
        preferred_element_type=jnp.float32,
    )
    first = summed.reshape(2, slice_width, hidden_width)
    first = lax.psum(first, "dp")
    stacked = jnp.stack([second[:, classes:], second[:, :classes]], axis=0)
    stacked = lax.psum(stacked, ("dp", "feat"))
    return (first[0], first[1], stacked[0], stacked[1])


def solution(mesh):
    placed = (
        P("feat", "dp"),
        P("feat", None),
        P("dp", None, None),
        P("dp"),
        P(None, "dp"),
        P("dp"),
        P(("dp", "feat"), None),
        P(("dp", "feat")),
        P(("dp", "feat"), None),
        P(("dp", "feat")),
        P(("dp", "feat"), None),
        P(),
        P(),
    )
    return jax.shard_map(
        body,
        mesh=mesh,
        in_specs=placed,
        out_specs=(P("feat", None), P("feat", None), P(), P()),
        check_vma=False,
    )
```

profile of v0, /device:TPU:1, one launch (start us, length us, event | category | flops | bytes accessed | tf_op | source)
XLA Modules:
  0.0 876.1 jit_solution(17878684508093012469)
XLA Ops:
  7.2 0.0 copy-start
  7.2 0.0 copy-start.11
  7.2 0.0 reduce-scatter.2.cloned.1.call-start
  7.2 1.1 fusion.90
  8.4 0.9 fusion.91
  9.2 0.7 broadcast_compare_fusion.24
  10.0 0.7 convert_element_type.135
  10.6 1.9 fusion.25
  12.6 0.0 copy-done.11
  12.6 32.3 %fusion.26 = f32[4096,172]{0,1:T(8,128)S(1)} fusion(s32[256]{0:T(256)S(1)} %bitcast.105, s32[256]{0:T(256)S(1)} %bitcast.106, s32[256]{0:T(256)S(1)} %bitcast.83, s32[256]{0:T(256)S(1)} %bitcast.84, s32[256]{0:T(256)S(1)} %bitcast.85, s32[256]{0:T(256)S(1)} %bitcast.86, s32[256]{0:T(256)S(1)} %bitcast.87, s32[256]{0:T(256)S(1)} %bitcast.88, ...), kind=kOutput, calls=%fused_computation.60 | convolution fusion | flops 465699840 | bytes 2939136 | tf_op jit(solution)/shard_map/dot_general | solution.py:52
  44.9 3.1 pad_maximum_fusion.1
  48.0 0.0 reduce-scatter.2.cloned.1.call-update
  48.0 1.2 copy-done.4
  49.2 1.1 copy.26
  50.3 0.0 copy-done.8
  50.4 115.0 %gather_fusion = bf16[32768,64]{1,0:T(8,128)(2,1)} fusion(bf16[8192,64]{1,0:T(8,128)(2,1)S(1)} %bitcast.71, s32[32768]{0:T(1024)S(1)} %broadcast_clamp_fusion.1), kind=kCustom, calls=%fused_computation | custom fusion | bytes 8519680 | tf_op jit(solution)/shard_map/jit(_take)/gather | solution.py:25
  165.4 8.6 copy.27
  174.0 4.6 broadcast_select_fusion.1
  178.6 7.8 all-to-all-start
  186.4 0.0 copy-start.12
  186.4 0.0 all-gather.2.cloned.1.call-start
  186.5 0.3 copy.29
  186.7 0.0 copy-done.5
  186.8 0.0 copy-done.13
  186.8 0.1 compare_select_fusion
  186.8 0.6 copy.30
  187.5 1.2 reshape.206
  188.6 0.1 compare_and_fusion
  188.7 0.8 copy.25
  189.6 0.0 copy-done.12
  189.6 1.9 iota_compare_fusion.27
  191.5 0.0 copy-start.6
  191.5 0.0 copy-start.10
  191.6 56.3 %all-to-all-done = bf16[16,2048,64]{1,2,0:T(8,128)(2,1)} async-done(((bf16[16,2048,64]{1,2,0:T(8,128)(2,1)}), bf16[16,2048,64]{1,2,0:T(8,128)(2,1)}, u32[]{:S(2)}, u32[]{:S(2)}) %all-to-all-start) | async-done | bytes 4194336 | tf_op jit(solution)/shard_map/all_to_all | solution.py:26
  247.9 8.3 copy.28
  256.2 0.0 copy-done
  256.2 1.3 fusion.85
  257.6 2.1 fusion.79
  259.7 0.0 all-gather.2.cloned.1.call-update
  259.7 0.0 all-reduce.5.cloned.1.call-start
  259.8 21.7 %pad_maximum_fusion = bf16[34816,64]{1,0:T(8,128)(2,1)} fusion(bf16[2048,64]{1,0:T(8,128)(2,1)S(1)} %bitcast.75, bf16[32768,64]{1,0:T(8,128)(2,1)} %bitcast.73), kind=kLoop, calls=%fused_computation.4 | loop fusion | flops 8912896 | bytes 8912896 | tf_op jit(solution)/shard_map/concatenate | solution.py:27
  281.5 155.9 %gather_fusion.1 = bf16[45056,64]{1,0:T(8,128)(2,1)} fusion(bf16[34816,64]{1,0:T(8,128)(2,1)} %pad_maximum_fusion, s32[45056]{0:T(1024)S(1)} %broadcast_clamp_fusion), kind=kCustom, calls=%fused_computation.1 | custom fusion | bytes 11714560 | tf_op jit(solution)/shard_map/jit(_take)/gather | solution.py:30
  437.4 21.6 %reshape.205 = bf16[4096,11,64]{2,1,0:T(8,128)(2,1)} reshape(bf16[45056,64]{1,0:T(8,128)(2,1)} %gather_fusion.1) | data formatting | bytes 11534336 | tf_op jit(solution)/shard_map/jit(_take)/gather | solution.py:30
  459.0 28.3 %broadcast_select_fusion = bf16[4096,11,64]{2,1,0:T(8,128)(2,1)S(1)} fusion(bf16[4096,11,64]{2,1,0:T(8,128)(2,1)} %reshape.205, pred[4096,11]{1,0:T(8,128)(4,1)S(1)} %copy.25), kind=kLoop, calls=%fused_computation.3 | loop fusion | flops 2883584 | bytes 11579392 | tf_op jit(solution)/shard_map/jit(_take)/select_n | solution.py:30
  487.3 0.0 copy-start.7
  487.3 23.0 %select_reduce_fusion = f32[4096,64]{1,0:T(8,128)S(1)} fusion(bf16[4096,11,64]{2,1,0:T(8,128)(2,1)S(1)} %broadcast_select_fusion, pred[4096,10]{1,0:T(8,128)(4,1)S(1)} %iota_compare_fusion.27), kind=kLoop, calls=%fused_computation.2 | loop fusion | flops 7602176 | bytes 6332416 | tf_op jit(solution)/shard_map/reduce_sum | solution.py:33
  510.3 0.0 copy-done.2
  510.4 0.5 convolution_bitcast_fusion
  510.8 0.1 slice_bitcast_fusion.3
  510.9 1.0 pad_maximum_fusion.2
  511.8 0.0 all-reduce.5.cloned.1.call-update
  511.9 0.0 all-reduce.3.cloned.1.call-start
  511.9 0.7 divide_convert_fusion
  512.7 4.5 slice.144
  517.2 0.1 copy.36
  517.3 0.0 all-gather.2.cloned.1.call-done
  517.4 0.0 copy-start.1
  517.4 4.2 fusion.80
  521.6 0.0 all-reduce.3.cloned.1.call-update
  521.6 250.1 %all-reduce.5.cloned.1.call-done = f32[2,512,172]{1,2,0:T(8,128)} async-done(((f32[2,512,172]{1,2,0:T(8,128)}), f32[2,512,172]{1,2,0:T(8,128)}) %all-reduce.5.cloned.1.call-update) | async-done | bytes 704528 | tf_op jit(solution)/shard_map/psum | solution.py:76
  771.7 2.0 slice_bitcast_fusion
  773.7 93.9 %all-reduce.3.cloned.1.call-done = f32[2,64,512]{2,1,0:T(8,128)} async-done(((f32[2,64,512]{2,1,0:T(8,128)}), f32[2,64,512]{2,1,0:T(8,128)}) %all-reduce.3.cloned.1.call-update) | async-done | bytes 262160 | tf_op jit(solution)/shard_map/psum | solution.py:74
  867.5 1.7 slice_bitcast_fusion.4
  869.2 0.0 copy-done.1
  (19 shorter events, 0.2 us)
Async XLA Ops:
  7.2 249.1 %copy-start = (bf16[512,172]{0,1:T(8,128)(2,1)S(1)}, bf16[512,172]{0,1:T(8,128)(2,1)}, u32[]{:S(2)}) copy-start(bf16[512,172]{0,1:T(8,128)(2,1)} %param.25) | copy-start | bytes 528388
  7.2 5.4 copy-start.11
  7.2 249.0 %reduce-scatter.2.cloned.1.call-start = ((), (), s32[]{:S(2)}) async-start(), calls=%async_computation.2 | async-start | bytes 5988352 | tf_op jit(solution)/shard_map/reduce_scatter | solution.py:56
  48.0 1.2 copy-start.4
  48.0 2.3 copy-start.8
  178.6 7.8 copy-start.9
  178.6 8.1 copy-start.5
  178.6 8.1 copy-start.13
  178.6 69.3 %all-to-all-start = ((bf16[16,2048,64]{1,2,0:T(8,128)(2,1)}), bf16[16,2048,64]{1,2,0:T(8,128)(2,1)}, u32[]{:S(2)}, u32[]{:S(2)}) async-start(bf16[16,2048,64]{1,2,0:T(8,128)(2,1)} %broadcast_select_fusion.1), calls=%async_computation | async-start | bytes 8388608 | tf_op jit(solution)/shard_map/all_to_all | solution.py:26
  186.4 3.2 copy-start.12
  186.4 331.0 %all-gather.2.cloned.1.call-start = ((), (), s32[]{:S(2)}) async-start(), calls=%async_computation.3 | async-start | bytes 4456448 | tf_op jit(solution)/shard_map/all_gather | solution.py:69
  191.5 66.1 %copy-start.6 = (bf16[256,512]{1,0:T(8,128)(2,1)S(1)}, bf16[256,512]{1,0:T(8,128)(2,1)}, u32[]{:S(2)}) copy-start(bf16[256,512]{1,0:T(8,128)(2,1)} %param.19) | copy-start | bytes 786436
  191.5 66.1 %copy-start.10 = (bf16[512,172]{0,1:T(8,128)(2,1)S(1)}, bf16[512,172]{0,1:T(8,128)(2,1)}, u32[]{:S(2)}) copy-start(bf16[512,172]{0,1:T(8,128)(2,1)} %param.24) | copy-start | bytes 528388
  259.7 512.0 %all-reduce.5.cloned.1.call-start = ((), (), s32[]{:S(2)}) async-start(), calls=%async_computation.5 | async-start | bytes 1441792 | tf_op jit(solution)/shard_map/psum | solution.py:76
  487.3 23.1 %copy-start.2 = (bf16[4096,11,64]{2,1,0:T(8,128)(2,1)}, bf16[4096,11,64]{2,1,0:T(8,128)(2,1)S(1)}, u32[]{:S(2)}) copy-start(bf16[4096,11,64]{2,1,0:T(8,128)(2,1)S(1)} %broadcast_select_fusion) | copy-start | bytes 17301508
  487.3 23.1 %copy-start.3 = (f32[256,344]{0,1:T(8,128)S(1)}, f32[256,344]{0,1:T(8,128)}, u32[]{:S(2)}) copy-start(f32[256,344]{0,1:T(8,128)} %reduce-scatter.2.cloned.1.call-done) | copy-start | bytes 1056772
  487.3 23.1 %copy-start.7 = (bf16[256,512]{1,0:T(8,128)(2,1)S(1)}, bf16[256,512]{1,0:T(8,128)(2,1)}, u32[]{:S(2)}) copy-start(bf16[256,512]{1,0:T(8,128)(2,1)} %param.19) | copy-start | bytes 786436
  511.9 355.7 %all-reduce.3.cloned.1.call-start = ((), (), s32[]{:S(2)}) async-start(), calls=%async_computation.4 | async-start | bytes 524288 | tf_op jit(solution)/shard_map/psum | solution.py:74
  517.4 351.9 %copy-start.1 = (bf16[512,172]{0,1:T(8,128)(2,1)S(1)}, bf16[512,172]{0,1:T(8,128)(2,1)}, u32[]{:S(2)}) copy-start(bf16[512,172]{0,1:T(8,128)(2,1)} %param.25) | copy-start | bytes 528388
Sparse Core Ops, SparseCore 0:
  48.1 66.0 reduce-scatter.1
  259.8 50.1 all-gather.1
  512.0 259.6 all-reduce.4
  775.0 92.4 all-reduce.2
where the time goes:
time: 886 us; the launch traced here: 876 us
  waiting for transfers between devices  400 us (45%)
  local copies, waits for them, and re-layouts  325 us (37%)
  other arithmetic  85.9 us (10%)
  matrix products  42.3 us (5%)
  between operations  14.5 us (2%)
    psum x1, waiting for transfers between devices, body(): stacked = lax.psum(stacked, ('dp', 'feat'))  250 us
    gather x2, local copies, waits for them, and re-layouts, body(): gathered = jnp.take(lookup, picks, axis=0)  178 us
    gather x2, local copies, waits for them, and re-layouts, body(): outgoing = jnp.take(node_rows, send_rows[0], axis=0)  124 us
    psum x1, waiting for transfers between devices, body(): first = lax.psum(first, 'dp')  93.9 us
    all_to_all x1, waiting for transfers between devices, body(): lax.all_to_all(outgoing, 'dp', split_axis=0, concat_axis=0, tiled=True)  56.3 us
    dot_general x1, matrix products, body(): lax.dot_general(tallies.astype(jnp.bfloat16), dz_mean, dims, preferred_el...  32.3 us
    select_n x2, other arithmetic, body(): gathered = jnp.take(lookup, picks, axis=0)  28.3 us
    reduce_sum x1, other arithmetic, body(): jnp.sum(jnp.where(valid[:, :, None], gathered[:, 1:, :].astype(jnp.float3...  23 us
  transfers between devices with their start and end apart: 5, of which 3 were waited for; matrix products, arithmetic and copies ran while one was open for 46% of the time, Pallas kernels for 0%

commit v1 on v0

v1 whole, which is shorter than its diff:
```python
import jax
import jax.numpy as jnp
from jax import lax
from jax.experimental import pallas as pl
from jax.experimental.pallas import tpu as pltpu
from jax.sharding import PartitionSpec as P

N_DP = 16
N_FEAT = 16
CAP = 2048
HALF = CAP // 2
HUBS = 2048
ROWS = 256
FAN1 = 10
FAN2 = 25
PICKS = 1 + FAN1
WIDE = 128
ZERO_ROW = N_DP * CAP + HUBS
MESH = pl.DeviceIdType.MESH
VMEM_LIMIT = 60 * 1024 * 1024


def vmem():
    return pl.BlockSpec(memory_space=pltpu.VMEM)


def smem():
    return pl.BlockSpec(memory_space=pltpu.SMEM)


def pick_kernel(idx_ref, table_ref, out_ref, rows_ref):
    step = 32

    def one_group(group, carry):
        def some_rows(block, inner):
            at = block * step
            first = group * HALF + at
            got = [table_ref[pl.ds(idx_ref[first + r], 1), :] for r in range(step)]
            for r in range(step):
                rows_ref[pl.ds(at + r, 1), :] = got[r]
            return inner

        lax.fori_loop(0, HALF // step, some_rows, 0)
        out_ref[group] = rows_ref[...].astype(jnp.bfloat16)
        return carry

    lax.fori_loop(0, N_DP, one_group, 0)


def pick(idx, table):
    return pl.pallas_call(
        pick_kernel,
        out_shape=jax.ShapeDtypeStruct((N_DP, HALF, WIDE), jnp.bfloat16),
        in_specs=[smem(), vmem()],
        out_specs=vmem(),
        scratch_shapes=[pltpu.VMEM((HALF, WIDE), jnp.float32)],
        compiler_params=pltpu.CompilerParams(vmem_limit_bytes=VMEM_LIMIT),
        name="pick",
    )(idx, table)


def fold_kernel(idx_ref, own_ref, other_ref, hub_ref, count_ref, out_ref, table_ref, self_ref, sum_ref):
    part = N_DP * HALF
    chunk = 1024

    def fill(block, carry):
        at = pl.multiple_of(block * chunk, chunk)
        table_ref[pl.ds(at, chunk), :] = own_ref[pl.ds(at, chunk), :].astype(jnp.float32)
        table_ref[pl.ds(part + at, chunk), :] = other_ref[pl.ds(at, chunk), :].astype(jnp.float32)
        return carry

    lax.fori_loop(0, part // chunk, fill, 0)
    table_ref[pl.ds(2 * part, HUBS), :] = hub_ref[...].astype(jnp.float32)
    table_ref[pl.ds(ZERO_ROW, 8), :] = jnp.zeros((8, WIDE), jnp.float32)
    step = 8

    def some_rows(block, carry):
        at = block * step
        for r in range(step):
            first = (at + r) * PICKS
            got = [table_ref[pl.ds(idx_ref[first + j], 1), :] for j in range(PICKS)]
            own = got[0]
            rest = got[1:]
            while len(rest) > 1:
                rest = [rest[k] + rest[k + 1] if k + 1 < len(rest) else rest[k] for k in range(0, len(rest), 2)]
            self_ref[pl.ds(at + r, 1), :] = own
            sum_ref[pl.ds(at + r, 1), :] = rest[0]
        return carry

    lax.fori_loop(0, 8 * ROWS // step, some_rows, 0)
    out_ref[:, :WIDE] = self_ref[...].astype(jnp.bfloat16)
    out_ref[:, WIDE:] = (sum_ref[...] / count_ref[...]).astype(jnp.bfloat16)


def fold(idx, own, other, hub, count):
    rows = 8 * ROWS
    return pl.pallas_call(
        fold_kernel,
        out_shape=jax.ShapeDtypeStruct((rows, 2 * WIDE), jnp.bfloat16),
        in_specs=[smem(), vmem(), vmem(), vmem(), vmem()],
        out_specs=vmem(),
        scratch_shapes=[
            pltpu.VMEM((ZERO_ROW + 8, WIDE), jnp.float32),
            pltpu.VMEM((rows, WIDE), jnp.float32),
            pltpu.VMEM((rows, WIDE), jnp.float32),
        ],
        compiler_params=pltpu.CompilerParams(vmem_limit_bytes=VMEM_LIMIT),
        name="fold",
    )(idx, own, other, hub, count)


def seeds_kernel(rel_ref, dl_ref, dz_ref, h_ref, ws_ref, wn_ref, dpre_ref, second_ref, tally_ref, hot_ref):
    seeds = rel_ref.shape[1]
    row_id = lax.broadcasted_iota(jnp.int32, (ROWS, 128), 0).astype(jnp.float32).astype(jnp.bfloat16)
    one = jnp.ones((ROWS, 128), jnp.bfloat16)
    none = jnp.zeros((ROWS, 128), jnp.bfloat16)

    def count(block, carry):
        cols = pl.ds(pl.multiple_of(block * 128, 128), 128)
        total = none
        for j in range(FAN2):
            line = jnp.broadcast_to(rel_ref[pl.ds(j, 1), cols].astype(jnp.bfloat16), (ROWS, 128))
            total = total + jnp.where(line == row_id, one, none)
        tally_ref[:, cols] = total
        line = jnp.broadcast_to(rel_ref[pl.ds(FAN2, 1), cols].astype(jnp.bfloat16), (ROWS, 128))
        hot_ref[:, cols] = jnp.where(line == row_id, one, none)
        return carry

    lax.fori_loop(0, seeds // 128, count, 0)
    chunk = 1024
    classes = dl_ref.shape[1]

    def gather(block, carry):
        at = pl.ds(pl.multiple_of(block * chunk, chunk), chunk)
        nbr = carry[0] + jnp.dot(tally_ref[:, at], dz_ref[at, :], preferred_element_type=jnp.float32)
        own = carry[1] + jnp.dot(hot_ref[:, at], dl_ref[at, :], preferred_element_type=jnp.float32)
        return nbr, own

    zero = jnp.zeros((ROWS, classes), jnp.float32)
    nbr, own = lax.fori_loop(0, seeds // chunk, gather, (zero, zero))
    highest = lax.Precision.HIGHEST
    last = (((1,), (1,)), ((), ()))
    h = h_ref[...].astype(jnp.float32)
    hidden = lax.dot_general(nbr, wn_ref[...].astype(jnp.float32), last, precision=highest, preferred_element_type=jnp.float32)
    hidden = hidden + lax.dot_general(own, ws_ref[...].astype(jnp.float32), last, precision=highest, preferred_element_type=jnp.float32)
    dpre_ref[...] = jnp.where(h > 0, hidden, 0.0).astype(jnp.bfloat16)
    ht = h.T
    second_ref[0] = jnp.dot(ht, own, precision=highest, preferred_element_type=jnp.float32)
    second_ref[1] = jnp.dot(ht, nbr, precision=highest, preferred_element_type=jnp.float32)


def seeds_step(rel, dl, dz, h, ws, wn):
    seeds = rel.shape[1]
    return pl.pallas_call(
        seeds_kernel,
        out_shape=(
            jax.ShapeDtypeStruct(h.shape, jnp.bfloat16),
            jax.ShapeDtypeStruct((2, h.shape[1], dl.shape[1]), jnp.float32),
        ),
        in_specs=[vmem()] * 6,
        out_specs=(vmem(), vmem()),
        scratch_shapes=[pltpu.VMEM((ROWS, seeds), jnp.bfloat16), pltpu.VMEM((ROWS, seeds), jnp.bfloat16)],
        compiler_params=pltpu.CompilerParams(vmem_limit_bytes=VMEM_LIMIT),
        name="seeds",
    )(rel, dl, dz, h, ws, wn)


def greet(peers):
    barrier = pltpu.get_barrier_semaphore()
    for peer in peers:
        pl.semaphore_signal(barrier, inc=1, device_id=peer, device_id_type=MESH)
    pl.semaphore_wait(barrier, len(peers))


def first_kernel(part_ref, out_ref, got_ref, done_ref, send_sem, recv_sem, send2_sem, recv2_sem):
    dp = lax.axis_index("dp")
    feat = lax.axis_index("feat")
    core = lax.rem(feat, 2)
    peers = []
    for flip in range(2):
        to_core = (1 - core) if flip else core
        to_feat = feat - core + to_core
        for shift in range(N_DP):
            if flip == 0 and shift == 0:
                continue
            to_dp = lax.rem(dp + shift, N_DP)
            peers.append((flip * N_DP + shift, to_dp, to_feat, to_core))
    greet([(d, f) for _, d, f, _ in peers])
    copies = []
    for slot, to_dp, to_feat, to_core in peers:
        copy = pltpu.make_async_remote_copy(
            src_ref=part_ref.at[to_core, pl.ds(pl.multiple_of(to_dp * 8, 8), 8), :],
            dst_ref=got_ref.at[slot],
            send_sem=send_sem.at[slot],
            recv_sem=recv_sem.at[slot],
            device_id=(to_dp, to_feat),
            device_id_type=MESH,
        )
        copy.start()
        copies.append(copy)
    mine = pl.ds(pl.multiple_of(dp * 8, 8), 8)
    total = part_ref[core, mine, :]
    for (slot, _, _, _), copy in zip(peers, copies):
        copy.wait_recv()
        total = total + got_ref[slot]
    done_ref[mine, :] = total
    spread = []
    for slot, to_dp, to_feat, _ in peers:
        if slot >= N_DP:
            continue
        copy = pltpu.make_async_remote_copy(
            src_ref=done_ref.at[mine, :],
            dst_ref=done_ref.at[mine, :],
            send_sem=send2_sem.at[slot],
            recv_sem=recv2_sem.at[slot],
            device_id=(to_dp, to_feat),
            device_id_type=MESH,
        )
        copy.start()
        spread.append(copy)
    for copy in copies:
        copy.wait_send()
    for copy in spread:
        copy.wait()
    out_ref[...] = done_ref[...]


def first_sum(part):
    width = part.shape[2]
    return pl.pallas_call(
        first_kernel,
        out_shape=jax.ShapeDtypeStruct((WIDE, width), jnp.float32),
        in_specs=[vmem()],
        out_specs=vmem(),
        scratch_shapes=[
            pltpu.VMEM((2 * N_DP, 8, width), jnp.float32),
            pltpu.VMEM((WIDE, width), jnp.float32),
            pltpu.SemaphoreType.DMA((2 * N_DP,)),
            pltpu.SemaphoreType.DMA((2 * N_DP,)),
            pltpu.SemaphoreType.DMA((N_DP,)),
            pltpu.SemaphoreType.DMA((N_DP,)),
        ],
        compiler_params=pltpu.CompilerParams(collective_id=1, has_side_effects=True, vmem_limit_bytes=VMEM_LIMIT),
        name="first_sum",
    )(part)


def second_kernel(part_ref, out_ref, got_ref, mid_ref, got2_ref, sems):
    dp = lax.axis_index("dp")
    feat = lax.axis_index("feat")
    along_feat = [(k, lax.rem(feat + k, N_FEAT)) for k in range(1, N_FEAT)]
    along_dp = [(k, lax.rem(dp + k, N_DP)) for k in range(1, N_DP)]
    greet([(dp, f) for _, f in along_feat] + [(d, feat) for _, d in along_dp])
    copies = []

    def push(src, dst, stage, slot, device):
        copy = pltpu.make_async_remote_copy(
            src_ref=src,
            dst_ref=dst,
            send_sem=sems.at[2 * stage, slot],
            recv_sem=sems.at[2 * stage + 1, slot],
            device_id=device,
            device_id_type=MESH,
        )
        copy.start()
        copies.append(copy)
        return copy

    scattered = [push(part_ref.at[f], got_ref.at[k], 0, k, (dp, f)) for k, f in along_feat]
    total = part_ref[feat]
    for (k, _), copy in zip(along_feat, scattered):
        copy.wait_recv()
        total = total + got_ref[k]
    mid_ref[...] = total
    summed = [push(mid_ref, got2_ref.at[k], 1, k, (d, feat)) for k, d in along_dp]
    for (k, _), copy in zip(along_dp, summed):
        copy.wait_recv()
        total = total + got2_ref[k]
    out_ref[feat] = total
    gathered = [push(out_ref.at[feat], out_ref.at[feat], 2, k, (dp, f)) for k, f in along_feat]
    for copy in gathered:
        copy.wait_recv()
    for copy in copies:
        copy.wait_send()


def second_sum(part):
    piece = part.shape[1:]
    return pl.pallas_call(
        second_kernel,
        out_shape=jax.ShapeDtypeStruct(part.shape, jnp.float32),
        in_specs=[vmem()],
        out_specs=vmem(),
        scratch_shapes=[
            pltpu.VMEM((N_FEAT,) + piece, jnp.float32),
            pltpu.VMEM(piece, jnp.float32),
            pltpu.VMEM((N_DP,) + piece, jnp.float32),
            pltpu.SemaphoreType.DMA((6, 16)),
        ],
        compiler_params=pltpu.CompilerParams(collective_id=2, has_side_effects=True, vmem_limit_bytes=VMEM_LIMIT),
        name="second_sum",
    )(part)


def body(
    x_table,
    hub_feats,
    send_rows,
    self_slot,
    nbr1,
    cnt1,
    h_saved,
    seed_self,
    nbr2,
    cnt2,
    d_logits,
    w_self2,
    w_nbr2,
):
    feat = lax.axis_index("feat")
    core = lax.rem(feat, 2)
    swap = [(i, i ^ 1) for i in range(N_FEAT)]

    mine = jnp.concatenate([x_table, hub_feats], axis=1)
    theirs = lax.ppermute(mine, "feat", swap)
    both = jnp.where(core == 0, jnp.concatenate([mine, theirs], axis=0), jnp.concatenate([theirs, mine], axis=0))
    nodes = x_table.shape[1]
    table = both[:, :nodes].T.astype(jnp.float32)
    hub = both[:, nodes:].T
    wanted = lax.dynamic_slice_in_dim(send_rows[0], core * HALF, HALF, axis=1).reshape(-1)
    outgoing = pick(wanted, table)
    own = lax.all_to_all(outgoing, "dp", split_axis=0, concat_axis=0, tiled=True)
    other = lax.ppermute(own, "feat", swap)

    kept = lax.iota(jnp.int32, FAN2)[:, None] < cnt2[None, :]
    ints = jnp.concatenate(
        [jnp.where(kept, nbr2.T, -1), seed_self[None], cnt2[None], jnp.zeros((32 - FAN2 - 2, ROWS), jnp.int32)], axis=0
    )
    ints = lax.all_gather(ints, "feat", axis=1, tiled=True)
    dl = lax.all_gather(d_logits, "feat", axis=0, tiled=True)
    dz = (dl.astype(jnp.float32) / ints[FAN2 + 1][:, None].astype(jnp.float32)).astype(jnp.bfloat16)
    rel = ints - feat * ROWS
    rel = jnp.where((rel >= 0) & (rel < ROWS), rel, -1).astype(jnp.float32)
    d_pre, second = seeds_step(rel, dl, dz, h_saved, w_self2, w_nbr2)
    lines = [[2 * z + c for z in range(N_FEAT // 2)] for c in range(2)]
    d_pre = lax.all_gather(d_pre, "feat", axis=0, tiled=True, axis_index_groups=lines)
    hidden, classes = second.shape[1:]
    second = second.reshape(2, N_FEAT, hidden // N_FEAT, classes).transpose(1, 0, 2, 3)
    second = second_sum(second).transpose(1, 0, 2, 3).reshape(2, hidden, classes)

    def half_rows(a):
        a = a.reshape(a.shape[:-1] + (N_FEAT // 2, 2, ROWS))
        return lax.dynamic_index_in_dim(a, core, axis=a.ndim - 2, keepdims=False).reshape(a.shape[:-3] + (-1,))

    count = half_rows(cnt1)
    slots = jnp.concatenate([half_rows(self_slot)[None], half_rows(nbr1)], axis=0)
    part = N_DP * HALF
    side = jnp.where(lax.rem(lax.div(slots, HALF), 2) == core, 0, part)
    place = jnp.where(slots < N_DP * CAP, side + lax.div(slots, CAP) * HALF + lax.rem(slots, HALF), slots)
    read = lax.iota(jnp.int32, PICKS)[:, None] <= count[None, :]
    place = jnp.where(read, place, ZERO_ROW).T.reshape(-1)
    rows = fold(
        place, own.reshape(part, WIDE), other.reshape(part, WIDE), hub, count[:, None].astype(jnp.float32)
    )
    summed = lax.dot_general(rows, d_pre, (((0,), (0,)), ((), ())), preferred_element_type=jnp.float32)
    width = h_saved.shape[1]
    summed = summed.reshape(2, 2, 64, width).transpose(1, 0, 2, 3).reshape(2, WIDE, width)
    first = first_sum(summed)
    return (first[:64], first[64:], second[0], second[1])


def solution(mesh):
    placed = (
        P("feat", "dp"),
        P("feat", None),
        P("dp", None, None),
        P("dp"),
        P(None, "dp"),
        P("dp"),
        P(("dp", "feat"), None),
        P(("dp", "feat")),
        P(("dp", "feat"), None),
        P(("dp", "feat")),
        P(("dp", "feat"), None),
        P(),
        P(),
    )
    return jax.shard_map(
        body,
        mesh=mesh,
        in_specs=placed,
        out_specs=(P("feat", None), P("feat", None), P(), P()),
        check_vma=False,
    )
```

time: 886 us -> 311 us (0.35)
  waiting for transfers between devices: 400 us -> 36.3 us
  local copies, waits for them, and re-layouts: 325 us -> 26.7 us
  Pallas kernels: 0 us -> 173 us
  other arithmetic: 85.9 us -> 24.5 us
  matrix products: 42.3 us -> 2.64 us
  blocking collectives: 0 us -> 22.1 us
    psum x2 -> x0, waiting for transfers between devices: 344 us -> none  [the longest x1 250 us: body(): stacked = lax.psum(stacked, ('dp', 'feat'))]
    gather x4 -> x0, local copies, waits for them, and re-layouts: 301 us -> none  [the longest x2 178 us: body(): gathered = jnp.take(lookup, picks, axis=0)]
    pallas_call x0 -> x5, Pallas kernels: none -> 173 us  [the longest x1 87 us: second_sum(): pl.pallas_call(second_kernel, out_shape=jax.ShapeDtypeStruct(part.shape,...]
    dot_general x6 -> x1, matrix products: 42.3 us -> 2.64 us  [body(): lax.dot_general(rows, d_pre, (((0,), (0,)), ((), ())), preferred_element_...]
    reduce_sum x1 -> x0, other arithmetic: 23 us -> none  [body(): jnp.sum(jnp.where(valid[:, :, None], gathered[:, 1:, :].astype(jnp.float3...]
    all_to_all x1, waiting for transfers between devices: 56.3 us -> 33.9 us  [body(): lax.all_to_all(outgoing, 'dp', split_axis=0, concat_axis=0, tiled=True)]
    select_n x3 -> x2, other arithmetic: 32.9 us -> 10.5 us  [the longest x1 10.5 us: body(): jnp.where(core == 0, jnp.concatenate([mine, theirs], axis=0), jnp.concate...]
    all_gather x0 -> x1, blocking collectives: none -> 22.1 us  [body(): ints = lax.all_gather(ints, 'feat', axis=1, tiled=True)]
  transfers between devices with their start and end apart: 5 -> 5, of which waited for: 3 -> 2; matrix products, arithmetic and copies ran while one was open for 46% -> 5% of each run, Pallas kernels for 0% -> 41%
where the time goes in v1:
time: 311 us; the launch traced here: 310 us
  Pallas kernels  173 us (56%)
  waiting for transfers between devices  36.3 us (12%)
  local copies, waits for them, and re-layouts  26.7 us (9%)
  other arithmetic  24.5 us (8%)
  blocking collectives  22.1 us (7%)
  between operations  14.3 us (5%)
  starting transfers between devices  10.1 us (3%)
    pallas_call x1, Pallas kernels, second_sum(): pl.pallas_call(second_kernel, out_shape=jax.ShapeDtypeStruct(part.shape,...  87 us
    all_to_all x1, waiting for transfers between devices, body(): lax.all_to_all(outgoing, 'dp', split_axis=0, concat_axis=0, tiled=True)  33.9 us
    pallas_call x1, Pallas kernels, fold(): pl.pallas_call(fold_kernel, out_shape=jax.ShapeDtypeStruct((rows, 2 * WID...  26.4 us
    pallas_call x1, Pallas kernels, first_sum(): pl.pallas_call(first_kernel, out_shape=jax.ShapeDtypeStruct((WIDE, width)...  26 us
    all_gather x1, blocking collectives, body(): ints = lax.all_gather(ints, 'feat', axis=1, tiled=True)  22.1 us
    pallas_call x1, Pallas kernels, pick(): pl.pallas_call(pick_kernel, out_shape=jax.ShapeDtypeStruct((N_DP, HALF, W...  20.3 us
    pallas_call x1, Pallas kernels, seeds_step(): pl.pallas_call(seeds_kernel, out_shape=(jax.ShapeDtypeStruct(h.shape, jnp...  13.5 us
    select_n x1, other arithmetic, body(): jnp.where(core == 0, jnp.concatenate([mine, theirs], axis=0), jnp.concate...  10.5 us
  transfers between devices with their start and end apart: 5, of which 2 were waited for; matrix products, arithmetic and copies ran while one was open for 5% of the time, Pallas kernels for 41%

profile of v1, /device:TPU:1, one launch (start us, length us, event | category | flops | bytes accessed | tf_op | source)
XLA Modules:
  0.0 310.0 jit_solution(1137450318732438246)
XLA Ops:
  7.2 0.0 copy-start
  7.2 1.3 copy.51
  8.4 2.0 copy.50
  10.5 7.6 %pad_maximum_fusion = bf16[64,10240]{0,1:T(8,128)(2,1)} fusion(bf16[64,2048]{0,1:T(8,128)(2,1)S(1)} %copy.51, bf16[64,8192]{0,1:T(8,128)(2,1)S(1)} %copy.50), kind=kLoop, calls=%fused_computation.2 | loop fusion | flops 2621440 | bytes 2621440 | tf_op jit(solution)/shard_map/concatenate | solution.py:324
  18.1 4.0 %copy.52 = bf16[64,10240]{1,0:T(8,128)(2,1)} copy(bf16[64,10240]{0,1:T(8,128)(2,1)} %pad_maximum_fusion) | data formatting | bytes 2621440 | tf_op jit(solution)/shard_map/concatenate | solution.py:324
  22.1 3.2 %collective-permute-start = (bf16[64,10240]{1,0:T(8,128)(2,1)}, bf16[64,10240]{1,0:T(8,128)(2,1)}, u32[]{:S(2)}, u32[]{:S(2)}) collective-permute-start(bf16[64,10240]{1,0:T(8,128)(2,1)} %copy.52), channel_id=1, source_target_pairs={{0,1},{1,0},{2,3},{3,2},{4,5},{5,4},{6,7},{7,6},{8,9},{9,8},{10,11... | collective-permute-start | bytes 3932168 | tf_op jit(solution)/shard_map/ppermute | solution.py:325
  25.3 0.0 copy-done
  25.3 0.6 copy.65
  26.0 2.3 collective-permute-done
  28.3 3.9 %copy.53 = bf16[64,10240]{0,1:T(8,128)(2,1)} copy(bf16[64,10240]{1,0:T(8,128)(2,1)} %collective-permute-done) | data formatting | bytes 2621440 | tf_op jit(solution)/shard_map/ppermute | solution.py:325
  32.2 10.5 %maximum_select_fusion = bf16[128,10240]{0,1:T(8,128)(2,1)S(1)} fusion(bf16[64,10240]{0,1:T(8,128)(2,1)} %copy.53, bf16[64,2048]{0,1:T(8,128)(2,1)S(1)} %copy.51, bf16[64,8192]{0,1:T(8,128)(2,1)S(1)} %copy.50, pred[]{:T(512)S(6)} %eq.11), kind=kLoop, calls=%fused_computation.3 | loop fusion | flops 17039360 | bytes 5242881 | tf_op jit(solution)/shard_map/jit(_where)/select_n | solution.py:326
  42.7 0.0 copy-start.1
  42.7 2.4 convert_bitcast_fusion.table_ref
  45.1 0.4 copy-done.1
  45.5 20.3 %pick.1 = bf16[16,1024,128]{2,1,0:T(8,128)(2,1)} custom-call(s32[16384]{0:T(1024)} %bitcast.49, f32[8192,128]{1,0:T(8,128)} %convert_bitcast_fusion.table_ref), custom_call_target="tpu_custom_call" | custom-call | tf_op jit(solution)/shard_map/pick/pallas_call | solution.py:51
  65.8 0.0 copy-start.6
  65.8 0.0 copy-start.4
  65.8 0.0 copy-start.10
  65.8 0.0 copy-start.11
  65.8 5.2 %all-to-all-start = ((bf16[16,1024,128]{2,1,0:T(8,128)(2,1)}), bf16[16,1024,128]{2,1,0:T(8,128)(2,1)}, u32[]{:S(2)}, u32[]{:S(2)}) async-start(bf16[16,1024,128]{2,1,0:T(8,128)(2,1)} %pick.1), calls=%async_computation | async-start | bytes 8388608 | tf_op jit(solution)/shard_map/all_to_all | solution.py:332
  71.0 0.0 all-gather.3.cloned.1.call-start
  71.1 0.0 copy-done.6
  71.1 0.8 copy.56
  71.9 0.0 all-gather.3.cloned.1.call-update
  71.9 0.0 all-gather.5.cloned.1.call-start
  71.9 0.1 pad.3.clone
  72.0 0.0 copy-done.4
  72.0 0.8 copy.57.ws_ref
  72.9 0.0 copy-done.5
  72.9 0.8 copy.58.wn_ref
  73.7 0.0 copy-done.7
  73.7 0.0 copy-done.10
  73.7 0.0 copy-done.11
  73.7 0.1 add_add_fusion
  73.8 22.1 %all_gather.9 = s32[32,4096]{1,0:T(8,128)S(1)} all-gather(s32[32,256]{1,0:T(8,128)S(1)} %add_add_fusion), channel_id=1, replica_groups=mesh['dp'=16,'feat'=16] {'feat'}, dimensions={1}, use_global_device_ids=true | all-gather | bytes 557056 | tf_op jit(solution)/shard_map/all_gather | solution.py:339
  95.9 0.9 select_convert_fusion.rel_ref
  96.8 33.9 %all-to-all-done = bf16[16,1024,128]{2,1,0:T(8,128)(2,1)} async-done(((bf16[16,1024,128]{2,1,0:T(8,128)(2,1)}), bf16[16,1024,128]{2,1,0:T(8,128)(2,1)}, u32[]{:S(2)}, u32[]{:S(2)}) %all-to-all-start) | async-done | bytes 4194336 | tf_op jit(solution)/shard_map/all_to_all | solution.py:332
  130.7 1.6 collective-permute-start.1
  132.3 2.9 divide_convert_fusion.dz_ref
  135.2 13.5 %seeds.1 = (bf16[256,512]{1,0:T(8,128)(2,1)}, f32[2,512,172]{2,1,0:T(8,128)}) custom-call(f32[32,4096]{1,0:T(8,128)} %select_convert_fusion.rel_ref, bf16[4096,172]{1,0:T(8,128)(2,1)} %all-gather.3.cloned.1.call-done.dl_ref, bf16[4096,172]{1,0:T(8,128)(2,1)} %divide_convert_fusion.dz_ref, bf16[256,512]{1,0:T(8,128)(2,1)} %h_ref.1, ...), custom_call_target="tpu_custom_call" | custom-call | tf_op jit(solution)/shard_map/seeds/pallas_call | solution.py:154
  148.8 0.0 all-gather.5.cloned.1.call-update
  148.8 0.0 copy-done.3
  148.8 0.1 reshape.77
  149.0 0.1 constant_dynamic-slice_fusion
  149.1 0.0 copy-start.2
  149.1 0.0 copy-done.8
  149.2 0.0 copy-done.9
  149.2 0.1 fusion.6
  149.4 0.4 copy.49
  149.7 1.3 reshape.79.idx_ref
  151.0 1.4 copy.55.count_ref
  152.4 1.9 slice_bitcast_fusion.hub_ref
  154.2 0.0 copy-done.2
  154.2 1.2 copy.68
  155.4 87.0 %second_sum.1 = f32[16,2,32,172]{3,2,1,0:T(8,128)} custom-call(f32[16,2,32,172]{3,2,1,0:T(8,128)} %bitcast.40), custom_call_target="tpu_custom_call" | custom-call | tf_op jit(solution)/shard_map/second_sum/pallas_call | solution.py:289
  242.4 1.3 fusion.9
  243.7 0.9 copy.61
  244.6 0.9 copy.62
  245.5 0.0 collective-permute-done.1
  245.5 26.4 %fold.1 = bf16[2048,256]{1,0:T(8,128)(2,1)} custom-call(s32[22528]{0:T(1024)} %reshape.79.idx_ref, bf16[16384,128]{1,0:T(8,128)(2,1)} %bitcast.4.own_ref, bf16[16384,128]{1,0:T(8,128)(2,1)} %bitcast.5.other_ref, bf16[2048,128]{1,0:T(8,128)(2,1)} %slice_bitcast_fusion.hub_ref, f32[2048,1]{1,0:T(8,128)} %copy.55.count_ref), custom_call_target="tpu_custom_call" | custom-call | tf_op jit(solution)/shard_map/fold/pallas_call | solution.py:97
  271.9 2.6 fusion.11
  274.6 0.8 copy.59
  275.4 26.0 %first_sum.1 = f32[128,512]{1,0:T(8,128)} custom-call(f32[2,128,512]{2,1,0:T(8,128)} %bitcast.43), custom_call_target="tpu_custom_call" | custom-call | tf_op jit(solution)/shard_map/first_sum/pallas_call | solution.py:230
  301.5 1.7 fusion.10
  (17 shorter events, 0.2 us)
Async XLA Ops:
  7.2 18.2 %copy-start = (s32[1,16,2048]{2,1,0:T(8,128)S(1)}, s32[1,16,2048]{2,1,0:T(8,128)}, u32[]{:S(2)}) copy-start(s32[1,16,2048]{2,1,0:T(8,128)} %param.15) | copy-start | bytes 393220
  22.1 6.2 %collective-permute-start = (bf16[64,10240]{1,0:T(8,128)(2,1)}, bf16[64,10240]{1,0:T(8,128)(2,1)}, u32[]{:S(2)}, u32[]{:S(2)}) collective-permute-start(bf16[64,10240]{1,0:T(8,128)(2,1)} %copy.52), channel_id=1, source_target_pairs={{0,1},{1,0},{2,3},{3,2},{4,5},{5,4},{6,7},{7,6},{8,9},{9,8},{10,11... | collective-permute-start | bytes 3932168 | tf_op jit(solution)/shard_map/ppermute | solution.py:325
  42.7 2.8 copy-start.1
  65.8 5.3 %copy-start.6 = (bf16[256,172]{0,1:T(8,128)(2,1)S(1)}, bf16[256,172]{0,1:T(8,128)(2,1)}, u32[]{:S(2)}) copy-start(bf16[256,172]{0,1:T(8,128)(2,1)} %param.23) | copy-start | bytes 264196
  65.8 6.2 %copy-start.4 = (bf16[512,172]{0,1:T(8,128)(2,1)S(1)}, bf16[512,172]{0,1:T(8,128)(2,1)}, u32[]{:S(2)}) copy-start(bf16[512,172]{0,1:T(8,128)(2,1)} %param.24) | copy-start | bytes 528388
  65.8 7.1 %copy-start.5 = (bf16[512,172]{0,1:T(8,128)(2,1)S(1)}, bf16[512,172]{0,1:T(8,128)(2,1)}, u32[]{:S(2)}) copy-start(bf16[512,172]{0,1:T(8,128)(2,1)} %param.25) | copy-start | bytes 528388
  65.8 7.9 %copy-start.7 = (s32[256,25]{0,1:T(8,128)S(1)}, s32[256,25]{0,1:T(8,128)}, u32[]{:S(2)}) copy-start(s32[256,25]{0,1:T(8,128)} %param.21) | copy-start | bytes 76804
  65.8 7.9 %copy-start.10 = (s32[256]{0:T(256)S(1)}, s32[256]{0:T(256)}, u32[]{:S(2)}) copy-start(s32[256]{0:T(256)} %param.22) | copy-start | bytes 3076
  65.8 7.9 %copy-start.11 = (s32[256]{0:T(256)S(1)}, s32[256]{0:T(256)}, u32[]{:S(2)}) copy-start(s32[256]{0:T(256)} %param.20) | copy-start | bytes 3076
  65.8 64.9 %all-to-all-start = ((bf16[16,1024,128]{2,1,0:T(8,128)(2,1)}), bf16[16,1024,128]{2,1,0:T(8,128)(2,1)}, u32[]{:S(2)}, u32[]{:S(2)}) async-start(bf16[16,1024,128]{2,1,0:T(8,128)(2,1)} %pick.1), calls=%async_computation | async-start | bytes 8388608 | tf_op jit(solution)/shard_map/all_to_all | solution.py:332
  71.0 61.3 %all-gather.3.cloned.1.call-start = ((), (), s32[]{:S(2)}) async-start(), calls=%async_computation.1 | async-start | bytes 2228224 | tf_op jit(solution)/shard_map/all_gather | solution.py:340
  71.9 200.0 %all-gather.5.cloned.1.call-start = ((), (), s32[]{:S(2)}) async-start(), calls=%async_computation.2 | async-start | bytes 2359296 | tf_op jit(solution)/shard_map/all_gather | solution.py:346
  130.7 114.8 %collective-permute-start.1 = (bf16[16,1024,128]{2,1,0:T(8,128)(2,1)}, bf16[16,1024,128]{2,1,0:T(8,128)(2,1)}, u32[]{:S(2)}, u32[]{:S(2)}) collective-permute-start(bf16[16,1024,128]{2,1,0:T(8,128)(2,1)} %all-to-all-done), channel_id=1, source_target_pairs={{0,1},{1,0},{2,3},{3,2},{4,5},{5,4},{6,7},{7,6},{8,9},{9,8},{10,11... | collective-permute-start | bytes 12582920 | tf_op jit(solution)/shard_map/ppermute | solution.py:333
  135.2 13.6 %copy-start.3 = (s32[10,4096]{1,0:T(8,128)S(1)}, s32[10,4096]{1,0:T(8,128)}, u32[]{:S(2)}) copy-start(s32[10,4096]{1,0:T(8,128)} %param.17) | copy-start | bytes 491524
  135.2 13.9 %copy-start.8 = (s32[4096]{0:T(1024)S(1)}, s32[4096]{0:T(1024)}, u32[]{:S(2)}) copy-start(s32[4096]{0:T(1024)} %param.18) | copy-start | bytes 49156
  135.2 13.9 %copy-start.9 = (s32[4096]{0:T(1024)S(1)}, s32[4096]{0:T(1024)}, u32[]{:S(2)}) copy-start(s32[4096]{0:T(1024)} %param.16) | copy-start | bytes 49156
  149.1 5.2 %copy-start.2 = (f32[2,512,172]{2,1,0:T(8,128)S(1)}, f32[2,512,172]{2,1,0:T(8,128)}, u32[]{:S(2)}) copy-start(f32[2,512,172]{2,1,0:T(8,128)} %get-tuple-element.7) | copy-start | bytes 2113540
Sparse Core Ops, SparseCore 0:
  74.3 43.2 all-gather.2
  148.9 68.4 all-gather.4

commit v2 on v1

--- a/solution.py
+++ b/solution.py
@@ -28,85 +28,146 @@
     return pl.BlockSpec(memory_space=pltpu.SMEM)
 
 
-def pick_kernel(idx_ref, table_ref, out_ref, rows_ref):
+def remote(src, dst, sems, slot, device):
+    return pltpu.make_async_remote_copy(
+        src_ref=src,
+        dst_ref=dst,
+        send_sem=sems.at[0, slot],
+        recv_sem=sems.at[1, slot],
+        device_id=device,
+        device_id_type=MESH,
+    )
+
+
+def greet(peers):
+    barrier = pltpu.get_barrier_semaphore()
+    for peer in peers:
+        pl.semaphore_signal(barrier, inc=1, device_id=peer, device_id_type=MESH)
+    pl.semaphore_wait(barrier, len(peers))
+
+
+def main_kernel(
+    send_ref, slot_ref, x_ref, hub_ref, count_ref, out_ref,
+    feats_ref, nodes_ref, stage_ref, own_ref, other_ref, table_ref, rows_ref, self_ref, sum_ref,
+    swap_sems, far_sems, near_sems,
+):
+    dp = lax.axis_index("dp")
+    feat = lax.axis_index("feat")
+    core = lax.rem(feat, 2)
+    partner = (dp, feat + 1 - 2 * core)
+    wide = [(k, lax.rem(dp + k, N_DP), lax.rem(dp + N_DP - k, N_DP)) for k in range(N_DP)]
+    greet([partner] + [(to, feat) for _, to, _ in wide[1:]])
+
+    nodes = x_ref.shape[1]
+    lane = pl.ds(pl.multiple_of(core * 64, 64), 64)
+    swaps = [
+        remote(x_ref, feats_ref.at[lane, pl.ds(0, nodes)], swap_sems, 0, partner),
+        remote(hub_ref, feats_ref.at[lane, pl.ds(nodes, HUBS)], swap_sems, 1, partner),
+    ]
+    for copy in swaps:
+        copy.start()
+    feats_ref[lane, pl.ds(0, nodes)] = x_ref[...]
+    feats_ref[lane, pl.ds(nodes, HUBS)] = hub_ref[...]
+    swaps[0].wait_recv()
+
+    def turn(block, carry):
+        at = pl.multiple_of(block * 128, 128)
+        nodes_ref[pl.ds(at, 128), :] = feats_ref[:, pl.ds(at, 128)].astype(jnp.float32).T
+        return carry
+
+    lax.fori_loop(0, nodes // 128, turn, 0)
+
     step = 32
-
-    def one_group(group, carry):
-        def some_rows(block, inner):
-            at = block * step
-            first = group * HALF + at
-            got = [table_ref[pl.ds(idx_ref[first + r], 1), :] for r in range(step)]
+    far = []
+    for k, to, _ in wide[1:] + wide[:1]:
+        first = to * HALF
+
+        def some_rows(block, carry, first=first):
+            at = pl.multiple_of(block * step, step)
+            got = [nodes_ref[pl.ds(send_ref[first + at + r], 1), :] for r in range(step)]
             for r in range(step):
                 rows_ref[pl.ds(at + r, 1), :] = got[r]
-            return inner
+            return carry
 
         lax.fori_loop(0, HALF // step, some_rows, 0)
-        out_ref[group] = rows_ref[...].astype(jnp.bfloat16)
+        if k == 0:
+            own_ref[dp] = rows_ref[...].astype(jnp.bfloat16)
+        else:
+            stage_ref[k] = rows_ref[...].astype(jnp.bfloat16)
+            copy = remote(stage_ref.at[k], own_ref.at[dp], far_sems, k, (to, feat))
+            copy.start()
+            far.append(copy)
+
+    part = N_DP * HALF
+    near = []
+    for k, _, source in wide:
+        if k:
+            far[k - 1].wait_recv()
+        copy = remote(own_ref.at[source], other_ref.at[source], near_sems, k, partner)
+        copy.start()
+        near.append(copy)
+        at = pl.multiple_of(source * HALF, HALF)
+        table_ref[pl.ds(at, HALF), :] = own_ref[source].astype(jnp.float32)
+    swaps[1].wait_recv()
+
+    def turn_hub(block, carry):
+        at = pl.multiple_of(block * 128, 128)
+        table_ref[pl.ds(2 * part + at, 128), :] = feats_ref[:, pl.ds(nodes + at, 128)].astype(jnp.float32).T
         return carry
 
-    lax.fori_loop(0, N_DP, one_group, 0)
-
-
-def pick(idx, table):
-    return pl.pallas_call(
-        pick_kernel,
-        out_shape=jax.ShapeDtypeStruct((N_DP, HALF, WIDE), jnp.bfloat16),
-        in_specs=[smem(), vmem()],
-        out_specs=vmem(),
-        scratch_shapes=[pltpu.VMEM((HALF, WIDE), jnp.float32)],
-        compiler_params=pltpu.CompilerParams(vmem_limit_bytes=VMEM_LIMIT),
-        name="pick",
-    )(idx, table)
-
-
-def fold_kernel(idx_ref, own_ref, other_ref, hub_ref, count_ref, out_ref, table_ref, self_ref, sum_ref):
-    part = N_DP * HALF
-    chunk = 1024
-
-    def fill(block, carry):
-        at = pl.multiple_of(block * chunk, chunk)
-        table_ref[pl.ds(at, chunk), :] = own_ref[pl.ds(at, chunk), :].astype(jnp.float32)
-        table_ref[pl.ds(part + at, chunk), :] = other_ref[pl.ds(at, chunk), :].astype(jnp.float32)
-        return carry
-
-    lax.fori_loop(0, part // chunk, fill, 0)
-    table_ref[pl.ds(2 * part, HUBS), :] = hub_ref[...].astype(jnp.float32)
+    lax.fori_loop(0, HUBS // 128, turn_hub, 0)
     table_ref[pl.ds(ZERO_ROW, 8), :] = jnp.zeros((8, WIDE), jnp.float32)
-    step = 8
-
-    def some_rows(block, carry):
-        at = block * step
-        for r in range(step):
+    for k, _, source in wide:
+        near[k].wait_recv()
+        at = pl.multiple_of(part + source * HALF, HALF)
+        table_ref[pl.ds(at, HALF), :] = other_ref[source].astype(jnp.float32)
+
+    unroll = 8
+
+    def some_sums(block, carry):
+        at = pl.multiple_of(block * unroll, unroll)
+        for r in range(unroll):
             first = (at + r) * PICKS
-            got = [table_ref[pl.ds(idx_ref[first + j], 1), :] for j in range(PICKS)]
-            own = got[0]
+            got = [table_ref[pl.ds(slot_ref[first + j], 1), :] for j in range(PICKS)]
             rest = got[1:]
             while len(rest) > 1:
-                rest = [rest[k] + rest[k + 1] if k + 1 < len(rest) else rest[k] for k in range(0, len(rest), 2)]
-            self_ref[pl.ds(at + r, 1), :] = own
+                rest = [rest[i] + rest[i + 1] if i + 1 < len(rest) else rest[i] for i in range(0, len(rest), 2)]
+            self_ref[pl.ds(at + r, 1), :] = got[0]
             sum_ref[pl.ds(at + r, 1), :] = rest[0]
         return carry
 
-    lax.fori_loop(0, 8 * ROWS // step, some_rows, 0)
+    lax.fori_loop(0, 8 * ROWS // unroll, some_sums, 0)
     out_ref[:, :WIDE] = self_ref[...].astype(jnp.bfloat16)
     out_ref[:, WIDE:] = (sum_ref[...] / count_ref[...]).astype(jnp.bfloat16)
-
-
-def fold(idx, own, other, hub, count):
+    for copy in swaps + far + near:
+        copy.wait_send()
+
+
+def main_step(send, slots, x, hub, count):
     rows = 8 * ROWS
+    nodes = x.shape[1]
     return pl.pallas_call(
-        fold_kernel,
+        main_kernel,
         out_shape=jax.ShapeDtypeStruct((rows, 2 * WIDE), jnp.bfloat16),
-        in_specs=[smem(), vmem(), vmem(), vmem(), vmem()],
+        in_specs=[smem(), smem(), vmem(), vmem(), vmem()],
         out_specs=vmem(),
         scratch_shapes=[
+            pltpu.VMEM((WIDE, nodes + HUBS), jnp.bfloat16),
+            pltpu.VMEM((nodes, WIDE), jnp.float32),
+            pltpu.VMEM((N_DP, HALF, WIDE), jnp.bfloat16),
+            pltpu.VMEM((N_DP, HALF, WIDE), jnp.bfloat16),
+            pltpu.VMEM((N_DP, HALF, WIDE), jnp.bfloat16),
             pltpu.VMEM((ZERO_ROW + 8, WIDE), jnp.float32),
+            pltpu.VMEM((HALF, WIDE), jnp.float32),
             pltpu.VMEM((rows, WIDE), jnp.float32),
             pltpu.VMEM((rows, WIDE), jnp.float32),
+            pltpu.SemaphoreType.DMA((2, 2)),
+            pltpu.SemaphoreType.DMA((2, N_DP)),
+            pltpu.SemaphoreType.DMA((2, N_DP)),
         ],
-        compiler_params=pltpu.CompilerParams(vmem_limit_bytes=VMEM_LIMIT),
-        name="fold",
-    )(idx, own, other, hub, count)
+        compiler_params=pltpu.CompilerParams(collective_id=3, has_side_effects=True, vmem_limit_bytes=VMEM_LIMIT),
+        name="main_step",
+    )(send, slots, x, hub, count)
 
 
 def seeds_kernel(rel_ref, dl_ref, dz_ref, h_ref, ws_ref, wn_ref, dpre_ref, second_ref, tally_ref, hot_ref):
@@ -163,13 +224,6 @@
         compiler_params=pltpu.CompilerParams(vmem_limit_bytes=VMEM_LIMIT),
         name="seeds",
     )(rel, dl, dz, h, ws, wn)
-
-
-def greet(peers):
-    barrier = pltpu.get_barrier_semaphore()
-    for peer in peers:
-        pl.semaphore_signal(barrier, inc=1, device_id=peer, device_id_type=MESH)
-    pl.semaphore_wait(barrier, len(peers))
 
 
 def first_kernel(part_ref, out_ref, got_ref, done_ref, send_sem, recv_sem, send2_sem, recv2_sem):
@@ -319,18 +373,7 @@
 ):
     feat = lax.axis_index("feat")
     core = lax.rem(feat, 2)
-    swap = [(i, i ^ 1) for i in range(N_FEAT)]
-
-    mine = jnp.concatenate([x_table, hub_feats], axis=1)
-    theirs = lax.ppermute(mine, "feat", swap)
-    both = jnp.where(core == 0, jnp.concatenate([mine, theirs], axis=0), jnp.concatenate([theirs, mine], axis=0))
-    nodes = x_table.shape[1]
-    table = both[:, :nodes].T.astype(jnp.float32)
-    hub = both[:, nodes:].T
     wanted = lax.dynamic_slice_in_dim(send_rows[0], core * HALF, HALF, axis=1).reshape(-1)
-    outgoing = pick(wanted, table)
-    own = lax.all_to_all(outgoing, "dp", split_axis=0, concat_axis=0, tiled=True)
-    other = lax.ppermute(own, "feat", swap)
 
     kept = lax.iota(jnp.int32, FAN2)[:, None] < cnt2[None, :]
     ints = jnp.concatenate(
@@ -359,9 +402,7 @@
     place = jnp.where(slots < N_DP * CAP, side + lax.div(slots, CAP) * HALF + lax.rem(slots, HALF), slots)
     read = lax.iota(jnp.int32, PICKS)[:, None] <= count[None, :]
     place = jnp.where(read, place, ZERO_ROW).T.reshape(-1)
-    rows = fold(
-        place, own.reshape(part, WIDE), other.reshape(part, WIDE), hub, count[:, None].astype(jnp.float32)
-    )
+    rows = main_step(wanted, place, x_table, hub_feats, count[:, None].astype(jnp.float32))
     summed = lax.dot_general(rows, d_pre, (((0,), (0,)), ((), ())), preferred_element_type=jnp.float32)
     width = h_saved.shape[1]
     summed = summed.reshape(2, 2, 64, width).transpose(1, 0, 2, 3).reshape(2, WIDE, width)

time: 311 us -> 322 us (1.035)
  Pallas kernels: 173 us -> 245 us
  waiting for transfers between devices: 36.3 us -> 16.2 us
  other arithmetic: 24.5 us -> 5.58 us
  local copies, waits for them, and re-layouts: 26.7 us -> 16.1 us
  starting transfers between devices: 10.1 us -> 0.08 us
    pallas_call x2 -> x1, Pallas kernels: 46.7 us -> 111 us  [main_step(): pl.pallas_call(main_kernel, out_shape=jax.ShapeDtypeStruct((rows, 2 * WID...]
    all_to_all x1 -> x0, waiting for transfers between devices: 33.9 us -> none  [body(): lax.all_to_all(outgoing, 'dp', split_axis=0, concat_axis=0, tiled=True)]
    all_gather x1, waiting for transfers between devices: 0.01 us -> 16.1 us  [body(): dl = lax.all_gather(d_logits, 'feat', axis=0, tiled=True)]
    select_n x1 -> x0, other arithmetic: 10.5 us -> none  [body(): jnp.where(core == 0, jnp.concatenate([mine, theirs], axis=0), jnp.concate...]
    pallas_call x1, Pallas kernels: 87 us -> 94.8 us  [second_sum(): pl.pallas_call(second_kernel, out_shape=jax.ShapeDtypeStruct(part.shape,...]
    concatenate x1 -> x0, other arithmetic: 7.58 us -> none  [body(): mine = jnp.concatenate([x_table, hub_feats], axis=1)]
    all_to_all x1 -> x0, starting transfers between devices: 5.21 us -> none  [body(): lax.all_to_all(outgoing, 'dp', split_axis=0, concat_axis=0, tiled=True)]
    ppermute x2 -> x0, starting transfers between devices: 4.85 us -> none  [the longest x1 3.24 us: body(): theirs = lax.ppermute(mine, 'feat', swap)]
  transfers between devices with their start and end apart: 5 -> 2, of which waited for: 2 -> 1; matrix products, arithmetic and copies ran while one was open for 5% -> 5% of each run, Pallas kernels for 41% -> 64%
where the time goes in v2:
time: 322 us
  Pallas kernels  245 us (76%)
  blocking collectives  22.9 us (7%)
  waiting for transfers between devices  16.2 us (5%)
  local copies, waits for them, and re-layouts  16.1 us (5%)
  between operations  14.3 us (4%)
  other arithmetic  5.58 us (2%)
    pallas_call x1, Pallas kernels, main_step(): pl.pallas_call(main_kernel, out_shape=jax.ShapeDtypeStruct((rows, 2 * WID...  111 us
    pallas_call x1, Pallas kernels, second_sum(): pl.pallas_call(second_kernel, out_shape=jax.ShapeDtypeStruct(part.shape,...  94.8 us
    pallas_call x1, Pallas kernels, first_sum(): pl.pallas_call(first_kernel, out_shape=jax.ShapeDtypeStruct((WIDE, width)...  25.6 us
    all_gather x1, blocking collectives, body(): ints = lax.all_gather(ints, 'feat', axis=1, tiled=True)  22.9 us
    all_gather x1, waiting for transfers between devices, body(): dl = lax.all_gather(d_logits, 'feat', axis=0, tiled=True)  16.1 us
    pallas_call x1, Pallas kernels, seeds_step(): pl.pallas_call(seeds_kernel, out_shape=(jax.ShapeDtypeStruct(h.shape, jnp...  13.5 us
    unnamed x22, local copies, waits for them, and re-layouts  7.78 us
  transfers between devices with their start and end apart: 2, of which 1 were waited for; matrix products, arithmetic and copies ran while one was open for 5% of the time, Pallas kernels for 64%

profile of v2, /device:TPU:1, one launch (start us, length us, event | category | flops | bytes accessed | tf_op | source)
XLA Modules:
  0.0 322.0 jit_solution(12547789856671709477)
XLA Ops:
  7.2 0.0 copy-start
  7.2 0.0 all-gather.3.cloned.1.call-start
  7.2 1.7 copy.45
  8.9 0.0 all-gather.3.cloned.1.call-update
  8.9 0.0 all-gather.5.cloned.1.call-start
  9.0 0.1 pad.3.clone
  9.1 1.8 copy.46.ws_ref
  10.8 1.8 copy.47.wn_ref
  12.6 0.8 bitcast_select_fusion
  13.4 0.8 add_add_fusion
  14.1 22.9 %all_gather.9 = s32[32,4096]{1,0:T(8,128)S(1)} all-gather(s32[32,256]{1,0:T(8,128)S(1)} %add_add_fusion), channel_id=1, replica_groups=mesh['dp'=16,'feat'=16] {'feat'}, dimensions={1}, use_global_device_ids=true | all-gather | bytes 557056 | tf_op jit(solution)/shard_map/all_gather | solution.py:382
  37.1 0.9 select_convert_fusion.rel_ref
  38.0 16.1 %all-gather.3.cloned.1.call-done.dl_ref = bf16[4096,172]{1,0:T(8,128)(2,1)} async-done(((bf16[256,172]{1,0:T(8,128)(2,1)}), bf16[4096,172]{1,0:T(8,128)(2,1)}) %all-gather.3.cloned.1.call-update) | async-done | bytes 1409040 | tf_op jit(solution)/shard_map/all_gather | solution.py:383
  54.2 2.9 divide_convert_fusion.dz_ref
  57.1 0.0 copy-start.4
  57.1 0.0 copy-start.5
  57.1 0.0 copy-start.3
  57.1 13.5 %seeds.1 = (bf16[256,512]{1,0:T(8,128)(2,1)}, f32[2,512,172]{2,1,0:T(8,128)}) custom-call(f32[32,4096]{1,0:T(8,128)} %select_convert_fusion.rel_ref, bf16[4096,172]{1,0:T(8,128)(2,1)} %all-gather.3.cloned.1.call-done.dl_ref, bf16[4096,172]{1,0:T(8,128)(2,1)} %divide_convert_fusion.dz_ref, bf16[256,512]{1,0:T(8,128)(2,1)} %h_ref.1, ...), custom_call_target="tpu_custom_call" | custom-call | tf_op jit(solution)/shard_map/seeds/pallas_call | solution.py:215
  70.6 0.0 all-gather.5.cloned.1.call-update
  70.6 0.0 copy-done.4
  70.6 0.0 copy-done.5
  70.7 0.0 copy-done
  70.7 0.6 copy.53
  71.3 0.0 copy-done.3
  71.4 0.1 reshape.72
  71.5 0.1 constant_dynamic-slice_fusion
  71.7 0.1 fusion.6
  71.9 0.4 copy.43
  72.2 1.3 reshape.74.slot_ref
  73.5 0.0 copy-start.2
  73.5 1.4 copy.44.count_ref
  74.9 110.7 %main_step.1 = bf16[2048,256]{1,0:T(8,128)(2,1)} custom-call(s32[16384]{0:T(1024)} %bitcast.43, s32[22528]{0:T(1024)} %reshape.74.slot_ref, bf16[64,8192]{1,0:T(8,128)(2,1)} %x_ref.1, bf16[64,2048]{1,0:T(8,128)(2,1)} %hub_ref.1, f32[2048,1]{1,0:T(8,128)} %copy.44.count_ref), custom_call_target="tpu_custom_call" | custom-call | tf_op jit(solution)/shard_map/main_step/pallas_call | solution.py:149
  185.6 0.0 copy-done.2
  185.6 1.1 copy.57
  186.7 94.8 %second_sum.1 = f32[16,2,32,172]{3,2,1,0:T(8,128)} custom-call(f32[16,2,32,172]{3,2,1,0:T(8,128)} %bitcast.34), custom_call_target="tpu_custom_call" | custom-call | tf_op jit(solution)/shard_map/second_sum/pallas_call | solution.py:343
  281.5 0.0 copy-start.1
  281.5 1.4 fusion.9
  282.9 0.9 copy.51
  283.8 0.9 copy.50
  284.7 0.0 all-gather.5.cloned.1.call-done
  284.7 0.0 copy-done.1
  284.7 2.3 fusion.11
  287.1 0.8 copy.48
  287.9 25.6 %first_sum.1 = f32[128,512]{1,0:T(8,128)} custom-call(f32[2,128,512]{2,1,0:T(8,128)} %bitcast.37), custom_call_target="tpu_custom_call" | custom-call | tf_op jit(solution)/shard_map/first_sum/pallas_call | solution.py:284
  313.5 1.7 fusion.10
  (9 shorter events, 0.1 us)
Async XLA Ops:
  7.2 63.5 %copy-start = (s32[1,16,2048]{2,1,0:T(8,128)S(1)}, s32[1,16,2048]{2,1,0:T(8,128)}, u32[]{:S(2)}) copy-start(s32[1,16,2048]{2,1,0:T(8,128)} %param.15) | copy-start | bytes 393220
  7.2 47.0 %all-gather.3.cloned.1.call-start = ((), (), s32[]{:S(2)}) async-start(), calls=%async_computation | async-start | bytes 2228224 | tf_op jit(solution)/shard_map/all_gather | solution.py:383
  8.9 275.8 %all-gather.5.cloned.1.call-start = ((), (), s32[]{:S(2)}) async-start(), calls=%async_computation.1 | async-start | bytes 2359296 | tf_op jit(solution)/shard_map/all_gather | solution.py:389
  57.1 13.5 %copy-start.4 = (s32[4096]{0:T(1024)S(1)}, s32[4096]{0:T(1024)}, u32[]{:S(2)}) copy-start(s32[4096]{0:T(1024)} %param.16) | copy-start | bytes 49156
  57.1 13.6 %copy-start.5 = (s32[4096]{0:T(1024)S(1)}, s32[4096]{0:T(1024)}, u32[]{:S(2)}) copy-start(s32[4096]{0:T(1024)} %param.18) | copy-start | bytes 49156
  57.1 14.3 %copy-start.3 = (s32[10,4096]{1,0:T(8,128)S(1)}, s32[10,4096]{1,0:T(8,128)}, u32[]{:S(2)}) copy-start(s32[10,4096]{1,0:T(8,128)} %param.17) | copy-start | bytes 491524
  73.5 112.1 %copy-start.2 = (f32[2,512,172]{2,1,0:T(8,128)S(1)}, f32[2,512,172]{2,1,0:T(8,128)}, u32[]{:S(2)}) copy-start(f32[2,512,172]{2,1,0:T(8,128)} %get-tuple-element.7) | copy-start | bytes 2113540
  281.5 3.2 %copy-start.1 = (bf16[2048,256]{1,0:T(8,128)(2,1)S(1)}, bf16[2048,256]{1,0:T(8,128)(2,1)}, u32[]{:S(2)}) copy-start(bf16[2048,256]{1,0:T(8,128)(2,1)} %main_step.1) | copy-start | bytes 3145732
Sparse Core Ops, SparseCore 0:
  10.4 43.6 all-gather.2
  70.7 35.7 all-gather.4

commit v3 on v0

v3 whole, which is shorter than its diff:
```python
import jax
import jax.numpy as jnp
from jax import lax
from jax.experimental import pallas as pl
from jax.experimental.pallas import tpu as pltpu
from jax.sharding import PartitionSpec as P

N_DP = 16
SIDE = 4
N_FEAT = 16
N_Z = 8
CAP = 2048
HALF = CAP // 2
QUARTER = HALF // 2
HUBS = 2048
NODES = 8192
ROWS = 256
GROUP = N_Z * ROWS
HIDDEN = 512
CLASSES = 172
TALL = 176
FAN1 = 10
FAN2 = 25
PICKS = 1 + FAN1
WIDE = 128
PART = N_DP * HALF
ZERO_ROW = 2 * PART + HUBS
NOTE = TALL + 64
MESH = pl.DeviceIdType.MESH
F32 = jnp.float32
BF16 = jnp.bfloat16
HIGHEST = lax.Precision.HIGHEST

TWO = [(2, 2), (2, 0), (0, 2), (2, 1), (2, 3), (1, 2), (3, 2)]
DIAGONAL = [(1, 1), (3, 3), (1, 3), (3, 1)]
NEXT = [(1, 0), (3, 0), (0, 1), (0, 3)]


def through(shift, half):
    one = 3 if half else 1
    dx, dy = shift
    if dx == 2:
        return (one, one if dy == 2 else 0)
    return (dx, one)


STAGED = [(shift, half) for shift in TWO for half in range(2)]


def main_kernel(
    send_ref, slot_ref, x_ref, hub_ref, cnt1_ref, h_ref, seed_ref, nbr2_ref, cnt2_ref, dl_ref, ws_ref, wn_ref,
    self1_ref, nbr1_ref, self2_ref, nbr2o_ref,
    feats_ref, nodes_ref, stage_ref, mid_ref, own_ref, other_ref, table_ref, rows_ref,
    note_ref, gn_ref, gs_ref, gnt_ref, gst_ref, dpre_ref, second_ref, extra_ref, piece_ref, pieces_ref, column_ref, columns_ref, final_ref,
    self_ref, sum_ref, acc_ref, part_ref, theirs_ref, got_ref, done_ref,
    swap_sems, mid_sems, far_sems, near_sems, note_up, note_down, note_over,
    dpre_up, dpre_down, over_sems, z_sems, dp_sems, z2_sems, first_sems, first2_sems,
):
    dp = lax.axis_index("dp")
    feat = lax.axis_index("feat")
    core = lax.rem(feat, 2)
    z = lax.div(feat, 2)
    px = lax.div(dp, SIDE)
    py = lax.rem(dp, SIDE)
    partner = (dp, feat + 1 - 2 * core)
    pending = []

    def at_shift(dx, dy):
        return lax.rem(px + dx + SIDE, SIDE) * SIDE + lax.rem(py + dy + SIDE, SIDE)

    def z_feat(step):
        return lax.rem(z + step + N_Z, N_Z) * 2 + core

    def push(src, dst, sems, slot, device):
        copy = pltpu.make_async_remote_copy(
            src_ref=src,
            dst_ref=dst,
            send_sem=sems.at[0, slot],
            recv_sem=sems.at[1, slot],
            device_id=device,
            device_id_type=MESH,
        )
        copy.start()
        pending.append(copy)
        return copy

    barrier = pltpu.get_barrier_semaphore()
    peers = [partner]
    peers += [(at_shift(k // SIDE, k % SIDE), feat) for k in range(1, N_DP)]
    peers += [(dp, z_feat(k)) for k in range(1, N_Z)]
    for peer in peers:
        pl.semaphore_signal(barrier, inc=1, device_id=peer, device_id_type=MESH)
    pl.semaphore_wait(barrier, len(peers))

    lane = pl.ds(pl.multiple_of(core * 64, 64), 64)
    swap_x = push(x_ref, feats_ref.at[lane, pl.ds(0, NODES)], swap_sems, 0, partner)
    swap_hub = push(hub_ref, feats_ref.at[lane, pl.ds(NODES, HUBS)], swap_sems, 1, partner)

    cnt2 = cnt2_ref[...]
    kept = lax.broadcasted_iota(jnp.int32, (FAN2, ROWS), 0) < cnt2
    named = jnp.concatenate([jnp.where(kept, nbr2_ref[...], N_FEAT * ROWS), seed_ref[...]], axis=0)
    high = lax.div(named, ROWS)
    low = named - high * ROWS
    blank = jnp.zeros((32 - FAN2 - 1, ROWS), jnp.int32)
    fours = jnp.zeros((32 - FAN2 - 2, ROWS), jnp.int32)
    note_ref[feat, pl.ds(0, TALL), :] = jnp.concatenate(
        [dl_ref[...].astype(F32), jnp.zeros((TALL - CLASSES, ROWS), F32)], axis=0
    ).astype(BF16)
    note_ref[feat, pl.ds(TALL, 32), :] = jnp.concatenate([high, cnt2, fours], axis=0).astype(F32).astype(BF16)
    note_ref[feat, pl.ds(TALL + 32, 32), :] = jnp.concatenate([low, blank], axis=0).astype(F32).astype(BF16)

    class Ring:
        def __init__(self, view, up, down, over=None):
            self.view, self.up, self.down, self.over = view, up, down, over
            self.from_below, self.from_above, self.crossed = {}, {}, []

        def send_up(self, step):
            block = self.view(1 - step)
            self.from_below[step] = push(block, block, self.up, step - 1, (dp, z_feat(1)))

        def send_down(self, step):
            block = self.view(step - 1)
            self.from_above[step] = push(block, block, self.down, step - 1, (dp, z_feat(-1)))

        def cross(self, step):
            if self.over is not None:
                block = self.view(step)
                self.crossed.append(push(block, block, self.over, len(self.crossed), partner))

        def start(self):
            self.send_up(1)
            self.send_down(1)
            self.cross(0)

        def take(self, step):
            self.from_below[step].wait_recv()
            if step < 4:
                self.send_up(step + 1)
            self.cross(-step)
            if step < 4:
                self.from_above[step].wait_recv()
                if step < 3:
                    self.send_down(step + 1)
                self.cross(step)

    notes = Ring(lambda step: note_ref.at[z_feat(step)], note_up, note_down, note_over)
    notes.start()

    feats_ref[lane, pl.ds(0, NODES)] = x_ref[...]
    feats_ref[lane, pl.ds(NODES, HUBS)] = hub_ref[...]
    swap_x.wait_recv()
    nodes_flat = nodes_ref.reshape(NODES, WIDE)
    table_flat = table_ref.reshape(ZERO_ROW + 8, WIDE)
    rows_flat = rows_ref.reshape(QUARTER, WIDE)

    def turn(block, carry):
        at = pl.multiple_of(block * 128, 128)
        nodes_flat[pl.ds(at, 128), :] = feats_ref[:, pl.ds(at, 128)].astype(F32).T
        return carry

    lax.fori_loop(0, NODES // 128, turn, 0)

    far = {}
    staged = {}

    def pick(shift, half):
        to = at_shift(*shift)
        first = to * HALF + half * QUARTER
        unroll = 32

        def some_rows(block, carry):
            at = pl.multiple_of(block * unroll, unroll)
            got = [nodes_ref[send_ref[first + at + r]] for r in range(unroll)]
            for r in range(unroll):
                rows_ref[at + r] = got[r]
            return carry

        lax.fori_loop(0, QUARTER // unroll, some_rows, 0)
        slot = 2 * (shift[0] * SIDE + shift[1]) + half
        if shift == (0, 0):
            own_ref[dp, half] = rows_flat[...].astype(BF16)
            return
        stage_ref[slot] = rows_flat[...].astype(BF16)
        if (shift, half) in STAGED:
            s = STAGED.index((shift, half))
            staged[s] = push(stage_ref.at[slot], mid_ref.at[s], mid_sems, s, (at_shift(*through(shift, half)), feat))
        else:
            far[slot] = push(stage_ref.at[slot], own_ref.at[dp, half], far_sems, slot, (to, feat))

    def pass_on(s):
        shift, half = STAGED[s]
        mx, my = through(shift, half)
        slot = 2 * (shift[0] * SIDE + shift[1]) + half
        staged[s].wait_recv()
        source = at_shift(-mx, -my)
        to = at_shift(shift[0] - mx, shift[1] - my)
        far[slot] = push(mid_ref.at[s], own_ref.at[source, half], far_sems, slot, (to, feat))

    near = {}

    def arrive(shift, half):
        slot = 2 * (shift[0] * SIDE + shift[1]) + half
        source = at_shift(-shift[0], -shift[1])
        if slot in far:
            far[slot].wait_recv()
        near[slot] = push(own_ref.at[source, half], other_ref.at[source, half], near_sems, slot, partner)
        at = pl.multiple_of(source * HALF + half * QUARTER, QUARTER)
        table_flat[pl.ds(at, QUARTER), :] = own_ref[source, half].astype(F32)

    def cross(shift, half):
        slot = 2 * (shift[0] * SIDE + shift[1]) + half
        source = at_shift(-shift[0], -shift[1])
        near[slot].wait_recv()
        at = pl.multiple_of(PART + source * HALF + half * QUARTER, QUARTER)
        table_flat[pl.ds(at, QUARTER), :] = other_ref[source, half].astype(F32)

    for number, shift in enumerate(TWO):
        for half in range(2):
            pick(shift, half)
        if number in (2, 4, 6):
            notes.take(number // 2)
    for shift in DIAGONAL:
        for half in range(2):
            pick(shift, half)
    notes.take(4)
    for s in range(len(STAGED)):
        pass_on(s)
    for copy in notes.crossed:
        copy.wait_recv()

    row_id = lax.broadcasted_iota(jnp.int32, (ROWS, 128), 0).astype(F32).astype(BF16)
    one = jnp.ones((ROWS, 128), BF16)
    none = jnp.zeros((ROWS, 128), BF16)
    both_last = (((1,), (1,)), ((), ()))
    mine = jnp.full((32, ROWS), feat, jnp.int32).astype(F32)
    for ref in (gn_ref, gs_ref, gnt_ref, gst_ref):
        ref[...] = jnp.zeros_like(ref)

    def one_device(f, carry):
        high_here = note_ref[f, pl.ds(TALL, 32), :].astype(F32)
        low_here = note_ref[f, pl.ds(TALL + 32, 32), :].astype(F32)
        place = jnp.where(high_here == mine, low_here, -1.0)
        counts = high_here[FAN2 + 1 : FAN2 + 2, :]
        tallies, hots = [], []
        for side in range(ROWS // 128):
            total = none
            for j in range(FAN2 + 1):
                line = place[j : j + 1, side * 128 : side * 128 + 128].astype(BF16)
                match = jnp.where(jnp.broadcast_to(line, (ROWS, 128)) == row_id, one, none)
                if j < FAN2:
                    total = total + match
                else:
                    hots.append(match)
            tallies.append(total)
        tally = jnp.concatenate(tallies, axis=1)
        hot = jnp.concatenate(hots, axis=1)
        dl = note_ref[f, pl.ds(0, TALL), :]
        dz = (dl.astype(F32) / counts).astype(BF16)
        gn_ref[...] += lax.dot_general(tally, dz, both_last, preferred_element_type=F32)
        gs_ref[...] += lax.dot_general(hot, dl, both_last, preferred_element_type=F32)
        gnt_ref[...] += lax.dot_general(dz, tally, both_last, preferred_element_type=F32)
        gst_ref[...] += lax.dot_general(dl, hot, both_last, preferred_element_type=F32)
        return carry

    lax.fori_loop(0, N_FEAT, one_device, 0)
    h = h_ref[...].astype(F32)
    hidden = jnp.dot(gn_ref[:, :CLASSES], wn_ref[...].astype(F32), precision=HIGHEST, preferred_element_type=F32)
    hidden += jnp.dot(gs_ref[:, :CLASSES], ws_ref[...].astype(F32), precision=HIGHEST, preferred_element_type=F32)
    dpre_ref[z] = jnp.where(h > 0, hidden, 0.0).T.astype(BF16)
    second_ref[0] = jnp.dot(gst_ref[...], h, precision=HIGHEST, preferred_element_type=F32)
    second_ref[1] = jnp.dot(gnt_ref[...], h, precision=HIGHEST, preferred_element_type=F32)
    rows_ring = Ring(lambda step: dpre_ref.at[lax.rem(z + step + N_Z, N_Z)], dpre_up, dpre_down)
    rows_ring.start()
    second_over = push(second_ref.at[1 - core], extra_ref, over_sems, 0, partner)

    for shift in NEXT:
        for half in range(2):
            pick(shift, half)
    rows_ring.take(1)
    for half in range(2):
        pick((0, 0), half)
    second_over.wait_recv()
    column_ref[...] = second_ref[core] + extra_ref[...]

    def piece(step):
        to = lax.rem(z + step + N_Z, N_Z)
        tall = pl.ds(pl.multiple_of(lax.div(to, 4) * (TALL // 2), 8), TALL // 2)
        return tall, pl.ds(pl.multiple_of(lax.rem(to, 4) * 128, 128), 128)

    scattered = [push(column_ref.at[piece(k)], pieces_ref.at[k], z_sems, k, (dp, z_feat(k))) for k in range(1, N_Z)]

    swap_hub.wait_recv()

    def turn_hub(block, carry):
        at = pl.multiple_of(block * 128, 128)
        table_flat[pl.ds(2 * PART + at, 128), :] = feats_ref[:, pl.ds(NODES + at, 128)].astype(F32).T
        return carry

    lax.fori_loop(0, HUBS // 128, turn_hub, 0)
    table_flat[pl.ds(ZERO_ROW, 8), :] = jnp.zeros((8, WIDE), F32)

    order = [(shift, half) for shift in [(0, 0)] + DIAGONAL + TWO + NEXT for half in range(2)]
    for number, (shift, half) in enumerate(order):
        arrive(shift, half)
        if number == 16:
            rows_ring.take(2)
    total = column_ref[piece(0)]
    for k, copy in enumerate(scattered):
        copy.wait_recv()
        total = total + pieces_ref[k + 1]
    piece_ref[...] = total
    for shift, half in order:
        cross(shift, half)
    summed = [
        push(piece_ref, columns_ref.at[k], dp_sems, k, (at_shift(k // SIDE, k % SIDE), feat)) for k in range(1, N_DP)
    ]
    rows_ring.take(3)

    self_flat = self_ref.reshape(ROWS, WIDE)
    sum_flat = sum_ref.reshape(ROWS, WIDE)
    unroll = 8

    def fold(step):
        of = lax.rem(z + step + N_Z, N_Z)
        base = of * ROWS

        def some_sums(block, carry):
            at = pl.multiple_of(block * unroll, unroll)
            for r in range(unroll):
                got = [table_ref[slot_ref[j * GROUP + base + at + r]] for j in range(PICKS)]
                rest = got[1:]
                while len(rest) > 1:
                    rest = [rest[i] + rest[i + 1] if i + 1 < len(rest) else rest[i] for i in range(0, len(rest), 2)]
                self_ref[at + r] = got[0]
                sum_ref[at + r] = rest[0]
            return carry

        lax.fori_loop(0, ROWS // unroll, some_sums, 0)
        count = jnp.broadcast_to(cnt1_ref[of].astype(F32), (WIDE, ROWS)).T
        own = self_flat[...].astype(BF16)
        mean = (sum_flat[...] / count).astype(BF16)
        both = jnp.concatenate([own, mean], axis=1)
        product = jnp.dot(dpre_ref[of], both, preferred_element_type=F32)
        if step == 0:
            acc_ref[...] = product
        else:
            acc_ref[...] += product

    gathered = []
    for number, step in enumerate((0, -1, 1, -2, 2, -3, 3, -4)):
        fold(step)
        if number == 3:
            rows_ring.take(4)
            total = piece_ref[...]
            for k, copy in enumerate(summed):
                copy.wait_recv()
                total = total + columns_ref[k + 1]
            mine_tall, mine_lanes = piece(0)
            block = final_ref.at[core, mine_tall, mine_lanes]
            final_ref[core, mine_tall, mine_lanes] = total
            for k in range(1, N_Z):
                gathered.append(push(block, block, z2_sems, k, (dp, z_feat(k))))
        if number == 6:
            for copy in gathered:
                copy.wait_recv()
            second_back = push(final_ref.at[core], final_ref.at[core], over_sems, 1, partner)

    part_ref[...] = acc_ref[...].T
    first_over = [
        push(
            part_ref.at[pl.ds(pl.multiple_of(64 * (2 * i + 1 - core), 64), 64), :],
            theirs_ref.at[i],
            over_sems,
            2 + i,
            partner,
        )
        for i in range(2)
    ]
    second_back.wait_recv()
    self2_ref[...] = final_ref[0, :CLASSES, :]
    nbr2o_ref[...] = final_ref[1, :CLASSES, :]
    for i in range(2):
        first_over[i].wait_recv()
        mine_here = part_ref[pl.ds(pl.multiple_of(64 * (2 * i + core), 64), 64), :] + theirs_ref[i]
        part_ref[pl.ds(pl.multiple_of(64 * (2 * i + core), 64), 64), :] = mine_here

    def eight(to):
        return pl.ds(pl.multiple_of(lax.div(to, 8) * 128 + core * 64 + lax.rem(to, 8) * 8, 8), 8)

    spread = []
    for k in range(1, N_DP):
        to = at_shift(k // SIDE, k % SIDE)
        spread.append(push(part_ref.at[eight(to), :], got_ref.at[k], first_sems, k, (to, feat)))
    total = part_ref[eight(dp), :]
    for k, copy in enumerate(spread):
        copy.wait_recv()
        total = total + got_ref[k + 1]
    done_ref[dp] = total
    last = []
    for k in range(1, N_DP):
        to = at_shift(k // SIDE, k % SIDE)
        last.append(push(done_ref.at[dp], done_ref.at[dp], first2_sems, k, (to, feat)))
    for copy in last:
        copy.wait_recv()
    for k in range(8):
        self1_ref[pl.ds(8 * k, 8), :] = done_ref[k]
        nbr1_ref[pl.ds(8 * k, 8), :] = done_ref[8 + k]
    for copy in pending:
        copy.wait_send()


def main_step(send, slots, x, hub, cnt1, h, seed, nbr2, cnt2, dl, ws, wn):
    smem = pl.BlockSpec(memory_space=pltpu.SMEM)
    vmem = pl.BlockSpec(memory_space=pltpu.VMEM)
    dma = pltpu.SemaphoreType.DMA
    return pl.pallas_call(
        main_kernel,
        out_shape=(
            jax.ShapeDtypeStruct((64, HIDDEN), F32),
            jax.ShapeDtypeStruct((64, HIDDEN), F32),
            jax.ShapeDtypeStruct((CLASSES, HIDDEN), F32),
            jax.ShapeDtypeStruct((CLASSES, HIDDEN), F32),
        ),
        in_specs=[smem, smem] + [vmem] * 10,
        out_specs=(vmem,) * 4,
        scratch_shapes=[
            pltpu.VMEM((WIDE, NODES + HUBS), BF16),
            pltpu.VMEM((NODES, 1, WIDE), F32),
            pltpu.VMEM((2 * N_DP, QUARTER, WIDE), BF16),
            pltpu.VMEM((len(STAGED), QUARTER, WIDE), BF16),
            pltpu.VMEM((N_DP, 2, QUARTER, WIDE), BF16),
            pltpu.VMEM((N_DP, 2, QUARTER, WIDE), BF16),
            pltpu.VMEM((ZERO_ROW + 8, 1, WIDE), F32),
            pltpu.VMEM((QUARTER, 1, WIDE), F32),
            pltpu.VMEM((N_FEAT, NOTE, ROWS), BF16),
            pltpu.VMEM((ROWS, TALL), F32),
            pltpu.VMEM((ROWS, TALL), F32),
            pltpu.VMEM((TALL, ROWS), F32),
            pltpu.VMEM((TALL, ROWS), F32),
            pltpu.VMEM((N_Z, HIDDEN, ROWS), BF16),
            pltpu.VMEM((2, TALL, HIDDEN), F32),
            pltpu.VMEM((TALL, HIDDEN), F32),
            pltpu.VMEM((TALL // 2, 128), F32),
            pltpu.VMEM((N_Z, TALL // 2, 128), F32),
            pltpu.VMEM((TALL, HIDDEN), F32),
            pltpu.VMEM((N_DP, TALL // 2, 128), F32),
            pltpu.VMEM((2, TALL, HIDDEN), F32),
            pltpu.VMEM((ROWS, 1, WIDE), F32),
            pltpu.VMEM((ROWS, 1, WIDE), F32),
            pltpu.VMEM((HIDDEN, 2 * WIDE), F32),
            pltpu.VMEM((2 * WIDE, HIDDEN), F32),
            pltpu.VMEM((2, 64, HIDDEN), F32),
            pltpu.VMEM((N_DP, 8, HIDDEN), F32),
            pltpu.VMEM((N_DP, 8, HIDDEN), F32),
            dma((2, 2)),
            dma((2, len(STAGED))),
            dma((2, 2 * N_DP)),
            dma((2, 2 * N_DP)),
            dma((2, 4)),
            dma((2, 4)),
            dma((2, N_Z)),
            dma((2, 4)),
            dma((2, 4)),
            dma((2, 4)),
            dma((2, N_Z)),
            dma((2, N_DP)),
            dma((2, N_Z)),
            dma((2, N_DP)),
            dma((2, N_DP)),
        ],
        compiler_params=pltpu.CompilerParams(
            collective_id=1, has_side_effects=True, vmem_limit_bytes=60 * 1024 * 1024
        ),
        name="main_step",
    )(send, slots, x, hub, cnt1, h, seed, nbr2, cnt2, dl, ws, wn)


def body(
    x_table,
    hub_feats,
    send_rows,
    self_slot,
    nbr1,
    cnt1,
    h_saved,
    seed_self,
    nbr2,
    cnt2,
    d_logits,
    w_self2,
    w_nbr2,
):
    core = lax.rem(lax.axis_index("feat"), 2)
    send = lax.dynamic_slice_in_dim(send_rows[0], core * HALF, HALF, axis=1).reshape(-1)

    def half_rows(a):
        a = a.reshape(a.shape[:-1] + (N_Z, 2, ROWS))
        return lax.dynamic_index_in_dim(a, core, axis=a.ndim - 2, keepdims=False).reshape(a.shape[:-3] + (-1,))

    count = half_rows(cnt1)
    slots = jnp.concatenate([half_rows(self_slot)[None], half_rows(nbr1)], axis=0)
    side = jnp.where(lax.rem(lax.div(slots, HALF), 2) == core, 0, PART)
    place = jnp.where(slots < N_DP * CAP, side + lax.div(slots, CAP) * HALF + lax.rem(slots, HALF), slots)
    read = lax.iota(jnp.int32, PICKS)[:, None] <= count[None, :]
    place = jnp.where(read, place, ZERO_ROW).reshape(-1)
    self1, nbr1_out, self2, nbr2_out = main_step(
        send,
        place,
        x_table,
        hub_feats,
        count.reshape(N_Z, 1, ROWS),
        h_saved,
        seed_self[None],
        nbr2.T,
        cnt2[None],
        d_logits.T,
        w_self2.T,
        w_nbr2.T,
    )
    return (self1, nbr1_out, self2.T, nbr2_out.T)


def solution(mesh):
    placed = (
        P("feat", "dp"),
        P("feat", None),
        P("dp", None, None),
        P("dp"),
        P(None, "dp"),
        P("dp"),
        P(("dp", "feat"), None),
        P(("dp", "feat")),
        P(("dp", "feat"), None),
        P(("dp", "feat")),
        P(("dp", "feat"), None),
        P(),
        P(),
    )
    return jax.shard_map(
        body,
        mesh=mesh,
        in_specs=placed,
        out_specs=(P("feat", None), P("feat", None), P(), P()),
        check_vma=False,
    )
```

time: 886 us -> 139 us (0.16); the launches traced: 876 us -> 139 us
  waiting for transfers between devices: 400 us -> 0 us
  local copies, waits for them, and re-layouts: 325 us -> 8.29 us
  Pallas kernels: 0 us -> 129 us
  other arithmetic: 85.9 us -> 0.77 us
  matrix products: 42.3 us -> 0 us
  between operations: 14.5 us -> 0.77 us
    psum x2 -> x0, waiting for transfers between devices: 344 us -> none  [the longest x1 250 us: body(): stacked = lax.psum(stacked, ('dp', 'feat'))]
    gather x4 -> x0, local copies, waits for them, and re-layouts: 301 us -> none  [the longest x2 178 us: body(): gathered = jnp.take(lookup, picks, axis=0)]
    pallas_call x0 -> x1, Pallas kernels: none -> 129 us  [main_step(): pl.pallas_call(main_kernel, out_shape=(jax.ShapeDtypeStruct((64, HIDDEN),...]
    all_to_all x1 -> x0, waiting for transfers between devices: 56.3 us -> none  [body(): lax.all_to_all(outgoing, 'dp', split_axis=0, concat_axis=0, tiled=True)]
    dot_general x6 -> x0, matrix products: 42.3 us -> none  [the longest x1 32.3 us: body(): lax.dot_general(tallies.astype(jnp.bfloat16), dz_mean, dims, preferred_el...]
    select_n x3 -> x1, other arithmetic: 32.9 us -> 0.73 us  [body(): place = jnp.where(read, place, ZERO_ROW).reshape(-1)]
    concatenate x2 -> x1, other arithmetic: 24.8 us -> 0.02 us  [body(): jnp.concatenate([half_rows(self_slot)[None], half_rows(nbr1)], axis=0)]
    reduce_sum x1 -> x0, other arithmetic: 23 us -> none  [body(): jnp.sum(jnp.where(valid[:, :, None], gathered[:, 1:, :].astype(jnp.float3...]
  transfers between devices with their start and end apart: 5 -> 0, of which waited for: 3 -> 0; matrix products, arithmetic and copies ran while one was open for 46% -> 0% of each run, Pallas kernels for 0% -> 0%
where the time goes in v3:
time: 139 us
  Pallas kernels  129 us (93%)
  local copies, waits for them, and re-layouts  8.29 us (6%)
    pallas_call x1, Pallas kernels, main_step(): pl.pallas_call(main_kernel, out_shape=(jax.ShapeDtypeStruct((64, HIDDEN),...  129 us
    unnamed x18, local copies, waits for them, and re-layouts  6.33 us

profile of v3, /device:TPU:1, one launch (start us, length us, event | category | flops | bytes accessed | tf_op | source)
XLA Modules:
  0.0 138.9 jit_solution(13628523589214391781)
XLA Ops:
  0.6 0.0 copy-start
  0.6 0.0 copy-start.3
  0.7 0.8 reshape.36
  1.5 0.7 reshape.35
  2.2 0.0 copy-start.4
  2.3 0.6 copy-done.4
  2.9 0.0 copy-done
  2.9 0.6 copy.17
  3.5 0.0 copy-done.3
  3.5 0.1 reshape.37
  3.7 0.2 dynamic-slice_reduce_fusion
  4.0 0.7 fusion.5.slot_ref
  4.8 129.1 %main_step.1 = (f32[64,512]{1,0:T(8,128)}, f32[64,512]{1,0:T(8,128)}, f32[172,512]{1,0:T(8,128)}, f32[172,512]{1,0:T(8,128)}) custom-call(s32[16384]{0:T(1024)} %bitcast.20, s32[22528]{0:T(1024)} %fusion.5.slot_ref, bf16[64,8192]{1,0:T(8,128)(2,1)} %x_ref.1, bf16[64,2048]{1,0:T(8,128)(2,1)} %hub_ref.1, s32[8,1,256]{2,1,0:T(1,128)} %copy-done.4, ...), custom_call_target="tpu_custom_call" | custom-call | tf_op jit(solution)/shard_map/main_step/pallas_call | solution.py:416
  133.8 0.0 copy-start.2
  133.9 1.6 %copy.23 = f32[64,512]{1,0:T(8,128)} copy(f32[64,512]{1,0:T(8,128)} %get-tuple-element.18) | data formatting | bytes 262144
  135.5 1.6 %copy.24 = f32[64,512]{1,0:T(8,128)} copy(f32[64,512]{1,0:T(8,128)} %get-tuple-element.19) | data formatting | bytes 262144
  137.0 0.0 copy-done.2
  137.0 0.0 copy-start.1
  137.0 0.7 copy.25
  137.8 0.4 copy-done.1
  138.2 0.7 copy.26
  (8 shorter events, 0.2 us)
Async XLA Ops:
  0.6 2.2 %copy-start = (s32[1,16,2048]{2,1,0:T(8,128)S(1)}, s32[1,16,2048]{2,1,0:T(8,128)}, u32[]{:S(2)}) copy-start(s32[1,16,2048]{2,1,0:T(8,128)} %param.15) | copy-start | bytes 393220
  0.6 2.9 %copy-start.3 = (s32[10,4096]{1,0:T(8,128)S(1)}, s32[10,4096]{1,0:T(8,128)}, u32[]{:S(2)}) copy-start(s32[10,4096]{1,0:T(8,128)} %param.17) | copy-start | bytes 491524
  2.2 0.6 copy-start.4
  133.8 3.2 %copy-start.2 = (f32[172,512]{1,0:T(8,128)S(1)}, f32[172,512]{1,0:T(8,128)}, u32[]{:S(2)}) copy-start(f32[172,512]{1,0:T(8,128)} %get-tuple-element.10) | copy-start | bytes 1056772
  137.0 1.1 copy-start.1

commit v4 on v3

--- a/solution.py
+++ b/solution.py
@@ -25,7 +25,8 @@
 WIDE = 128
 PART = N_DP * HALF
 ZERO_ROW = 2 * PART + HUBS
-NOTE = TALL + 64
+NOTE = TALL + 32
+NAMES = FAN2 + 1
 MESH = pl.DeviceIdType.MESH
 F32 = jnp.float32
 BF16 = jnp.bfloat16
@@ -48,12 +49,12 @@
 
 
 def main_kernel(
-    send_ref, slot_ref, x_ref, hub_ref, cnt1_ref, h_ref, seed_ref, nbr2_ref, cnt2_ref, dl_ref, ws_ref, wn_ref,
+    send_rows_ref, self_slot_ref, slots_ref, x_ref, hub_ref, cnt1_ref, h_ref, seed_ref, nbr2_ref, cnt2_ref, dl_ref, ws_ref, wn_ref,
     self1_ref, nbr1_ref, self2_ref, nbr2o_ref,
     feats_ref, nodes_ref, stage_ref, mid_ref, own_ref, other_ref, table_ref, rows_ref,
-    note_ref, gn_ref, gs_ref, gnt_ref, gst_ref, dpre_ref, second_ref, extra_ref, piece_ref, pieces_ref, column_ref, columns_ref, final_ref,
+    send_ref, place_ref, slot_ref, code_ref, note_ref, gnt_ref, gst_ref, dpre_ref, second_ref, extra_ref, piece_ref, pieces_ref, column_ref, columns_ref, final_ref,
     self_ref, sum_ref, acc_ref, part_ref, theirs_ref, got_ref, done_ref,
-    swap_sems, mid_sems, far_sems, near_sems, note_up, note_down, note_over,
+    index_sems, swap_sems, mid_sems, far_sems, near_sems, note_up, note_down, note_over,
     dpre_up, dpre_down, over_sems, z_sems, dp_sems, z2_sems, first_sems, first2_sems,
 ):
     dp = lax.axis_index("dp")
@@ -84,6 +85,11 @@
         pending.append(copy)
         return copy
 
+    wanted = pltpu.make_async_copy(
+        send_rows_ref.at[0, :, pl.ds(pl.multiple_of(core * HALF, HALF), HALF)], send_ref, index_sems.at[0]
+    )
+    wanted.start()
+
     barrier = pltpu.get_barrier_semaphore()
     peers = [partner]
     peers += [(at_shift(k // SIDE, k % SIDE), feat) for k in range(1, N_DP)]
@@ -96,18 +102,21 @@
     swap_x = push(x_ref, feats_ref.at[lane, pl.ds(0, NODES)], swap_sems, 0, partner)
     swap_hub = push(hub_ref, feats_ref.at[lane, pl.ds(NODES, HUBS)], swap_sems, 1, partner)
 
+    def code(row):
+        power = jnp.where((row & 128) != 0, 2.0, 1.0)
+        for bit in range(1, 5):
+            power = power * jnp.where((row & (128 << bit)) != 0, 2.0 ** (2**bit), 1.0)
+        return power * (128 + (row & 127)).astype(F32)
+
     cnt2 = cnt2_ref[...]
     kept = lax.broadcasted_iota(jnp.int32, (FAN2, ROWS), 0) < cnt2
-    named = jnp.concatenate([jnp.where(kept, nbr2_ref[...], N_FEAT * ROWS), seed_ref[...]], axis=0)
-    high = lax.div(named, ROWS)
-    low = named - high * ROWS
-    blank = jnp.zeros((32 - FAN2 - 1, ROWS), jnp.int32)
-    fours = jnp.zeros((32 - FAN2 - 2, ROWS), jnp.int32)
+    names = jnp.concatenate([jnp.where(kept, code(nbr2_ref[...]), 0.0), code(seed_ref[...]), cnt2.astype(F32)], axis=0)
     note_ref[feat, pl.ds(0, TALL), :] = jnp.concatenate(
         [dl_ref[...].astype(F32), jnp.zeros((TALL - CLASSES, ROWS), F32)], axis=0
     ).astype(BF16)
-    note_ref[feat, pl.ds(TALL, 32), :] = jnp.concatenate([high, cnt2, fours], axis=0).astype(F32).astype(BF16)
-    note_ref[feat, pl.ds(TALL + 32, 32), :] = jnp.concatenate([low, blank], axis=0).astype(F32).astype(BF16)
+    note_ref[feat, pl.ds(TALL, 32), :] = jnp.concatenate(
+        [names, jnp.zeros((32 - NAMES - 1, ROWS), F32)], axis=0
+    ).astype(BF16)
 
     class Ring:
         def __init__(self, view, up, down, over=None):
@@ -148,29 +157,40 @@
 
     feats_ref[lane, pl.ds(0, NODES)] = x_ref[...]
     feats_ref[lane, pl.ds(NODES, HUBS)] = hub_ref[...]
+
+    def places(slots):
+        mine_first = jnp.where(((slots >> 10) & 1) == core, 0, PART)
+        return jnp.where(slots < N_DP * CAP, mine_first + (slots >> 11) * HALF + (slots & (HALF - 1)), slots)
+
+    used = lax.broadcasted_iota(jnp.int32, (FAN1, N_FEAT * ROWS), 0) < cnt1_ref[...]
+    place_ref[pl.ds(0, FAN1), :] = jnp.where(used, places(slots_ref[...]), ZERO_ROW)
+    place_ref[pl.ds(FAN1, 1), :] = places(self_slot_ref[...])
+    located = pltpu.make_async_copy(place_ref, slot_ref, index_sems.at[1])
+    located.start()
     swap_x.wait_recv()
     nodes_flat = nodes_ref.reshape(NODES, WIDE)
     table_flat = table_ref.reshape(ZERO_ROW + 8, WIDE)
     rows_flat = rows_ref.reshape(QUARTER, WIDE)
 
     def turn(block, carry):
-        at = pl.multiple_of(block * 128, 128)
-        nodes_flat[pl.ds(at, 128), :] = feats_ref[:, pl.ds(at, 128)].astype(F32).T
+        at = pl.multiple_of(block * 1024, 1024)
+        nodes_flat[pl.ds(at, 1024), :] = feats_ref[:, pl.ds(at, 1024)].astype(F32).T
         return carry
 
-    lax.fori_loop(0, NODES // 128, turn, 0)
+    lax.fori_loop(0, NODES // 1024, turn, 0)
+    wanted.wait()
 
     far = {}
     staged = {}
 
     def pick(shift, half):
         to = at_shift(*shift)
-        first = to * HALF + half * QUARTER
+        first = half * QUARTER
         unroll = 32
 
         def some_rows(block, carry):
             at = pl.multiple_of(block * unroll, unroll)
-            got = [nodes_ref[send_ref[first + at + r]] for r in range(unroll)]
+            got = [nodes_ref[send_ref[to, first + at + r]] for r in range(unroll)]
             for r in range(unroll):
                 rows_ref[at + r] = got[r]
             return carry
@@ -217,36 +237,36 @@
     for number, shift in enumerate(TWO):
         for half in range(2):
             pick(shift, half)
-        if number in (2, 4, 6):
-            notes.take(number // 2)
-    for shift in DIAGONAL:
+        if number in (1, 3, 5):
+            notes.take((number + 1) // 2)
+    for number, shift in enumerate(DIAGONAL):
         for half in range(2):
             pick(shift, half)
-    notes.take(4)
-    for s in range(len(STAGED)):
-        pass_on(s)
+        if number == 0:
+            notes.take(4)
+        for s in range(4 * number, min(4 * number + 4, len(STAGED))):
+            pass_on(s)
+    for shift in NEXT:
+        for half in range(2):
+            pick(shift, half)
     for copy in notes.crossed:
         copy.wait_recv()
 
-    row_id = lax.broadcasted_iota(jnp.int32, (ROWS, 128), 0).astype(F32).astype(BF16)
+    code_ref[...] = code(feat * ROWS + lax.broadcasted_iota(jnp.int32, (ROWS, 128), 0)).astype(BF16)
     one = jnp.ones((ROWS, 128), BF16)
     none = jnp.zeros((ROWS, 128), BF16)
     both_last = (((1,), (1,)), ((), ()))
-    mine = jnp.full((32, ROWS), feat, jnp.int32).astype(F32)
-    for ref in (gn_ref, gs_ref, gnt_ref, gst_ref):
+    for ref in (gnt_ref, gst_ref):
         ref[...] = jnp.zeros_like(ref)
 
     def one_device(f, carry):
-        high_here = note_ref[f, pl.ds(TALL, 32), :].astype(F32)
-        low_here = note_ref[f, pl.ds(TALL + 32, 32), :].astype(F32)
-        place = jnp.where(high_here == mine, low_here, -1.0)
-        counts = high_here[FAN2 + 1 : FAN2 + 2, :]
+        names_here = note_ref[f, pl.ds(TALL, 32), :].astype(F32)
         tallies, hots = [], []
         for side in range(ROWS // 128):
             total = none
-            for j in range(FAN2 + 1):
-                line = place[j : j + 1, side * 128 : side * 128 + 128].astype(BF16)
-                match = jnp.where(jnp.broadcast_to(line, (ROWS, 128)) == row_id, one, none)
+            for j in range(NAMES):
+                line = names_here[j : j + 1, side * 128 : side * 128 + 128].astype(BF16)
+                match = jnp.where(jnp.broadcast_to(line, (ROWS, 128)) == code_ref[...], one, none)
                 if j < FAN2:
                     total = total + match
                 else:
@@ -255,30 +275,54 @@
         tally = jnp.concatenate(tallies, axis=1)
         hot = jnp.concatenate(hots, axis=1)
         dl = note_ref[f, pl.ds(0, TALL), :]
-        dz = (dl.astype(F32) / counts).astype(BF16)
-        gn_ref[...] += lax.dot_general(tally, dz, both_last, preferred_element_type=F32)
-        gs_ref[...] += lax.dot_general(hot, dl, both_last, preferred_element_type=F32)
+        dz = (dl.astype(F32) / names_here[NAMES : NAMES + 1, :]).astype(BF16)
         gnt_ref[...] += lax.dot_general(dz, tally, both_last, preferred_element_type=F32)
         gst_ref[...] += lax.dot_general(dl, hot, both_last, preferred_element_type=F32)
         return carry
 
     lax.fori_loop(0, N_FEAT, one_device, 0)
-    h = h_ref[...].astype(F32)
-    hidden = jnp.dot(gn_ref[:, :CLASSES], wn_ref[...].astype(F32), precision=HIGHEST, preferred_element_type=F32)
-    hidden += jnp.dot(gs_ref[:, :CLASSES], ws_ref[...].astype(F32), precision=HIGHEST, preferred_element_type=F32)
-    dpre_ref[z] = jnp.where(h > 0, hidden, 0.0).T.astype(BF16)
-    second_ref[0] = jnp.dot(gst_ref[...], h, precision=HIGHEST, preferred_element_type=F32)
-    second_ref[1] = jnp.dot(gnt_ref[...], h, precision=HIGHEST, preferred_element_type=F32)
+
+    def twice(value, other, left):
+        top = value.astype(BF16)
+        rest = (value - top.astype(F32)).astype(BF16)
+        if left:
+            return jnp.dot(top, other, preferred_element_type=F32) + jnp.dot(rest, other, preferred_element_type=F32)
+        return jnp.dot(other, top, preferred_element_type=F32) + jnp.dot(other, rest, preferred_element_type=F32)
+
+    def upright(w_ref):
+        return jnp.concatenate([w_ref[...].astype(F32), jnp.zeros((256 - CLASSES, HIDDEN), F32)], axis=0).T.astype(BF16)
+
+    below = jnp.zeros((256 - TALL, ROWS), F32)
+    gnt = gnt_ref[...]
+    gst = gst_ref[...]
+    hidden = twice(jnp.concatenate([gnt, below], axis=0), upright(wn_ref), False)
+    hidden += twice(jnp.concatenate([gst, below], axis=0), upright(ws_ref), False)
+    dpre_ref[z] = jnp.where(h_ref[...].astype(F32).T > 0, hidden, 0.0).astype(BF16)
     rows_ring = Ring(lambda step: dpre_ref.at[lax.rem(z + step + N_Z, N_Z)], dpre_up, dpre_down)
     rows_ring.start()
+    second_ref[0] = twice(gst, h_ref[...], True)
+    second_ref[1] = twice(gnt, h_ref[...], True)
     second_over = push(second_ref.at[1 - core], extra_ref, over_sems, 0, partner)
 
-    for shift in NEXT:
-        for half in range(2):
-            pick(shift, half)
-    rows_ring.take(1)
     for half in range(2):
         pick((0, 0), half)
+    swap_hub.wait_recv()
+
+    def turn_hub(block, carry):
+        at = pl.multiple_of(block * 1024, 1024)
+        table_flat[pl.ds(2 * PART + at, 1024), :] = feats_ref[:, pl.ds(NODES + at, 1024)].astype(F32).T
+        return carry
+
+    lax.fori_loop(0, HUBS // 1024, turn_hub, 0)
+    table_flat[pl.ds(ZERO_ROW, 8), :] = jnp.zeros((8, WIDE), F32)
+
+    order = [(shift, half) for shift in [(0, 0)] + DIAGONAL + TWO + NEXT for half in range(2)]
+    for number, (shift, half) in enumerate(order):
+        arrive(shift, half)
+        if number == 9:
+            rows_ring.take(1)
+        if number == 23:
+            rows_ring.take(2)
     second_over.wait_recv()
     column_ref[...] = second_ref[core] + extra_ref[...]
 
@@ -289,32 +333,9 @@
 
     scattered = [push(column_ref.at[piece(k)], pieces_ref.at[k], z_sems, k, (dp, z_feat(k))) for k in range(1, N_Z)]
 
-    swap_hub.wait_recv()
-
-    def turn_hub(block, carry):
-        at = pl.multiple_of(block * 128, 128)
-        table_flat[pl.ds(2 * PART + at, 128), :] = feats_ref[:, pl.ds(NODES + at, 128)].astype(F32).T
-        return carry
-
-    lax.fori_loop(0, HUBS // 128, turn_hub, 0)
-    table_flat[pl.ds(ZERO_ROW, 8), :] = jnp.zeros((8, WIDE), F32)
-
-    order = [(shift, half) for shift in [(0, 0)] + DIAGONAL + TWO + NEXT for half in range(2)]
-    for number, (shift, half) in enumerate(order):
-        arrive(shift, half)
-        if number == 16:
-            rows_ring.take(2)
-    total = column_ref[piece(0)]
-    for k, copy in enumerate(scattered):
-        copy.wait_recv()
-        total = total + pieces_ref[k + 1]
-    piece_ref[...] = total
     for shift, half in order:
         cross(shift, half)
-    summed = [
-        push(piece_ref, columns_ref.at[k], dp_sems, k, (at_shift(k // SIDE, k % SIDE), feat)) for k in range(1, N_DP)
-    ]
-    rows_ring.take(3)
+    located.wait()
 
     self_flat = self_ref.reshape(ROWS, WIDE)
     sum_flat = sum_ref.reshape(ROWS, WIDE)
@@ -322,21 +343,22 @@
 
     def fold(step):
         of = lax.rem(z + step + N_Z, N_Z)
-        base = of * ROWS
+        base = (2 * of + core) * ROWS
 
         def some_sums(block, carry):
             at = pl.multiple_of(block * unroll, unroll)
             for r in range(unroll):
-                got = [table_ref[slot_ref[j * GROUP + base + at + r]] for j in range(PICKS)]
-                rest = got[1:]
+                got = [table_ref[slot_ref[j, base + at + r]] for j in range(PICKS)]
+                rest = got[:FAN1]
                 while len(rest) > 1:
                     rest = [rest[i] + rest[i + 1] if i + 1 < len(rest) else rest[i] for i in range(0, len(rest), 2)]
-                self_ref[at + r] = got[0]
+                self_ref[at + r] = got[FAN1]
                 sum_ref[at + r] = rest[0]
             return carry
 
         lax.fori_loop(0, ROWS // unroll, some_sums, 0)
-        count = jnp.broadcast_to(cnt1_ref[of].astype(F32), (WIDE, ROWS)).T
+        here = pl.ds(pl.multiple_of(base, ROWS), ROWS)
+        count = jnp.broadcast_to(cnt1_ref[:, here].astype(F32), (WIDE, ROWS)).T
         own = self_flat[...].astype(BF16)
         mean = (sum_flat[...] / count).astype(BF16)
         both = jnp.concatenate([own, mean], axis=1)
@@ -349,6 +371,17 @@
     gathered = []
     for number, step in enumerate((0, -1, 1, -2, 2, -3, 3, -4)):
         fold(step)
+        if number == 0:
+            rows_ring.take(3)
+            total = column_ref[piece(0)]
+            for k, copy in enumerate(scattered):
+                copy.wait_recv()
+                total = total + pieces_ref[k + 1]
+            piece_ref[...] = total
+            summed = [
+                push(piece_ref, columns_ref.at[k], dp_sems, k, (at_shift(k // SIDE, k % SIDE), feat))
+                for k in range(1, N_DP)
+            ]
         if number == 3:
             rows_ring.take(4)
             total = piece_ref[...]
@@ -409,8 +442,7 @@
         copy.wait_send()
 
 
-def main_step(send, slots, x, hub, cnt1, h, seed, nbr2, cnt2, dl, ws, wn):
-    smem = pl.BlockSpec(memory_space=pltpu.SMEM)
+def main_step(*operands):
     vmem = pl.BlockSpec(memory_space=pltpu.VMEM)
     dma = pltpu.SemaphoreType.DMA
     return pl.pallas_call(
@@ -421,7 +453,7 @@
             jax.ShapeDtypeStruct((CLASSES, HIDDEN), F32),
             jax.ShapeDtypeStruct((CLASSES, HIDDEN), F32),
         ),
-        in_specs=[smem, smem] + [vmem] * 10,
+        in_specs=[vmem] * len(operands),
         out_specs=(vmem,) * 4,
         scratch_shapes=[
             pltpu.VMEM((WIDE, NODES + HUBS), BF16),
@@ -432,9 +464,11 @@
             pltpu.VMEM((N_DP, 2, QUARTER, WIDE), BF16),
             pltpu.VMEM((ZERO_ROW + 8, 1, WIDE), F32),
             pltpu.VMEM((QUARTER, 1, WIDE), F32),
+            pltpu.SMEM((N_DP, HALF), jnp.int32),
+            pltpu.VMEM((PICKS, N_FEAT * ROWS), jnp.int32),
+            pltpu.SMEM((PICKS, N_FEAT * ROWS), jnp.int32),
+            pltpu.VMEM((ROWS, 128), BF16),
             pltpu.VMEM((N_FEAT, NOTE, ROWS), BF16),
-            pltpu.VMEM((ROWS, TALL), F32),
-            pltpu.VMEM((ROWS, TALL), F32),
             pltpu.VMEM((TALL, ROWS), F32),
             pltpu.VMEM((TALL, ROWS), F32),
             pltpu.VMEM((N_Z, HIDDEN, ROWS), BF16),
@@ -452,6 +486,7 @@
             pltpu.VMEM((2, 64, HIDDEN), F32),
             pltpu.VMEM((N_DP, 8, HIDDEN), F32),
             pltpu.VMEM((N_DP, 8, HIDDEN), F32),
+            dma((2,)),
             dma((2, 2)),
             dma((2, len(STAGED))),
             dma((2, 2 * N_DP)),
@@ -472,7 +507,29 @@
             collective_id=1, has_side_effects=True, vmem_limit_bytes=60 * 1024 * 1024
         ),
         name="main_step",
-    )(send, slots, x, hub, cnt1, h, seed, nbr2, cnt2, dl, ws, wn)
+    )(*operands)
+
+
+def hand_kernel(*refs):
+    sources, results, sems = refs[:4], refs[4:8], refs[8]
+    copies = [pltpu.make_async_copy(src, dst, sems.at[i]) for i, (src, dst) in enumerate(zip(sources, results))]
+    for copy in copies:
+        copy.start()
+    for copy in copies:
+        copy.wait()
+
+
+def hand_out(arrays):
+    anywhere = pl.BlockSpec(memory_space=pl.ANY)
+    return pl.pallas_call(
+        hand_kernel,
+        out_shape=tuple(jax.ShapeDtypeStruct(a.shape, a.dtype) for a in arrays),
+        in_specs=[anywhere] * 4,
+        out_specs=(anywhere,) * 4,
+        scratch_shapes=[pltpu.SemaphoreType.DMA((4,))],
+        compiler_params=pltpu.CompilerParams(vmem_limit_bytes=60 * 1024 * 1024),
+        name="hand_out",
+    )(*arrays)
 
 
 def body(
@@ -490,25 +547,13 @@
     w_self2,
     w_nbr2,
 ):
-    core = lax.rem(lax.axis_index("feat"), 2)
-    send = lax.dynamic_slice_in_dim(send_rows[0], core * HALF, HALF, axis=1).reshape(-1)
-
-    def half_rows(a):
-        a = a.reshape(a.shape[:-1] + (N_Z, 2, ROWS))
-        return lax.dynamic_index_in_dim(a, core, axis=a.ndim - 2, keepdims=False).reshape(a.shape[:-3] + (-1,))
-
-    count = half_rows(cnt1)
-    slots = jnp.concatenate([half_rows(self_slot)[None], half_rows(nbr1)], axis=0)
-    side = jnp.where(lax.rem(lax.div(slots, HALF), 2) == core, 0, PART)
-    place = jnp.where(slots < N_DP * CAP, side + lax.div(slots, CAP) * HALF + lax.rem(slots, HALF), slots)
-    read = lax.iota(jnp.int32, PICKS)[:, None] <= count[None, :]
-    place = jnp.where(read, place, ZERO_ROW).reshape(-1)
-    self1, nbr1_out, self2, nbr2_out = main_step(
-        send,
-        place,
+    sums = main_step(
+        send_rows,
+        self_slot[None],
+        nbr1,
         x_table,
         hub_feats,
-        count.reshape(N_Z, 1, ROWS),
+        cnt1[None],
         h_saved,
         seed_self[None],
         nbr2.T,
@@ -517,6 +562,7 @@
         w_self2.T,
         w_nbr2.T,
     )
+    self1, nbr1_out, self2, nbr2_out = hand_out(sums)
     return (self1, nbr1_out, self2.T, nbr2_out.T)
 
 

time: 139 us -> 173 us (1.24)
  Pallas kernels: 129 us -> 173 us
  local copies, waits for them, and re-layouts: 8.29 us -> 0 us
    pallas_call x0 -> x1, Pallas kernels: none -> 30.9 us  [hand_out(): pl.pallas_call(hand_kernel, out_shape=tuple((jax.ShapeDtypeStruct(a.shape...]
    pallas_call x1, Pallas kernels: 129 us -> 142 us  [main_step(): pl.pallas_call(main_kernel, out_shape=(jax.ShapeDtypeStruct((64, HIDDEN),...]
    unnamed x18 -> x0, local copies, waits for them, and re-layouts: 6.33 us -> none
where the time goes in v4:
time: 173 us
  Pallas kernels  173 us (100%)
    pallas_call x1, Pallas kernels, main_step(): pl.pallas_call(main_kernel, out_shape=(jax.ShapeDtypeStruct((64, HIDDEN),...  142 us
    pallas_call x1, Pallas kernels, hand_out(): pl.pallas_call(hand_kernel, out_shape=tuple((jax.ShapeDtypeStruct(a.shape...  30.9 us

profile of v4, /device:TPU:1, one launch (start us, length us, event | category | flops | bytes accessed | tf_op | source)
XLA Modules:
  0.0 173.2 jit_solution(16411409731258215758)
XLA Ops:
  0.6 141.6 %main_step.1 = (f32[64,512]{1,0:T(8,128)}, f32[64,512]{1,0:T(8,128)}, f32[172,512]{1,0:T(8,128)}, f32[172,512]{1,0:T(8,128)}) custom-call(s32[1,16,2048]{2,1,0:T(8,128)} %send_rows_ref.1, s32[1,4096]{1,0:T(1,128)} %bitcast.14, s32[10,4096]{1,0:T(8,128)} %slots_ref.1, bf16[64,8192]{1,0:T(8,128)(2,1)} %x_ref.1, bf16[64,2048]{1,0:T(8,128)(2,1)} %hub_ref.1, ...), custom_call_target="tpu_custom_call" | custom-call | tf_op jit(solution)/shard_map/main_step/pallas_call | solution.py:448
  142.3 30.9 %hand_out.1 = (f32[64,512]{1,0:T(8,128)}, f32[64,512]{1,0:T(8,128)}, f32[172,512]{1,0:T(8,128)}, f32[172,512]{1,0:T(8,128)}) custom-call(f32[64,512]{1,0:T(8,128)} %get-tuple-element.12.refs_0_, f32[64,512]{1,0:T(8,128)} %get-tuple-element.13.refs_1_, f32[172,512]{1,0:T(8,128)} %get-tuple-element.14.refs_2_, f32[172,512]{1,0:T(8,128)} %get-tuple-element.15.refs_3_), custom_call_target="tpu_custom_call" | custom-call | tf_op jit(solution)/shard_map/hand_out/pallas_call | solution.py:524

commit v5 on v4

--- a/solution.py
+++ b/solution.py
@@ -168,13 +168,10 @@
     located = pltpu.make_async_copy(place_ref, slot_ref, index_sems.at[1])
     located.start()
     swap_x.wait_recv()
-    nodes_flat = nodes_ref.reshape(NODES, WIDE)
-    table_flat = table_ref.reshape(ZERO_ROW + 8, WIDE)
-    rows_flat = rows_ref.reshape(QUARTER, WIDE)
 
     def turn(block, carry):
         at = pl.multiple_of(block * 1024, 1024)
-        nodes_flat[pl.ds(at, 1024), :] = feats_ref[:, pl.ds(at, 1024)].astype(F32).T
+        nodes_ref[pl.ds(at, 1024), :] = feats_ref[:, pl.ds(at, 1024)].astype(F32).T
         return carry
 
     lax.fori_loop(0, NODES // 1024, turn, 0)
@@ -190,17 +187,17 @@
 
         def some_rows(block, carry):
             at = pl.multiple_of(block * unroll, unroll)
-            got = [nodes_ref[send_ref[to, first + at + r]] for r in range(unroll)]
+            got = [nodes_ref[pl.ds(send_ref[to, first + at + r], 1), :] for r in range(unroll)]
             for r in range(unroll):
-                rows_ref[at + r] = got[r]
+                rows_ref[pl.ds(at + r, 1), :] = got[r]
             return carry
 
         lax.fori_loop(0, QUARTER // unroll, some_rows, 0)
         slot = 2 * (shift[0] * SIDE + shift[1]) + half
         if shift == (0, 0):
-            own_ref[dp, half] = rows_flat[...].astype(BF16)
+            own_ref[dp, half] = rows_ref[...].astype(BF16)
             return
-        stage_ref[slot] = rows_flat[...].astype(BF16)
+        stage_ref[slot] = rows_ref[...].astype(BF16)
         if (shift, half) in STAGED:
             s = STAGED.index((shift, half))
             staged[s] = push(stage_ref.at[slot], mid_ref.at[s], mid_sems, s, (at_shift(*through(shift, half)), feat))
@@ -225,14 +222,14 @@
             far[slot].wait_recv()
         near[slot] = push(own_ref.at[source, half], other_ref.at[source, half], near_sems, slot, partner)
         at = pl.multiple_of(source * HALF + half * QUARTER, QUARTER)
-        table_flat[pl.ds(at, QUARTER), :] = own_ref[source, half].astype(F32)
+        table_ref[pl.ds(at, QUARTER), :] = own_ref[source, half].astype(F32)
 
     def cross(shift, half):
         slot = 2 * (shift[0] * SIDE + shift[1]) + half
         source = at_shift(-shift[0], -shift[1])
         near[slot].wait_recv()
         at = pl.multiple_of(PART + source * HALF + half * QUARTER, QUARTER)
-        table_flat[pl.ds(at, QUARTER), :] = other_ref[source, half].astype(F32)
+        table_ref[pl.ds(at, QUARTER), :] = other_ref[source, half].astype(F32)
 
     for number, shift in enumerate(TWO):
         for half in range(2):
@@ -310,11 +307,11 @@
 
     def turn_hub(block, carry):
         at = pl.multiple_of(block * 1024, 1024)
-        table_flat[pl.ds(2 * PART + at, 1024), :] = feats_ref[:, pl.ds(NODES + at, 1024)].astype(F32).T
+        table_ref[pl.ds(2 * PART + at, 1024), :] = feats_ref[:, pl.ds(NODES + at, 1024)].astype(F32).T
         return carry
 
     lax.fori_loop(0, HUBS // 1024, turn_hub, 0)
-    table_flat[pl.ds(ZERO_ROW, 8), :] = jnp.zeros((8, WIDE), F32)
+    table_ref[pl.ds(ZERO_ROW, 8), :] = jnp.zeros((8, WIDE), F32)
 
     order = [(shift, half) for shift in [(0, 0)] + DIAGONAL + TWO + NEXT for half in range(2)]
     for number, (shift, half) in enumerate(order):
@@ -337,8 +334,6 @@
         cross(shift, half)
     located.wait()
 
-    self_flat = self_ref.reshape(ROWS, WIDE)
-    sum_flat = sum_ref.reshape(ROWS, WIDE)
     unroll = 8
 
     def fold(step):
@@ -348,19 +343,19 @@
         def some_sums(block, carry):
             at = pl.multiple_of(block * unroll, unroll)
             for r in range(unroll):
-                got = [table_ref[slot_ref[j, base + at + r]] for j in range(PICKS)]
+                got = [table_ref[pl.ds(slot_ref[j, base + at + r], 1), :] for j in range(PICKS)]
                 rest = got[:FAN1]
                 while len(rest) > 1:
                     rest = [rest[i] + rest[i + 1] if i + 1 < len(rest) else rest[i] for i in range(0, len(rest), 2)]
-                self_ref[at + r] = got[FAN1]
-                sum_ref[at + r] = rest[0]
+                self_ref[pl.ds(at + r, 1), :] = got[FAN1]
+                sum_ref[pl.ds(at + r, 1), :] = rest[0]
             return carry
 
         lax.fori_loop(0, ROWS // unroll, some_sums, 0)
         here = pl.ds(pl.multiple_of(base, ROWS), ROWS)
         count = jnp.broadcast_to(cnt1_ref[:, here].astype(F32), (WIDE, ROWS)).T
-        own = self_flat[...].astype(BF16)
-        mean = (sum_flat[...] / count).astype(BF16)
+        own = self_ref[...].astype(BF16)
+        mean = (sum_ref[...] / count).astype(BF16)
         both = jnp.concatenate([own, mean], axis=1)
         product = jnp.dot(dpre_ref[of], both, preferred_element_type=F32)
         if step == 0:
@@ -457,13 +452,13 @@
         out_specs=(vmem,) * 4,
         scratch_shapes=[
             pltpu.VMEM((WIDE, NODES + HUBS), BF16),
-            pltpu.VMEM((NODES, 1, WIDE), F32),
+            pltpu.VMEM((NODES, WIDE), F32),
             pltpu.VMEM((2 * N_DP, QUARTER, WIDE), BF16),
             pltpu.VMEM((len(STAGED), QUARTER, WIDE), BF16),
             pltpu.VMEM((N_DP, 2, QUARTER, WIDE), BF16),
             pltpu.VMEM((N_DP, 2, QUARTER, WIDE), BF16),
-            pltpu.VMEM((ZERO_ROW + 8, 1, WIDE), F32),
-            pltpu.VMEM((QUARTER, 1, WIDE), F32),
+            pltpu.VMEM((ZERO_ROW + 8, WIDE), F32),
+            pltpu.VMEM((QUARTER, WIDE), F32),
             pltpu.SMEM((N_DP, HALF), jnp.int32),
             pltpu.VMEM((PICKS, N_FEAT * ROWS), jnp.int32),
             pltpu.SMEM((PICKS, N_FEAT * ROWS), jnp.int32),
@@ -479,8 +474,8 @@
             pltpu.VMEM((TALL, HIDDEN), F32),
             pltpu.VMEM((N_DP, TALL // 2, 128), F32),
             pltpu.VMEM((2, TALL, HIDDEN), F32),
-            pltpu.VMEM((ROWS, 1, WIDE), F32),
-            pltpu.VMEM((ROWS, 1, WIDE), F32),
+            pltpu.VMEM((ROWS, WIDE), F32),
+            pltpu.VMEM((ROWS, WIDE), F32),
             pltpu.VMEM((HIDDEN, 2 * WIDE), F32),
             pltpu.VMEM((2 * WIDE, HIDDEN), F32),
             pltpu.VMEM((2, 64, HIDDEN), F32),
@@ -511,22 +506,17 @@
 
 
 def hand_kernel(*refs):
-    sources, results, sems = refs[:4], refs[4:8], refs[8]
-    copies = [pltpu.make_async_copy(src, dst, sems.at[i]) for i, (src, dst) in enumerate(zip(sources, results))]
-    for copy in copies:
-        copy.start()
-    for copy in copies:
-        copy.wait()
+    for source, result in zip(refs[:4], refs[4:]):
+        result[...] = source[...]
 
 
 def hand_out(arrays):
-    anywhere = pl.BlockSpec(memory_space=pl.ANY)
+    vmem = pl.BlockSpec(memory_space=pltpu.VMEM)
     return pl.pallas_call(
         hand_kernel,
         out_shape=tuple(jax.ShapeDtypeStruct(a.shape, a.dtype) for a in arrays),
-        in_specs=[anywhere] * 4,
-        out_specs=(anywhere,) * 4,
-        scratch_shapes=[pltpu.SemaphoreType.DMA((4,))],
+        in_specs=[vmem] * 4,
+        out_specs=(vmem,) * 4,
         compiler_params=pltpu.CompilerParams(vmem_limit_bytes=60 * 1024 * 1024),
         name="hand_out",
     )(*arrays)

time: 173 us -> 145 us (0.84)
  Pallas kernels: 173 us -> 144 us
    pallas_call x1, Pallas kernels: 30.9 us -> 2.18 us  [hand_out(): pl.pallas_call(hand_kernel, out_shape=tuple((jax.ShapeDtypeStruct(a.shape...]
where the time goes in v5:
time: 145 us; the launch traced here: 144 us
  Pallas kernels  144 us (99%)
    pallas_call x1, Pallas kernels, main_step(): pl.pallas_call(main_kernel, out_shape=(jax.ShapeDtypeStruct((64, HIDDEN),...  142 us

profile of v5, /device:TPU:1, one launch (start us, length us, event | category | flops | bytes accessed | tf_op | source)
XLA Modules:
  0.0 144.5 jit_solution(10937962395415340713)
XLA Ops:
  0.6 141.6 %main_step.1 = (f32[64,512]{1,0:T(8,128)}, f32[64,512]{1,0:T(8,128)}, f32[172,512]{1,0:T(8,128)}, f32[172,512]{1,0:T(8,128)}) custom-call(s32[1,16,2048]{2,1,0:T(8,128)} %send_rows_ref.1, s32[1,4096]{1,0:T(1,128)} %bitcast.14, s32[10,4096]{1,0:T(8,128)} %slots_ref.1, bf16[64,8192]{1,0:T(8,128)(2,1)} %x_ref.1, bf16[64,2048]{1,0:T(8,128)(2,1)} %hub_ref.1, ...), custom_call_target="tpu_custom_call" | custom-call | tf_op jit(solution)/shard_map/main_step/pallas_call | solution.py:443
  142.3 2.2 %hand_out.1 = (f32[64,512]{1,0:T(8,128)}, f32[64,512]{1,0:T(8,128)}, f32[172,512]{1,0:T(8,128)}, f32[172,512]{1,0:T(8,128)}) custom-call(f32[64,512]{1,0:T(8,128)} %get-tuple-element.12.refs_0_, f32[64,512]{1,0:T(8,128)} %get-tuple-element.13.refs_1_, f32[172,512]{1,0:T(8,128)} %get-tuple-element.14.refs_2_, f32[172,512]{1,0:T(8,128)} %get-tuple-element.15.refs_3_), custom_call_target="tpu_custom_call" | custom-call | tf_op jit(solution)/shard_map/hand_out/pallas_call | solution.py:515

commit v6 on v5

--- a/solution.py
+++ b/solution.py
@@ -37,25 +37,14 @@
 NEXT = [(1, 0), (3, 0), (0, 1), (0, 3)]
 
 
-def through(shift, half):
-    one = 3 if half else 1
-    dx, dy = shift
-    if dx == 2:
-        return (one, one if dy == 2 else 0)
-    return (dx, one)
-
-
-STAGED = [(shift, half) for shift in TWO for half in range(2)]
-
-
 def main_kernel(
     send_rows_ref, self_slot_ref, slots_ref, x_ref, hub_ref, cnt1_ref, h_ref, seed_ref, nbr2_ref, cnt2_ref, dl_ref, ws_ref, wn_ref,
     self1_ref, nbr1_ref, self2_ref, nbr2o_ref,
-    feats_ref, nodes_ref, stage_ref, mid_ref, own_ref, other_ref, table_ref, rows_ref,
+    feats_ref, nodes_ref, stage_ref, own_ref, other_ref, table_ref, rows_ref,
     send_ref, place_ref, slot_ref, code_ref, note_ref, gnt_ref, gst_ref, dpre_ref, second_ref, extra_ref, piece_ref, pieces_ref, column_ref, columns_ref, final_ref,
     self_ref, sum_ref, acc_ref, part_ref, theirs_ref, got_ref, done_ref,
-    index_sems, swap_sems, mid_sems, far_sems, near_sems, note_up, note_down, note_over,
-    dpre_up, dpre_down, over_sems, z_sems, dp_sems, z2_sems, first_sems, first2_sems,
+    index_sems, swap_sems, far_sems, near_sems, note_sems, note_over,
+    dpre_sems, over_sems, z_sems, dp_sems, z2_sems, first_sems, first2_sems,
 ):
     dp = lax.axis_index("dp")
     feat = lax.axis_index("feat")
@@ -118,42 +107,9 @@
         [names, jnp.zeros((32 - NAMES - 1, ROWS), F32)], axis=0
     ).astype(BF16)
 
-    class Ring:
-        def __init__(self, view, up, down, over=None):
-            self.view, self.up, self.down, self.over = view, up, down, over
-            self.from_below, self.from_above, self.crossed = {}, {}, []
-
-        def send_up(self, step):
-            block = self.view(1 - step)
-            self.from_below[step] = push(block, block, self.up, step - 1, (dp, z_feat(1)))
-
-        def send_down(self, step):
-            block = self.view(step - 1)
-            self.from_above[step] = push(block, block, self.down, step - 1, (dp, z_feat(-1)))
-
-        def cross(self, step):
-            if self.over is not None:
-                block = self.view(step)
-                self.crossed.append(push(block, block, self.over, len(self.crossed), partner))
-
-        def start(self):
-            self.send_up(1)
-            self.send_down(1)
-            self.cross(0)
-
-        def take(self, step):
-            self.from_below[step].wait_recv()
-            if step < 4:
-                self.send_up(step + 1)
-            self.cross(-step)
-            if step < 4:
-                self.from_above[step].wait_recv()
-                if step < 3:
-                    self.send_down(step + 1)
-                self.cross(step)
-
-    notes = Ring(lambda step: note_ref.at[z_feat(step)], note_up, note_down, note_over)
-    notes.start()
+    around = (1, 7, 2, 6, 3, 5, 4)
+    noted = {k: push(note_ref.at[feat], note_ref.at[feat], note_sems, k, (dp, z_feat(k))) for k in around}
+    crossed = [push(note_ref.at[feat], note_ref.at[feat], note_over, 0, partner)]
 
     feats_ref[lane, pl.ds(0, NODES)] = x_ref[...]
     feats_ref[lane, pl.ds(NODES, HUBS)] = hub_ref[...]
@@ -178,7 +134,6 @@
     wanted.wait()
 
     far = {}
-    staged = {}
 
     def pick(shift, half):
         to = at_shift(*shift)
@@ -193,25 +148,14 @@
             return carry
 
         lax.fori_loop(0, QUARTER // unroll, some_rows, 0)
-        slot = 2 * (shift[0] * SIDE + shift[1]) + half
         if shift == (0, 0):
             own_ref[dp, half] = rows_ref[...].astype(BF16)
-            return
-        stage_ref[slot] = rows_ref[...].astype(BF16)
-        if (shift, half) in STAGED:
-            s = STAGED.index((shift, half))
-            staged[s] = push(stage_ref.at[slot], mid_ref.at[s], mid_sems, s, (at_shift(*through(shift, half)), feat))
         else:
-            far[slot] = push(stage_ref.at[slot], own_ref.at[dp, half], far_sems, slot, (to, feat))
-
-    def pass_on(s):
-        shift, half = STAGED[s]
-        mx, my = through(shift, half)
+            stage_ref[2 * (shift[0] * SIDE + shift[1]) + half] = rows_ref[...].astype(BF16)
+
+    def send(shift, half):
         slot = 2 * (shift[0] * SIDE + shift[1]) + half
-        staged[s].wait_recv()
-        source = at_shift(-mx, -my)
-        to = at_shift(shift[0] - mx, shift[1] - my)
-        far[slot] = push(mid_ref.at[s], own_ref.at[source, half], far_sems, slot, (to, feat))
+        far[slot] = push(stage_ref.at[slot], own_ref.at[dp, half], far_sems, slot, (at_shift(*shift), feat))
 
     near = {}
 
@@ -231,22 +175,21 @@
         at = pl.multiple_of(PART + source * HALF + half * QUARTER, QUARTER)
         table_ref[pl.ds(at, QUARTER), :] = other_ref[source, half].astype(F32)
 
-    for number, shift in enumerate(TWO):
-        for half in range(2):
-            pick(shift, half)
-        if number in (1, 3, 5):
-            notes.take((number + 1) // 2)
-    for number, shift in enumerate(DIAGONAL):
-        for half in range(2):
-            pick(shift, half)
-        if number == 0:
-            notes.take(4)
-        for s in range(4 * number, min(4 * number + 4, len(STAGED))):
-            pass_on(s)
-    for shift in NEXT:
-        for half in range(2):
-            pick(shift, half)
-    for copy in notes.crossed:
+    away = [(shift, half) for shift in TWO + DIAGONAL + NEXT for half in range(2)]
+    for number, block in enumerate(away):
+        pick(*block)
+        if number < 4:
+            send(*block)
+        if number == 11:
+            for k in around:
+                noted[k].wait_recv()
+                landed = note_ref.at[z_feat(-k)]
+                crossed.append(push(landed, landed, note_over, k, partner))
+            for earlier in away[4:12]:
+                send(*earlier)
+        if number > 11:
+            send(*block)
+    for copy in crossed:
         copy.wait_recv()
 
     code_ref[...] = code(feat * ROWS + lax.broadcasted_iota(jnp.int32, (ROWS, 128), 0)).astype(BF16)
@@ -295,8 +238,6 @@
     hidden = twice(jnp.concatenate([gnt, below], axis=0), upright(wn_ref), False)
     hidden += twice(jnp.concatenate([gst, below], axis=0), upright(ws_ref), False)
     dpre_ref[z] = jnp.where(h_ref[...].astype(F32).T > 0, hidden, 0.0).astype(BF16)
-    rows_ring = Ring(lambda step: dpre_ref.at[lax.rem(z + step + N_Z, N_Z)], dpre_up, dpre_down)
-    rows_ring.start()
     second_ref[0] = twice(gst, h_ref[...], True)
     second_ref[1] = twice(gnt, h_ref[...], True)
     second_over = push(second_ref.at[1 - core], extra_ref, over_sems, 0, partner)
@@ -313,13 +254,6 @@
     lax.fori_loop(0, HUBS // 1024, turn_hub, 0)
     table_ref[pl.ds(ZERO_ROW, 8), :] = jnp.zeros((8, WIDE), F32)
 
-    order = [(shift, half) for shift in [(0, 0)] + DIAGONAL + TWO + NEXT for half in range(2)]
-    for number, (shift, half) in enumerate(order):
-        arrive(shift, half)
-        if number == 9:
-            rows_ring.take(1)
-        if number == 23:
-            rows_ring.take(2)
     second_over.wait_recv()
     column_ref[...] = second_ref[core] + extra_ref[...]
 
@@ -328,10 +262,23 @@
         tall = pl.ds(pl.multiple_of(lax.div(to, 4) * (TALL // 2), 8), TALL // 2)
         return tall, pl.ds(pl.multiple_of(lax.rem(to, 4) * 128, 128), 128)
 
-    scattered = [push(column_ref.at[piece(k)], pieces_ref.at[k], z_sems, k, (dp, z_feat(k))) for k in range(1, N_Z)]
-
-    for shift, half in order:
-        cross(shift, half)
+    scattered = {k: push(column_ref.at[piece(k)], pieces_ref.at[k], z_sems, k, (dp, z_feat(k))) for k in around}
+
+    order = [((0, 0), half) for half in range(2)] + away
+    shared = {}
+    for number, block in enumerate(order):
+        arrive(*block)
+        if number % 4 == 3 and len(shared) < len(around):
+            k = around[len(shared)]
+            shared[k] = push(dpre_ref.at[z], dpre_ref.at[z], dpre_sems, k, (dp, z_feat(k)))
+    total = column_ref[piece(0)]
+    for k in around:
+        scattered[k].wait_recv()
+        total = total + pieces_ref[k]
+    piece_ref[0] = total
+    along_x = [push(piece_ref.at[0], columns_ref.at[k], dp_sems, k, (at_shift(k, 0), feat)) for k in range(1, SIDE)]
+    for block in order:
+        cross(*block)
     located.wait()
 
     unroll = 8
@@ -364,30 +311,30 @@
             acc_ref[...] += product
 
     gathered = []
-    for number, step in enumerate((0, -1, 1, -2, 2, -3, 3, -4)):
-        fold(step)
-        if number == 0:
-            rows_ring.take(3)
-            total = column_ref[piece(0)]
-            for k, copy in enumerate(scattered):
+    for number, k in enumerate((0,) + around):
+        if number:
+            shared[k].wait_recv()
+        fold(-k)
+        if number == 1:
+            total = piece_ref[0]
+            for i, copy in enumerate(along_x):
                 copy.wait_recv()
-                total = total + pieces_ref[k + 1]
-            piece_ref[...] = total
-            summed = [
-                push(piece_ref, columns_ref.at[k], dp_sems, k, (at_shift(k // SIDE, k % SIDE), feat))
-                for k in range(1, N_DP)
+                total = total + columns_ref[i + 1]
+            piece_ref[1] = total
+            along_y = [
+                push(piece_ref.at[1], columns_ref.at[SIDE + i], dp_sems, SIDE + i, (at_shift(0, i), feat))
+                for i in range(1, SIDE)
             ]
         if number == 3:
-            rows_ring.take(4)
-            total = piece_ref[...]
-            for k, copy in enumerate(summed):
+            total = piece_ref[1]
+            for i, copy in enumerate(along_y):
                 copy.wait_recv()
-                total = total + columns_ref[k + 1]
+                total = total + columns_ref[SIDE + i + 1]
             mine_tall, mine_lanes = piece(0)
             block = final_ref.at[core, mine_tall, mine_lanes]
             final_ref[core, mine_tall, mine_lanes] = total
-            for k in range(1, N_Z):
-                gathered.append(push(block, block, z2_sems, k, (dp, z_feat(k))))
+            for i in around:
+                gathered.append(push(block, block, z2_sems, i, (dp, z_feat(i))))
         if number == 6:
             for copy in gathered:
                 copy.wait_recv()
@@ -423,16 +370,18 @@
     for k, copy in enumerate(spread):
         copy.wait_recv()
         total = total + got_ref[k + 1]
-    done_ref[dp] = total
+    done_ref[dp] = jnp.concatenate([total[:, : HIDDEN // 2], total[:, HIDDEN // 2 :]], axis=0).astype(BF16)
     last = []
     for k in range(1, N_DP):
         to = at_shift(k // SIDE, k % SIDE)
         last.append(push(done_ref.at[dp], done_ref.at[dp], first2_sems, k, (to, feat)))
     for copy in last:
         copy.wait_recv()
-    for k in range(8):
-        self1_ref[pl.ds(8 * k, 8), :] = done_ref[k]
-        nbr1_ref[pl.ds(8 * k, 8), :] = done_ref[8 + k]
+    for k in range(N_DP):
+        result = (self1_ref, nbr1_ref)[k // 8]
+        eight_rows = done_ref[k].astype(F32)
+        result[pl.ds(8 * (k % 8), 8), pl.ds(0, HIDDEN // 2)] = eight_rows[:8]
+        result[pl.ds(8 * (k % 8), 8), pl.ds(HIDDEN // 2, HIDDEN // 2)] = eight_rows[8:]
     for copy in pending:
         copy.wait_send()
 
@@ -454,7 +403,6 @@
             pltpu.VMEM((WIDE, NODES + HUBS), BF16),
             pltpu.VMEM((NODES, WIDE), F32),
             pltpu.VMEM((2 * N_DP, QUARTER, WIDE), BF16),
-            pltpu.VMEM((len(STAGED), QUARTER, WIDE), BF16),
             pltpu.VMEM((N_DP, 2, QUARTER, WIDE), BF16),
             pltpu.VMEM((N_DP, 2, QUARTER, WIDE), BF16),
             pltpu.VMEM((ZERO_ROW + 8, WIDE), F32),
@@ -469,10 +417,10 @@
             pltpu.VMEM((N_Z, HIDDEN, ROWS), BF16),
             pltpu.VMEM((2, TALL, HIDDEN), F32),
             pltpu.VMEM((TALL, HIDDEN), F32),
-            pltpu.VMEM((TALL // 2, 128), F32),
+            pltpu.VMEM((2, TALL // 2, 128), F32),
             pltpu.VMEM((N_Z, TALL // 2, 128), F32),
             pltpu.VMEM((TALL, HIDDEN), F32),
-            pltpu.VMEM((N_DP, TALL // 2, 128), F32),
+            pltpu.VMEM((2 * SIDE, TALL // 2, 128), F32),
             pltpu.VMEM((2, TALL, HIDDEN), F32),
             pltpu.VMEM((ROWS, WIDE), F32),
             pltpu.VMEM((ROWS, WIDE), F32),
@@ -480,17 +428,14 @@
             pltpu.VMEM((2 * WIDE, HIDDEN), F32),
             pltpu.VMEM((2, 64, HIDDEN), F32),
             pltpu.VMEM((N_DP, 8, HIDDEN), F32),
-            pltpu.VMEM((N_DP, 8, HIDDEN), F32),
+            pltpu.VMEM((N_DP, 16, HIDDEN // 2), BF16),
             dma((2,)),
             dma((2, 2)),
-            dma((2, len(STAGED))),
             dma((2, 2 * N_DP)),
             dma((2, 2 * N_DP)),
-            dma((2, 4)),
-            dma((2, 4)),
             dma((2, N_Z)),
-            dma((2, 4)),
-            dma((2, 4)),
+            dma((2, N_Z)),
+            dma((2, N_Z)),
             dma((2, 4)),
             dma((2, N_Z)),
             dma((2, N_DP)),

time: 145 us -> 159 us (1.097)
  Pallas kernels: 144 us -> 158 us
    pallas_call x1, Pallas kernels: 142 us -> 156 us  [main_step(): pl.pallas_call(main_kernel, out_shape=(jax.ShapeDtypeStruct((64, HIDDEN),...]
where the time goes in v6:
time: 159 us
  Pallas kernels  158 us (99%)
    pallas_call x1, Pallas kernels, main_step(): pl.pallas_call(main_kernel, out_shape=(jax.ShapeDtypeStruct((64, HIDDEN),...  156 us

profile of v6, /device:TPU:1, one launch (start us, length us, event | category | flops | bytes accessed | tf_op | source)
XLA Modules:
  0.0 158.9 jit_solution(624484196873282932)
XLA Ops:
  0.6 156.0 %main_step.1 = (f32[64,512]{1,0:T(8,128)}, f32[64,512]{1,0:T(8,128)}, f32[172,512]{1,0:T(8,128)}, f32[172,512]{1,0:T(8,128)}) custom-call(s32[1,16,2048]{2,1,0:T(8,128)} %send_rows_ref.1, s32[1,4096]{1,0:T(1,128)} %bitcast.14, s32[10,4096]{1,0:T(8,128)} %slots_ref.1, bf16[64,8192]{1,0:T(8,128)(2,1)} %x_ref.1, bf16[64,2048]{1,0:T(8,128)(2,1)} %hub_ref.1, ...), custom_call_target="tpu_custom_call" | custom-call | tf_op jit(solution)/shard_map/main_step/pallas_call | solution.py:392
  156.7 2.2 %hand_out.1 = (f32[64,512]{1,0:T(8,128)}, f32[64,512]{1,0:T(8,128)}, f32[172,512]{1,0:T(8,128)}, f32[172,512]{1,0:T(8,128)}) custom-call(f32[64,512]{1,0:T(8,128)} %get-tuple-element.12.refs_0_, f32[64,512]{1,0:T(8,128)} %get-tuple-element.13.refs_1_, f32[172,512]{1,0:T(8,128)} %get-tuple-element.14.refs_2_, f32[172,512]{1,0:T(8,128)} %get-tuple-element.15.refs_3_), custom_call_target="tpu_custom_call" | custom-call | tf_op jit(solution)/shard_map/hand_out/pallas_call | solution.py:460

commit v7 on v5

--- a/solution.py
+++ b/solution.py
@@ -118,6 +118,8 @@
         [names, jnp.zeros((32 - NAMES - 1, ROWS), F32)], axis=0
     ).astype(BF16)
 
+    around = (1, 7, 2, 6, 3, 5, 4)
+
     class Ring:
         def __init__(self, view, up, down, over=None):
             self.view, self.up, self.down, self.over = view, up, down, over
@@ -193,16 +195,18 @@
             return carry
 
         lax.fori_loop(0, QUARTER // unroll, some_rows, 0)
-        slot = 2 * (shift[0] * SIDE + shift[1]) + half
         if shift == (0, 0):
             own_ref[dp, half] = rows_ref[...].astype(BF16)
-            return
-        stage_ref[slot] = rows_ref[...].astype(BF16)
+        else:
+            stage_ref[2 * (shift[0] * SIDE + shift[1]) + half] = rows_ref[...].astype(BF16)
+
+    def send(shift, half):
+        slot = 2 * (shift[0] * SIDE + shift[1]) + half
         if (shift, half) in STAGED:
             s = STAGED.index((shift, half))
             staged[s] = push(stage_ref.at[slot], mid_ref.at[s], mid_sems, s, (at_shift(*through(shift, half)), feat))
         else:
-            far[slot] = push(stage_ref.at[slot], own_ref.at[dp, half], far_sems, slot, (to, feat))
+            far[slot] = push(stage_ref.at[slot], own_ref.at[dp, half], far_sems, slot, (at_shift(*shift), feat))
 
     def pass_on(s):
         shift, half = STAGED[s]
@@ -231,21 +235,16 @@
         at = pl.multiple_of(PART + source * HALF + half * QUARTER, QUARTER)
         table_ref[pl.ds(at, QUARTER), :] = other_ref[source, half].astype(F32)
 
-    for number, shift in enumerate(TWO):
-        for half in range(2):
-            pick(shift, half)
-        if number in (1, 3, 5):
-            notes.take((number + 1) // 2)
-    for number, shift in enumerate(DIAGONAL):
-        for half in range(2):
-            pick(shift, half)
-        if number == 0:
-            notes.take(4)
-        for s in range(4 * number, min(4 * number + 4, len(STAGED))):
-            pass_on(s)
-    for shift in NEXT:
-        for half in range(2):
-            pick(shift, half)
+    diagonal = [(shift, half) for shift in DIAGONAL for half in range(2)]
+    nearest = [(shift, half) for half in range(2) for shift in NEXT]
+    away = STAGED + diagonal + nearest
+    notes.take(1)
+    for number, block in enumerate(STAGED + diagonal):
+        pick(*block)
+        if number < len(STAGED):
+            send(*block)
+        if number in (5, 11, 17):
+            notes.take(number // 6 + 2)
     for copy in notes.crossed:
         copy.wait_recv()
 
@@ -277,7 +276,10 @@
         gst_ref[...] += lax.dot_general(dl, hot, both_last, preferred_element_type=F32)
         return carry
 
-    lax.fori_loop(0, N_FEAT, one_device, 0)
+    for part in range(8):
+        lax.fori_loop(2 * part, 2 * part + 2, one_device, 0)
+        for s in range(2 * part, min(2 * part + 2, len(STAGED))):
+            pass_on(s)
 
     def twice(value, other, left):
         top = value.astype(BF16)
@@ -297,12 +299,17 @@
     dpre_ref[z] = jnp.where(h_ref[...].astype(F32).T > 0, hidden, 0.0).astype(BF16)
     rows_ring = Ring(lambda step: dpre_ref.at[lax.rem(z + step + N_Z, N_Z)], dpre_up, dpre_down)
     rows_ring.start()
+    for number, block in enumerate(nearest):
+        send(*diagonal[number])
+        pick(*block)
+        send(*block)
     second_ref[0] = twice(gst, h_ref[...], True)
     second_ref[1] = twice(gnt, h_ref[...], True)
     second_over = push(second_ref.at[1 - core], extra_ref, over_sems, 0, partner)
 
     for half in range(2):
         pick((0, 0), half)
+    rows_ring.take(1)
     swap_hub.wait_recv()
 
     def turn_hub(block, carry):
@@ -313,13 +320,12 @@
     lax.fori_loop(0, HUBS // 1024, turn_hub, 0)
     table_ref[pl.ds(ZERO_ROW, 8), :] = jnp.zeros((8, WIDE), F32)
 
-    order = [(shift, half) for shift in [(0, 0)] + DIAGONAL + TWO + NEXT for half in range(2)]
-    for number, (shift, half) in enumerate(order):
-        arrive(shift, half)
-        if number == 9:
-            rows_ring.take(1)
-        if number == 23:
+    order = [((0, 0), half) for half in range(2)] + away
+    for number, block in enumerate(order):
+        arrive(*block)
+        if number == 15:
             rows_ring.take(2)
+    rows_ring.take(3)
     second_over.wait_recv()
     column_ref[...] = second_ref[core] + extra_ref[...]
 
@@ -328,10 +334,9 @@
         tall = pl.ds(pl.multiple_of(lax.div(to, 4) * (TALL // 2), 8), TALL // 2)
         return tall, pl.ds(pl.multiple_of(lax.rem(to, 4) * 128, 128), 128)
 
-    scattered = [push(column_ref.at[piece(k)], pieces_ref.at[k], z_sems, k, (dp, z_feat(k))) for k in range(1, N_Z)]
-
-    for shift, half in order:
-        cross(shift, half)
+    scattered = {k: push(column_ref.at[piece(k)], pieces_ref.at[k], z_sems, k, (dp, z_feat(k))) for k in around}
+    for block in order:
+        cross(*block)
     located.wait()
 
     unroll = 8
@@ -366,28 +371,34 @@
     gathered = []
     for number, step in enumerate((0, -1, 1, -2, 2, -3, 3, -4)):
         fold(step)
-        if number == 0:
-            rows_ring.take(3)
+        if number == 1:
+            rows_ring.take(4)
             total = column_ref[piece(0)]
-            for k, copy in enumerate(scattered):
+            for k in around:
+                scattered[k].wait_recv()
+                total = total + pieces_ref[k]
+            piece_ref[0] = total
+            along_x = [push(piece_ref.at[0], columns_ref.at[k], dp_sems, k, (at_shift(k, 0), feat)) for k in range(1, SIDE)]
+        if number == 2:
+            total = piece_ref[0]
+            for i, copy in enumerate(along_x):
                 copy.wait_recv()
-                total = total + pieces_ref[k + 1]
-            piece_ref[...] = total
-            summed = [
-                push(piece_ref, columns_ref.at[k], dp_sems, k, (at_shift(k // SIDE, k % SIDE), feat))
-                for k in range(1, N_DP)
+                total = total + columns_ref[i + 1]
+            piece_ref[1] = total
+            along_y = [
+                push(piece_ref.at[1], columns_ref.at[SIDE + i], dp_sems, SIDE + i, (at_shift(0, i), feat))
+                for i in range(1, SIDE)
             ]
         if number == 3:
-            rows_ring.take(4)
-            total = piece_ref[...]
-            for k, copy in enumerate(summed):
+            total = piece_ref[1]
+            for i, copy in enumerate(along_y):
                 copy.wait_recv()
-                total = total + columns_ref[k + 1]
+                total = total + columns_ref[SIDE + i + 1]
             mine_tall, mine_lanes = piece(0)
             block = final_ref.at[core, mine_tall, mine_lanes]
             final_ref[core, mine_tall, mine_lanes] = total
-            for k in range(1, N_Z):
-                gathered.append(push(block, block, z2_sems, k, (dp, z_feat(k))))
+            for i in around:
+                gathered.append(push(block, block, z2_sems, i, (dp, z_feat(i))))
         if number == 6:
             for copy in gathered:
                 copy.wait_recv()
@@ -423,16 +434,18 @@
     for k, copy in enumerate(spread):
         copy.wait_recv()
         total = total + got_ref[k + 1]
-    done_ref[dp] = total
+    done_ref[dp] = jnp.concatenate([total[:, : HIDDEN // 2], total[:, HIDDEN // 2 :]], axis=0).astype(BF16)
     last = []
     for k in range(1, N_DP):
         to = at_shift(k // SIDE, k % SIDE)
         last.append(push(done_ref.at[dp], done_ref.at[dp], first2_sems, k, (to, feat)))
     for copy in last:
         copy.wait_recv()
-    for k in range(8):
-        self1_ref[pl.ds(8 * k, 8), :] = done_ref[k]
-        nbr1_ref[pl.ds(8 * k, 8), :] = done_ref[8 + k]
+    for k in range(N_DP):
+        result = (self1_ref, nbr1_ref)[k // 8]
+        eight_rows = done_ref[k].astype(F32)
+        result[pl.ds(8 * (k % 8), 8), pl.ds(0, HIDDEN // 2)] = eight_rows[:8]
+        result[pl.ds(8 * (k % 8), 8), pl.ds(HIDDEN // 2, HIDDEN // 2)] = eight_rows[8:]
     for copy in pending:
         copy.wait_send()
 
@@ -469,10 +482,10 @@
             pltpu.VMEM((N_Z, HIDDEN, ROWS), BF16),
             pltpu.VMEM((2, TALL, HIDDEN), F32),
             pltpu.VMEM((TALL, HIDDEN), F32),
-            pltpu.VMEM((TALL // 2, 128), F32),
+            pltpu.VMEM((2, TALL // 2, 128), F32),
             pltpu.VMEM((N_Z, TALL // 2, 128), F32),
             pltpu.VMEM((TALL, HIDDEN), F32),
-            pltpu.VMEM((N_DP, TALL // 2, 128), F32),
+            pltpu.VMEM((2 * SIDE, TALL // 2, 128), F32),
             pltpu.VMEM((2, TALL, HIDDEN), F32),
             pltpu.VMEM((ROWS, WIDE), F32),
             pltpu.VMEM((ROWS, WIDE), F32),
@@ -480,7 +493,7 @@
             pltpu.VMEM((2 * WIDE, HIDDEN), F32),
             pltpu.VMEM((2, 64, HIDDEN), F32),
             pltpu.VMEM((N_DP, 8, HIDDEN), F32),
-            pltpu.VMEM((N_DP, 8, HIDDEN), F32),
+            pltpu.VMEM((N_DP, 16, HIDDEN // 2), BF16),
             dma((2,)),
             dma((2, 2)),
             dma((2, len(STAGED))),

time: 145 us -> 144 us (level)
  no operation moved by 1% of the time
where the time goes in v7:
time: 144 us
  Pallas kernels  143 us (99%)
    pallas_call x1, Pallas kernels, main_step(): pl.pallas_call(main_kernel, out_shape=(jax.ShapeDtypeStruct((64, HIDDEN),...  141 us

profile of v7, /device:TPU:1, one launch (start us, length us, event | category | flops | bytes accessed | tf_op | source)
XLA Modules:
  0.0 144.1 jit_solution(8284794997838398963)
XLA Ops:
  0.6 141.3 %main_step.1 = (f32[64,512]{1,0:T(8,128)}, f32[64,512]{1,0:T(8,128)}, f32[172,512]{1,0:T(8,128)}, f32[172,512]{1,0:T(8,128)}) custom-call(s32[1,16,2048]{2,1,0:T(8,128)} %send_rows_ref.1, s32[1,4096]{1,0:T(1,128)} %bitcast.14, s32[10,4096]{1,0:T(8,128)} %slots_ref.1, bf16[64,8192]{1,0:T(8,128)(2,1)} %x_ref.1, bf16[64,2048]{1,0:T(8,128)(2,1)} %hub_ref.1, ...), custom_call_target="tpu_custom_call" | custom-call | tf_op jit(solution)/shard_map/main_step/pallas_call | solution.py:456
  141.9 2.2 %hand_out.1 = (f32[64,512]{1,0:T(8,128)}, f32[64,512]{1,0:T(8,128)}, f32[172,512]{1,0:T(8,128)}, f32[172,512]{1,0:T(8,128)}) custom-call(f32[64,512]{1,0:T(8,128)} %get-tuple-element.12.refs_0_, f32[64,512]{1,0:T(8,128)} %get-tuple-element.13.refs_1_, f32[172,512]{1,0:T(8,128)} %get-tuple-element.14.refs_2_, f32[172,512]{1,0:T(8,128)} %get-tuple-element.15.refs_3_), custom_call_target="tpu_custom_call" | custom-call | tf_op jit(solution)/shard_map/hand_out/pallas_call | solution.py:528

commit v8 on v7

--- a/solution.py
+++ b/solution.py
@@ -52,7 +52,7 @@
     send_rows_ref, self_slot_ref, slots_ref, x_ref, hub_ref, cnt1_ref, h_ref, seed_ref, nbr2_ref, cnt2_ref, dl_ref, ws_ref, wn_ref,
     self1_ref, nbr1_ref, self2_ref, nbr2o_ref,
     feats_ref, nodes_ref, stage_ref, mid_ref, own_ref, other_ref, table_ref, rows_ref,
-    send_ref, place_ref, slot_ref, code_ref, note_ref, gnt_ref, gst_ref, dpre_ref, second_ref, extra_ref, piece_ref, pieces_ref, column_ref, columns_ref, final_ref,
+    send_ref, slot_ref, self_at_ref, code_ref, note_ref, gnt_ref, gst_ref, dpre_ref, second_ref, extra_ref, piece_ref, pieces_ref, column_ref, columns_ref, final_ref,
     self_ref, sum_ref, acc_ref, part_ref, theirs_ref, got_ref, done_ref,
     index_sems, swap_sems, mid_sems, far_sems, near_sems, note_up, note_down, note_over,
     dpre_up, dpre_down, over_sems, z_sems, dp_sems, z2_sems, first_sems, first2_sems,
@@ -85,10 +85,20 @@
         pending.append(copy)
         return copy
 
-    wanted = pltpu.make_async_copy(
-        send_rows_ref.at[0, :, pl.ds(pl.multiple_of(core * HALF, HALF), HALF)], send_ref, index_sems.at[0]
-    )
-    wanted.start()
+    wanted = [
+        pltpu.make_async_copy(
+            send_rows_ref.at[pl.ds(pl.multiple_of(k * CAP + core * HALF, HALF), HALF)],
+            send_ref.at[pl.ds(k * HALF, HALF)],
+            index_sems.at[k],
+        )
+        for k in range(N_DP)
+    ]
+    located = [
+        pltpu.make_async_copy(slots_ref, slot_ref, index_sems.at[N_DP]),
+        pltpu.make_async_copy(self_slot_ref, self_at_ref, index_sems.at[N_DP + 1]),
+    ]
+    for copy in wanted + located:
+        copy.start()
 
     barrier = pltpu.get_barrier_semaphore()
     peers = [partner]
@@ -159,37 +169,37 @@
 
     feats_ref[lane, pl.ds(0, NODES)] = x_ref[...]
     feats_ref[lane, pl.ds(NODES, HUBS)] = hub_ref[...]
-
-    def places(slots):
-        mine_first = jnp.where(((slots >> 10) & 1) == core, 0, PART)
-        return jnp.where(slots < N_DP * CAP, mine_first + (slots >> 11) * HALF + (slots & (HALF - 1)), slots)
-
-    used = lax.broadcasted_iota(jnp.int32, (FAN1, N_FEAT * ROWS), 0) < cnt1_ref[...]
-    place_ref[pl.ds(0, FAN1), :] = jnp.where(used, places(slots_ref[...]), ZERO_ROW)
-    place_ref[pl.ds(FAN1, 1), :] = places(self_slot_ref[...])
-    located = pltpu.make_async_copy(place_ref, slot_ref, index_sems.at[1])
-    located.start()
     swap_x.wait_recv()
 
+    eye_rows = lax.broadcasted_iota(jnp.int32, (256, 256), 0)
+    eye_columns = lax.broadcasted_iota(jnp.int32, (256, 256), 1)
+    eye = jnp.where(eye_rows == eye_columns, 1.0, 0.0).astype(BF16)
+    across = (((1,), (1,)), ((), ()))
+
+    def turned(at):
+        return lax.dot_general(eye, feats_ref[:, pl.ds(at, 256)], across, preferred_element_type=F32)
+
     def turn(block, carry):
-        at = pl.multiple_of(block * 1024, 1024)
-        nodes_ref[pl.ds(at, 1024), :] = feats_ref[:, pl.ds(at, 1024)].astype(F32).T
+        for i in range(4):
+            at = pl.multiple_of(block * 1024 + i * 256, 256)
+            nodes_ref[pl.ds(at, 256), :] = turned(at)
         return carry
 
     lax.fori_loop(0, NODES // 1024, turn, 0)
-    wanted.wait()
+    for copy in wanted:
+        copy.wait()
 
     far = {}
     staged = {}
 
     def pick(shift, half):
         to = at_shift(*shift)
-        first = half * QUARTER
+        first = to * HALF + half * QUARTER
         unroll = 32
 
         def some_rows(block, carry):
             at = pl.multiple_of(block * unroll, unroll)
-            got = [nodes_ref[pl.ds(send_ref[to, first + at + r], 1), :] for r in range(unroll)]
+            got = [nodes_ref[pl.ds(send_ref[first + at + r], 1), :] for r in range(unroll)]
             for r in range(unroll):
                 rows_ref[pl.ds(at + r, 1), :] = got[r]
             return carry
@@ -225,14 +235,14 @@
         if slot in far:
             far[slot].wait_recv()
         near[slot] = push(own_ref.at[source, half], other_ref.at[source, half], near_sems, slot, partner)
-        at = pl.multiple_of(source * HALF + half * QUARTER, QUARTER)
+        at = pl.multiple_of(source * CAP + core * HALF + half * QUARTER, QUARTER)
         table_ref[pl.ds(at, QUARTER), :] = own_ref[source, half].astype(F32)
 
     def cross(shift, half):
         slot = 2 * (shift[0] * SIDE + shift[1]) + half
         source = at_shift(-shift[0], -shift[1])
         near[slot].wait_recv()
-        at = pl.multiple_of(PART + source * HALF + half * QUARTER, QUARTER)
+        at = pl.multiple_of(source * CAP + (1 - core) * HALF + half * QUARTER, QUARTER)
         table_ref[pl.ds(at, QUARTER), :] = other_ref[source, half].astype(F32)
 
     diagonal = [(shift, half) for shift in DIAGONAL for half in range(2)]
@@ -313,8 +323,9 @@
     swap_hub.wait_recv()
 
     def turn_hub(block, carry):
-        at = pl.multiple_of(block * 1024, 1024)
-        table_ref[pl.ds(2 * PART + at, 1024), :] = feats_ref[:, pl.ds(NODES + at, 1024)].astype(F32).T
+        for i in range(4):
+            at = pl.multiple_of(block * 1024 + i * 256, 256)
+            table_ref[pl.ds(2 * PART + at, 256), :] = turned(NODES + at)
         return carry
 
     lax.fori_loop(0, HUBS // 1024, turn_hub, 0)
@@ -337,7 +348,8 @@
     scattered = {k: push(column_ref.at[piece(k)], pieces_ref.at[k], z_sems, k, (dp, z_feat(k))) for k in around}
     for block in order:
         cross(*block)
-    located.wait()
+    for copy in located:
+        copy.wait()
 
     unroll = 8
 
@@ -347,8 +359,10 @@
 
         def some_sums(block, carry):
             at = pl.multiple_of(block * unroll, unroll)
+            first = base + at
             for r in range(unroll):
-                got = [table_ref[pl.ds(slot_ref[j, base + at + r], 1), :] for j in range(PICKS)]
+                got = [table_ref[pl.ds(slot_ref[j * N_FEAT * ROWS + first + r], 1), :] for j in range(FAN1)]
+                got.append(table_ref[pl.ds(self_at_ref[first + r], 1), :])
                 rest = got[:FAN1]
                 while len(rest) > 1:
                     rest = [rest[i] + rest[i + 1] if i + 1 < len(rest) else rest[i] for i in range(0, len(rest), 2)]
@@ -461,7 +475,7 @@
             jax.ShapeDtypeStruct((CLASSES, HIDDEN), F32),
             jax.ShapeDtypeStruct((CLASSES, HIDDEN), F32),
         ),
-        in_specs=[vmem] * len(operands),
+        in_specs=[pl.BlockSpec(memory_space=pl.ANY)] * 3 + [vmem] * (len(operands) - 3),
         out_specs=(vmem,) * 4,
         scratch_shapes=[
             pltpu.VMEM((WIDE, NODES + HUBS), BF16),
@@ -472,9 +486,9 @@
             pltpu.VMEM((N_DP, 2, QUARTER, WIDE), BF16),
             pltpu.VMEM((ZERO_ROW + 8, WIDE), F32),
             pltpu.VMEM((QUARTER, WIDE), F32),
-            pltpu.SMEM((N_DP, HALF), jnp.int32),
-            pltpu.VMEM((PICKS, N_FEAT * ROWS), jnp.int32),
-            pltpu.SMEM((PICKS, N_FEAT * ROWS), jnp.int32),
+            pltpu.SMEM((N_DP * HALF,), jnp.int32),
+            pltpu.SMEM((FAN1 * N_FEAT * ROWS,), jnp.int32),
+            pltpu.SMEM((N_FEAT * ROWS,), jnp.int32),
             pltpu.VMEM((ROWS, 128), BF16),
             pltpu.VMEM((N_FEAT, NOTE, ROWS), BF16),
             pltpu.VMEM((TALL, ROWS), F32),
@@ -494,7 +508,7 @@
             pltpu.VMEM((2, 64, HIDDEN), F32),
             pltpu.VMEM((N_DP, 8, HIDDEN), F32),
             pltpu.VMEM((N_DP, 16, HIDDEN // 2), BF16),
-            dma((2,)),
+            dma((N_DP + 2,)),
             dma((2, 2)),
             dma((2, len(STAGED))),
             dma((2, 2 * N_DP)),
@@ -550,10 +564,11 @@
     w_self2,
     w_nbr2,
 ):
+    read = lax.iota(jnp.int32, FAN1)[:, None] < cnt1[None]
     sums = main_step(
-        send_rows,
-        self_slot[None],
-        nbr1,
+        send_rows.reshape(-1),
+        self_slot,
+        jnp.where(read, nbr1, ZERO_ROW).reshape(-1),
         x_table,
         hub_feats,
         cnt1[None],

time: 144 us -> 134 us (0.931)
  Pallas kernels: 143 us -> 131 us
  local copies, waits for them, and re-layouts: 0 us -> 2.34 us
    pallas_call x1, Pallas kernels: 141 us -> 129 us  [main_step(): pl.pallas_call(main_kernel, out_shape=(jax.ShapeDtypeStruct((64, HIDDEN),...]
    unnamed x0 -> x5, local copies, waits for them, and re-layouts: none -> 1.64 us
where the time goes in v8:
time: 134 us
  Pallas kernels  131 us (98%)
  local copies, waits for them, and re-layouts  2.34 us (2%)
    pallas_call x1, Pallas kernels, main_step(): pl.pallas_call(main_kernel, out_shape=(jax.ShapeDtypeStruct((64, HIDDEN),...  129 us

profile of v8, /device:TPU:1, one launch (start us, length us, event | category | flops | bytes accessed | tf_op | source)
XLA Modules:
  0.0 134.2 jit_solution(8552848117255581579)
XLA Ops:
  0.6 0.0 copy-start
  0.6 0.0 copy-start.1
  0.7 1.6 %copy.17 = s32[2,16,8,128]{3,1,2,0:T(8,128)} copy(s32[2,16,8,128]{3,2,1,0:T(8,128)} %bitcast.14) | data formatting | bytes 262144
  2.3 0.0 copy-done
  2.3 0.0 copy-done.1
  2.3 0.7 reshape.16.slots_ref
  3.0 129.0 %main_step.1 = (f32[64,512]{1,0:T(8,128)}, f32[64,512]{1,0:T(8,128)}, f32[172,512]{1,0:T(8,128)}, f32[172,512]{1,0:T(8,128)}) custom-call(s32[32768]{0:T(1024)} %bitcast.11, s32[4096]{0:T(1024)} %self_slot_ref.1, s32[40960]{0:T(1024)} %reshape.16.slots_ref, bf16[64,8192]{1,0:T(8,128)(2,1)} %x_ref.1, bf16[64,2048]{1,0:T(8,128)(2,1)} %hub_ref.1, ...), custom_call_target="tpu_custom_call" | custom-call | tf_op jit(solution)/shard_map/main_step/pallas_call | solution.py:470
  132.0 2.2 %hand_out.1 = (f32[64,512]{1,0:T(8,128)}, f32[64,512]{1,0:T(8,128)}, f32[172,512]{1,0:T(8,128)}, f32[172,512]{1,0:T(8,128)}) custom-call(f32[64,512]{1,0:T(8,128)} %get-tuple-element.12.refs_0_, f32[64,512]{1,0:T(8,128)} %get-tuple-element.13.refs_1_, f32[172,512]{1,0:T(8,128)} %get-tuple-element.14.refs_2_, f32[172,512]{1,0:T(8,128)} %get-tuple-element.15.refs_3_), custom_call_target="tpu_custom_call" | custom-call | tf_op jit(solution)/shard_map/hand_out/pallas_call | solution.py:542
  (1 shorter events, 0.0 us)
Async XLA Ops:
  0.6 1.7 %copy-start = (s32[10,4096]{1,0:T(8,128)S(1)}, s32[10,4096]{1,0:T(8,128)}, u32[]{:S(2)}) copy-start(s32[10,4096]{1,0:T(8,128)} %param.17) | copy-start | bytes 491524
  0.6 1.6 %copy-start.1 = (s32[4096]{0:T(1024)S(1)}, s32[4096]{0:T(1024)}, u32[]{:S(2)}) copy-start(s32[4096]{0:T(1024)} %param.18) | copy-start | bytes 49156

commit v9 on v8

--- a/solution.py
+++ b/solution.py
@@ -52,8 +52,8 @@
     send_rows_ref, self_slot_ref, slots_ref, x_ref, hub_ref, cnt1_ref, h_ref, seed_ref, nbr2_ref, cnt2_ref, dl_ref, ws_ref, wn_ref,
     self1_ref, nbr1_ref, self2_ref, nbr2o_ref,
     feats_ref, nodes_ref, stage_ref, mid_ref, own_ref, other_ref, table_ref, rows_ref,
-    send_ref, slot_ref, self_at_ref, code_ref, note_ref, gnt_ref, gst_ref, dpre_ref, second_ref, extra_ref, piece_ref, pieces_ref, column_ref, columns_ref, final_ref,
-    self_ref, sum_ref, acc_ref, part_ref, theirs_ref, got_ref, done_ref,
+    send_ref, slot_ref, self_at_ref, code_ref, tally_ref, hot_ref, mean_ref, note_ref, gnt_ref, gst_ref, dpre_ref, second_ref, extra_ref, piece_ref, pieces_ref, column_ref, columns_ref, final_ref,
+    self_ref, sum_ref, both_ref, acc_ref, part_ref, theirs_ref, got_ref, done_ref,
     index_sems, swap_sems, mid_sems, far_sems, near_sems, note_up, note_down, note_over,
     dpre_up, dpre_down, over_sems, z_sems, dp_sems, z2_sems, first_sems, first2_sems,
 ):
@@ -195,7 +195,7 @@
     def pick(shift, half):
         to = at_shift(*shift)
         first = to * HALF + half * QUARTER
-        unroll = 32
+        unroll = 64
 
         def some_rows(block, carry):
             at = pl.multiple_of(block * unroll, unroll)
@@ -229,6 +229,14 @@
 
     near = {}
 
+    def widen(ref, source, half, at):
+        def some(block, carry):
+            inner = pl.multiple_of(block * 128, 128)
+            table_ref[pl.ds(pl.multiple_of(at + inner, 128), 128), :] = ref[source, half, pl.ds(inner, 128), :].astype(F32)
+            return carry
+
+        lax.fori_loop(0, QUARTER // 128, some, 0)
+
     def arrive(shift, half):
         slot = 2 * (shift[0] * SIDE + shift[1]) + half
         source = at_shift(-shift[0], -shift[1])
@@ -236,14 +244,14 @@
             far[slot].wait_recv()
         near[slot] = push(own_ref.at[source, half], other_ref.at[source, half], near_sems, slot, partner)
         at = pl.multiple_of(source * CAP + core * HALF + half * QUARTER, QUARTER)
-        table_ref[pl.ds(at, QUARTER), :] = own_ref[source, half].astype(F32)
+        widen(own_ref, source, half, at)
 
     def cross(shift, half):
         slot = 2 * (shift[0] * SIDE + shift[1]) + half
         source = at_shift(-shift[0], -shift[1])
         near[slot].wait_recv()
         at = pl.multiple_of(source * CAP + (1 - core) * HALF + half * QUARTER, QUARTER)
-        table_ref[pl.ds(at, QUARTER), :] = other_ref[source, half].astype(F32)
+        widen(other_ref, source, half, at)
 
     diagonal = [(shift, half) for shift in DIAGONAL for half in range(2)]
     nearest = [(shift, half) for half in range(2) for shift in NEXT]
@@ -251,10 +259,16 @@
     notes.take(1)
     for number, block in enumerate(STAGED + diagonal):
         pick(*block)
-        if number < len(STAGED):
-            send(*block)
+        send(*block)
         if number in (5, 11, 17):
             notes.take(number // 6 + 2)
+    for number, block in enumerate(nearest):
+        for s in range(2 * number, min(2 * number + 2, len(STAGED))):
+            pass_on(s)
+        pick(*block)
+        send(*block)
+    for half in range(2):
+        pick((0, 0), half)
     for copy in notes.crossed:
         copy.wait_recv()
 
@@ -278,18 +292,27 @@
                 else:
                     hots.append(match)
             tallies.append(total)
-        tally = jnp.concatenate(tallies, axis=1)
-        hot = jnp.concatenate(hots, axis=1)
+        tally_ref[f] = jnp.concatenate(tallies, axis=1)
+        hot_ref[f] = jnp.concatenate(hots, axis=1)
         dl = note_ref[f, pl.ds(0, TALL), :]
-        dz = (dl.astype(F32) / names_here[NAMES : NAMES + 1, :]).astype(BF16)
-        gnt_ref[...] += lax.dot_general(dz, tally, both_last, preferred_element_type=F32)
-        gst_ref[...] += lax.dot_general(dl, hot, both_last, preferred_element_type=F32)
+        mean_ref[f] = (dl.astype(F32) / names_here[NAMES : NAMES + 1, :]).astype(BF16)
         return carry
 
-    for part in range(8):
-        lax.fori_loop(2 * part, 2 * part + 2, one_device, 0)
-        for s in range(2 * part, min(2 * part + 2, len(STAGED))):
-            pass_on(s)
+    def four_devices(block, carry):
+        nbr = gnt_ref[...]
+        own = gst_ref[...]
+        for i in range(4):
+            f = 4 * block + i
+            nbr += lax.dot_general(mean_ref[f], tally_ref[f], both_last, preferred_element_type=F32)
+            own += lax.dot_general(
+                note_ref[f, pl.ds(0, TALL), :], hot_ref[f], both_last, preferred_element_type=F32
+            )
+        gnt_ref[...] = nbr
+        gst_ref[...] = own
+        return carry
+
+    lax.fori_loop(0, N_FEAT, one_device, 0)
+    lax.fori_loop(0, N_FEAT // 4, four_devices, 0)
 
     def twice(value, other, left):
         top = value.astype(BF16)
@@ -309,17 +332,10 @@
     dpre_ref[z] = jnp.where(h_ref[...].astype(F32).T > 0, hidden, 0.0).astype(BF16)
     rows_ring = Ring(lambda step: dpre_ref.at[lax.rem(z + step + N_Z, N_Z)], dpre_up, dpre_down)
     rows_ring.start()
-    for number, block in enumerate(nearest):
-        send(*diagonal[number])
-        pick(*block)
-        send(*block)
     second_ref[0] = twice(gst, h_ref[...], True)
     second_ref[1] = twice(gnt, h_ref[...], True)
     second_over = push(second_ref.at[1 - core], extra_ref, over_sems, 0, partner)
 
-    for half in range(2):
-        pick((0, 0), half)
-    rows_ring.take(1)
     swap_hub.wait_recv()
 
     def turn_hub(block, carry):
@@ -335,8 +351,8 @@
     for number, block in enumerate(order):
         arrive(*block)
         if number == 15:
-            rows_ring.take(2)
-    rows_ring.take(3)
+            rows_ring.take(1)
+    rows_ring.take(2)
     second_over.wait_recv()
     column_ref[...] = second_ref[core] + extra_ref[...]
 
@@ -351,7 +367,7 @@
     for copy in located:
         copy.wait()
 
-    unroll = 8
+    unroll = 16
 
     def fold(step):
         of = lax.rem(z + step + N_Z, N_Z)
@@ -373,20 +389,15 @@
         lax.fori_loop(0, ROWS // unroll, some_sums, 0)
         here = pl.ds(pl.multiple_of(base, ROWS), ROWS)
         count = jnp.broadcast_to(cnt1_ref[:, here].astype(F32), (WIDE, ROWS)).T
-        own = self_ref[...].astype(BF16)
-        mean = (sum_ref[...] / count).astype(BF16)
-        both = jnp.concatenate([own, mean], axis=1)
-        product = jnp.dot(dpre_ref[of], both, preferred_element_type=F32)
-        if step == 0:
-            acc_ref[...] = product
-        else:
-            acc_ref[...] += product
+        both_ref[of, :, pl.ds(0, WIDE)] = self_ref[...].astype(BF16)
+        both_ref[of, :, pl.ds(WIDE, WIDE)] = (sum_ref[...] / count).astype(BF16)
 
     gathered = []
     for number, step in enumerate((0, -1, 1, -2, 2, -3, 3, -4)):
         fold(step)
+        if number == 0:
+            rows_ring.take(3)
         if number == 1:
-            rows_ring.take(4)
             total = column_ref[piece(0)]
             for k in around:
                 scattered[k].wait_recv()
@@ -399,6 +410,7 @@
                 copy.wait_recv()
                 total = total + columns_ref[i + 1]
             piece_ref[1] = total
+            rows_ring.take(4)
             along_y = [
                 push(piece_ref.at[1], columns_ref.at[SIDE + i], dp_sems, SIDE + i, (at_shift(0, i), feat))
                 for i in range(1, SIDE)
@@ -418,6 +430,14 @@
                 copy.wait_recv()
             second_back = push(final_ref.at[core], final_ref.at[core], over_sems, 1, partner)
 
+    def two_devices(block, carry):
+        total = jnp.dot(dpre_ref[2 * block], both_ref[2 * block], preferred_element_type=F32)
+        total += jnp.dot(dpre_ref[2 * block + 1], both_ref[2 * block + 1], preferred_element_type=F32)
+        acc_ref[...] += total
+        return carry
+
+    acc_ref[...] = jnp.zeros_like(acc_ref)
+    lax.fori_loop(0, N_Z // 2, two_devices, 0)
     part_ref[...] = acc_ref[...].T
     first_over = [
         push(
@@ -490,6 +510,9 @@
             pltpu.SMEM((FAN1 * N_FEAT * ROWS,), jnp.int32),
             pltpu.SMEM((N_FEAT * ROWS,), jnp.int32),
             pltpu.VMEM((ROWS, 128), BF16),
+            pltpu.VMEM((N_FEAT, ROWS, ROWS), BF16),
+            pltpu.VMEM((N_FEAT, ROWS, ROWS), BF16),
+            pltpu.VMEM((N_FEAT, TALL, ROWS), BF16),
             pltpu.VMEM((N_FEAT, NOTE, ROWS), BF16),
             pltpu.VMEM((TALL, ROWS), F32),
             pltpu.VMEM((TALL, ROWS), F32),
@@ -503,6 +526,7 @@
             pltpu.VMEM((2, TALL, HIDDEN), F32),
             pltpu.VMEM((ROWS, WIDE), F32),
             pltpu.VMEM((ROWS, WIDE), F32),
+            pltpu.VMEM((N_Z, ROWS, 2 * WIDE), BF16),
             pltpu.VMEM((HIDDEN, 2 * WIDE), F32),
             pltpu.VMEM((2 * WIDE, HIDDEN), F32),
             pltpu.VMEM((2, 64, HIDDEN), F32),

time: 134 us -> 140 us (1.045)
  Pallas kernels: 131 us -> 137 us
    pallas_call x1, Pallas kernels: 129 us -> 135 us  [main_step(): pl.pallas_call(main_kernel, out_shape=(jax.ShapeDtypeStruct((64, HIDDEN),...]
where the time goes in v9:
time: 140 us
  Pallas kernels  137 us (98%)
  local copies, waits for them, and re-layouts  2.34 us (2%)
    pallas_call x1, Pallas kernels, main_step(): pl.pallas_call(main_kernel, out_shape=(jax.ShapeDtypeStruct((64, HIDDEN),...  135 us

profile of v9, /device:TPU:1, one launch (start us, length us, event | category | flops | bytes accessed | tf_op | source)
XLA Modules:
  0.0 140.2 jit_solution(5260843679251068315)
XLA Ops:
  0.6 0.0 copy-start
  0.6 0.0 copy-start.1
  0.7 1.6 %copy.17 = s32[2,16,8,128]{3,1,2,0:T(8,128)} copy(s32[2,16,8,128]{3,2,1,0:T(8,128)} %bitcast.14) | data formatting | bytes 262144
  2.3 0.0 copy-done
  2.3 0.0 copy-done.1
  2.3 0.7 reshape.16.slots_ref
  3.0 134.9 %main_step.1 = (f32[64,512]{1,0:T(8,128)}, f32[64,512]{1,0:T(8,128)}, f32[172,512]{1,0:T(8,128)}, f32[172,512]{1,0:T(8,128)}) custom-call(s32[32768]{0:T(1024)} %bitcast.11, s32[4096]{0:T(1024)} %self_slot_ref.1, s32[40960]{0:T(1024)} %reshape.16.slots_ref, bf16[64,8192]{1,0:T(8,128)(2,1)} %x_ref.1, bf16[64,2048]{1,0:T(8,128)(2,1)} %hub_ref.1, ...), custom_call_target="tpu_custom_call" | custom-call | tf_op jit(solution)/shard_map/main_step/pallas_call | solution.py:490
  138.0 2.2 %hand_out.1 = (f32[64,512]{1,0:T(8,128)}, f32[64,512]{1,0:T(8,128)}, f32[172,512]{1,0:T(8,128)}, f32[172,512]{1,0:T(8,128)}) custom-call(f32[64,512]{1,0:T(8,128)} %get-tuple-element.12.refs_0_, f32[64,512]{1,0:T(8,128)} %get-tuple-element.13.refs_1_, f32[172,512]{1,0:T(8,128)} %get-tuple-element.14.refs_2_, f32[172,512]{1,0:T(8,128)} %get-tuple-element.15.refs_3_), custom_call_target="tpu_custom_call" | custom-call | tf_op jit(solution)/shard_map/hand_out/pallas_call | solution.py:566
  (1 shorter events, 0.0 us)
Async XLA Ops:
  0.6 1.7 %copy-start = (s32[10,4096]{1,0:T(8,128)S(1)}, s32[10,4096]{1,0:T(8,128)}, u32[]{:S(2)}) copy-start(s32[10,4096]{1,0:T(8,128)} %param.17) | copy-start | bytes 491524
  0.6 1.6 %copy-start.1 = (s32[4096]{0:T(1024)S(1)}, s32[4096]{0:T(1024)}, u32[]{:S(2)}) copy-start(s32[4096]{0:T(1024)} %param.18) | copy-start | bytes 49156

commit v10 on v9

--- a/solution.py
+++ b/solution.py
@@ -259,16 +259,11 @@
     notes.take(1)
     for number, block in enumerate(STAGED + diagonal):
         pick(*block)
-        send(*block)
-        if number in (5, 11, 17):
-            notes.take(number // 6 + 2)
-    for number, block in enumerate(nearest):
-        for s in range(2 * number, min(2 * number + 2, len(STAGED))):
-            pass_on(s)
-        pick(*block)
-        send(*block)
-    for half in range(2):
-        pick((0, 0), half)
+        if number in (4, 9, 14):
+            notes.take(number // 5 + 2)
+        if number == 14:
+            for earlier in STAGED:
+                send(*earlier)
     for copy in notes.crossed:
         copy.wait_recv()
 
@@ -311,7 +306,10 @@
         gst_ref[...] = own
         return carry
 
-    lax.fori_loop(0, N_FEAT, one_device, 0)
+    for quarter in range(4):
+        lax.fori_loop(4 * quarter, 4 * quarter + 4, one_device, 0)
+        for s in range(4 * quarter, min(4 * quarter + 4, len(STAGED))):
+            pass_on(s)
     lax.fori_loop(0, N_FEAT // 4, four_devices, 0)
 
     def twice(value, other, left):
@@ -332,10 +330,17 @@
     dpre_ref[z] = jnp.where(h_ref[...].astype(F32).T > 0, hidden, 0.0).astype(BF16)
     rows_ring = Ring(lambda step: dpre_ref.at[lax.rem(z + step + N_Z, N_Z)], dpre_up, dpre_down)
     rows_ring.start()
+    for number, block in enumerate(nearest):
+        send(*diagonal[number])
+        pick(*block)
+        send(*block)
     second_ref[0] = twice(gst, h_ref[...], True)
     second_ref[1] = twice(gnt, h_ref[...], True)
     second_over = push(second_ref.at[1 - core], extra_ref, over_sems, 0, partner)
 
+    for half in range(2):
+        pick((0, 0), half)
+    rows_ring.take(1)
     swap_hub.wait_recv()
 
     def turn_hub(block, carry):
@@ -351,8 +356,8 @@
     for number, block in enumerate(order):
         arrive(*block)
         if number == 15:
-            rows_ring.take(1)
-    rows_ring.take(2)
+            rows_ring.take(2)
+    rows_ring.take(3)
     second_over.wait_recv()
     column_ref[...] = second_ref[core] + extra_ref[...]
 
@@ -395,9 +400,8 @@
     gathered = []
     for number, step in enumerate((0, -1, 1, -2, 2, -3, 3, -4)):
         fold(step)
-        if number == 0:
-            rows_ring.take(3)
         if number == 1:
+            rows_ring.take(4)
             total = column_ref[piece(0)]
             for k in around:
                 scattered[k].wait_recv()
@@ -410,7 +414,6 @@
                 copy.wait_recv()
                 total = total + columns_ref[i + 1]
             piece_ref[1] = total
-            rows_ring.take(4)
             along_y = [
                 push(piece_ref.at[1], columns_ref.at[SIDE + i], dp_sems, SIDE + i, (at_shift(0, i), feat))
                 for i in range(1, SIDE)

time: 140 us -> 139 us (level)
  no operation moved by 1% of the time
where the time goes in v10:
time: 139 us
  Pallas kernels  136 us (98%)
  local copies, waits for them, and re-layouts  2.34 us (2%)
    pallas_call x1, Pallas kernels, main_step(): pl.pallas_call(main_kernel, out_shape=(jax.ShapeDtypeStruct((64, HIDDEN),...  134 us

profile of v10, /device:TPU:1, one launch (start us, length us, event | category | flops | bytes accessed | tf_op | source)
XLA Modules:
  0.0 139.1 jit_solution(4879978023417479016)
XLA Ops:
  0.6 0.0 copy-start
  0.6 0.0 copy-start.1
  0.7 1.6 %copy.17 = s32[2,16,8,128]{3,1,2,0:T(8,128)} copy(s32[2,16,8,128]{3,2,1,0:T(8,128)} %bitcast.14) | data formatting | bytes 262144
  2.3 0.0 copy-done
  2.3 0.0 copy-done.1
  2.3 0.7 reshape.16.slots_ref
  3.0 133.8 %main_step.1 = (f32[64,512]{1,0:T(8,128)}, f32[64,512]{1,0:T(8,128)}, f32[172,512]{1,0:T(8,128)}, f32[172,512]{1,0:T(8,128)}) custom-call(s32[32768]{0:T(1024)} %bitcast.11, s32[4096]{0:T(1024)} %self_slot_ref.1, s32[40960]{0:T(1024)} %reshape.16.slots_ref, bf16[64,8192]{1,0:T(8,128)(2,1)} %x_ref.1, bf16[64,2048]{1,0:T(8,128)(2,1)} %hub_ref.1, ...), custom_call_target="tpu_custom_call" | custom-call | tf_op jit(solution)/shard_map/main_step/pallas_call | solution.py:493
  136.9 2.2 %hand_out.1 = (f32[64,512]{1,0:T(8,128)}, f32[64,512]{1,0:T(8,128)}, f32[172,512]{1,0:T(8,128)}, f32[172,512]{1,0:T(8,128)}) custom-call(f32[64,512]{1,0:T(8,128)} %get-tuple-element.12.refs_0_, f32[64,512]{1,0:T(8,128)} %get-tuple-element.13.refs_1_, f32[172,512]{1,0:T(8,128)} %get-tuple-element.14.refs_2_, f32[172,512]{1,0:T(8,128)} %get-tuple-element.15.refs_3_), custom_call_target="tpu_custom_call" | custom-call | tf_op jit(solution)/shard_map/hand_out/pallas_call | solution.py:569
  (1 shorter events, 0.0 us)
Async XLA Ops:
  0.6 1.7 %copy-start = (s32[10,4096]{1,0:T(8,128)S(1)}, s32[10,4096]{1,0:T(8,128)}, u32[]{:S(2)}) copy-start(s32[10,4096]{1,0:T(8,128)} %param.17) | copy-start | bytes 491524
  0.6 1.6 %copy-start.1 = (s32[4096]{0:T(1024)S(1)}, s32[4096]{0:T(1024)}, u32[]{:S(2)}) copy-start(s32[4096]{0:T(1024)} %param.18) | copy-start | bytes 49156

commit v11 on v10

--- a/solution.py
+++ b/solution.py
@@ -195,7 +195,7 @@
     def pick(shift, half):
         to = at_shift(*shift)
         first = to * HALF + half * QUARTER
-        unroll = 64
+        unroll = 32
 
         def some_rows(block, carry):
             at = pl.multiple_of(block * unroll, unroll)
@@ -230,12 +230,7 @@
     near = {}
 
     def widen(ref, source, half, at):
-        def some(block, carry):
-            inner = pl.multiple_of(block * 128, 128)
-            table_ref[pl.ds(pl.multiple_of(at + inner, 128), 128), :] = ref[source, half, pl.ds(inner, 128), :].astype(F32)
-            return carry
-
-        lax.fori_loop(0, QUARTER // 128, some, 0)
+        table_ref[pl.ds(at, QUARTER), :] = ref[source, half].astype(F32)
 
     def arrive(shift, half):
         slot = 2 * (shift[0] * SIDE + shift[1]) + half
@@ -259,11 +254,10 @@
     notes.take(1)
     for number, block in enumerate(STAGED + diagonal):
         pick(*block)
-        if number in (4, 9, 14):
-            notes.take(number // 5 + 2)
-        if number == 14:
-            for earlier in STAGED:
-                send(*earlier)
+        if number < len(STAGED):
+            send(*block)
+        if number in (5, 11, 17):
+            notes.take(number // 6 + 2)
     for copy in notes.crossed:
         copy.wait_recv()
 

time: 139 us -> 135 us (0.971)
  Pallas kernels: 136 us -> 132 us
    pallas_call x1, Pallas kernels: 134 us -> 130 us  [main_step(): pl.pallas_call(main_kernel, out_shape=(jax.ShapeDtypeStruct((64, HIDDEN),...]
where the time goes in v11:
time: 135 us
  Pallas kernels  132 us (98%)
  local copies, waits for them, and re-layouts  2.34 us (2%)
    pallas_call x1, Pallas kernels, main_step(): pl.pallas_call(main_kernel, out_shape=(jax.ShapeDtypeStruct((64, HIDDEN),...  130 us

profile of v11, /device:TPU:1, one launch (start us, length us, event | category | flops | bytes accessed | tf_op | source)
XLA Modules:
  0.0 134.8 jit_solution(1615140995796416583)
XLA Ops:
  0.6 0.0 copy-start
  0.6 0.0 copy-start.1
  0.7 1.6 %copy.17 = s32[2,16,8,128]{3,1,2,0:T(8,128)} copy(s32[2,16,8,128]{3,2,1,0:T(8,128)} %bitcast.14) | data formatting | bytes 262144
  2.3 0.0 copy-done
  2.3 0.0 copy-done.1
  2.3 0.7 reshape.16.slots_ref
  3.0 129.6 %main_step.1 = (f32[64,512]{1,0:T(8,128)}, f32[64,512]{1,0:T(8,128)}, f32[172,512]{1,0:T(8,128)}, f32[172,512]{1,0:T(8,128)}) custom-call(s32[32768]{0:T(1024)} %bitcast.11, s32[4096]{0:T(1024)} %self_slot_ref.1, s32[40960]{0:T(1024)} %reshape.16.slots_ref, bf16[64,8192]{1,0:T(8,128)(2,1)} %x_ref.1, bf16[64,2048]{1,0:T(8,128)(2,1)} %hub_ref.1, ...), custom_call_target="tpu_custom_call" | custom-call | tf_op jit(solution)/shard_map/main_step/pallas_call | solution.py:487
  132.7 2.2 %hand_out.1 = (f32[64,512]{1,0:T(8,128)}, f32[64,512]{1,0:T(8,128)}, f32[172,512]{1,0:T(8,128)}, f32[172,512]{1,0:T(8,128)}) custom-call(f32[64,512]{1,0:T(8,128)} %get-tuple-element.12.refs_0_, f32[64,512]{1,0:T(8,128)} %get-tuple-element.13.refs_1_, f32[172,512]{1,0:T(8,128)} %get-tuple-element.14.refs_2_, f32[172,512]{1,0:T(8,128)} %get-tuple-element.15.refs_3_), custom_call_target="tpu_custom_call" | custom-call | tf_op jit(solution)/shard_map/hand_out/pallas_call | solution.py:563
  (1 shorter events, 0.0 us)
Async XLA Ops:
  0.6 1.7 %copy-start = (s32[10,4096]{1,0:T(8,128)S(1)}, s32[10,4096]{1,0:T(8,128)}, u32[]{:S(2)}) copy-start(s32[10,4096]{1,0:T(8,128)} %param.17) | copy-start | bytes 491524
  0.6 1.6 %copy-start.1 = (s32[4096]{0:T(1024)S(1)}, s32[4096]{0:T(1024)}, u32[]{:S(2)}) copy-start(s32[4096]{0:T(1024)} %param.18) | copy-start | bytes 49156
